TPU v7x, 32 devices: a whole 2x2x4 slice. The times are simulated.
32 devices in a mesh: dp: 4 (over y, core), expert: 8 (over z, x).
Axes of the slice: x: 2, y: 2, z: 4, core: 2. Of those that a mesh axis runs over, the one named last changes fastest.
Arguments:
- hidden_in: bfloat16 [8, 4, 640, 1024], P('expert', 'dp'), may hold values from -6 to 6
- down_weight: bfloat16 [8, 1024, 3584], P('expert'), may hold values from -0.1875 to 0.1875
- routes: int32 [4096, 4], P(('dp', 'expert')), may hold values from 0 to 7, all different within a row; in each aligned block of 128 rows (0 to 127, 128 to 255, ...) at most 80 rows name the same one
- gate_prob: float32 [4096, 4], P(('dp', 'expert')), may hold values from 0.05 to 1
- cotangent: bfloat16 [4096, 3584], P(('dp', 'expert')), may hold values from -0.59765625 to 0.59765625
Outputs:
- combined: bfloat16 [4096, 3584], P(('dp', 'expert'))
- gate_grad: float32 [4096, 4], P(('dp', 'expert'))
- hidden_grad: bfloat16 [8, 4, 640, 1024], P('expert', 'dp')
- weight_grad: bfloat16 [8, 1024, 3584], P('expert', 'dp')
Inputs may be any that keep to these rules, and one draw needn't show every extreme that they name: `routes`: each row names 4 different experts. Within the rows of one device (aligned blocks of 128 rows) no expert is named by more than 80 rows, a bound that some block reaches.
All inputs are finite; a program needn't handle non-finite values.
Results may differ from a plain program's by a relative error of at most 0.017.
Values may be sent and summed in bfloat16 or wider, within the bound.
No kernel may reach another device: no remote copies, remote signals or barrier semaphores. Data moves between devices by JAX's collectives and lax.ppermute only.
A program may use at most 128 MiB of HBM per device.

v0:
```python
import jax
import jax.numpy as jnp
from jax import lax
from jax.sharding import PartitionSpec as P


def slot_positions(routes, experts):
    flattened = routes.reshape(-1)
    onehot = (flattened[:, None] == jnp.arange(experts, dtype=jnp.int32)[None, :]).astype(jnp.int32)
    before = jnp.cumsum(onehot, axis=0) - onehot
    within = jnp.sum(before * onehot, axis=1)
    return (flattened, within)


def local(hidden_in, down_weight, routes, gate_prob, cotangent):
    experts = lax.axis_size("expert")
    capacity = hidden_in.shape[2] // experts
    tok_rows = routes.shape[0]
    choices_per = routes.shape[1]
    features = down_weight.shape[2]
    chosen, within = slot_positions(routes, experts)
    slot_index = chosen * capacity + within
    weight = down_weight[0]
    rows_in = hidden_in[0, 0]
    produced = jnp.dot(rows_in, weight, preferred_element_type=jnp.float32).astype(jnp.bfloat16)
    by_source = produced.reshape(experts, capacity, features)
    scaled = (gate_prob[:, :, None] * cotangent.astype(jnp.float32)[:, None, :]).astype(
        jnp.bfloat16
    )
    outgoing = jnp.zeros((experts * capacity, features), jnp.bfloat16)
    outgoing = outgoing.at[slot_index].set(scaled.reshape(tok_rows * choices_per, features))
    outgoing = outgoing.reshape(experts, capacity, features)
    returned = lax.all_to_all(by_source, "expert", split_axis=0, concat_axis=0, tiled=True)
    arrived = lax.all_to_all(outgoing, "expert", split_axis=0, concat_axis=0, tiled=True)
    picked = returned.reshape(experts * capacity, features)[slot_index]
    picked = picked.reshape(tok_rows, choices_per, features)
    combined = jnp.sum(gate_prob[:, :, None] * picked.astype(jnp.float32), axis=1).astype(
        jnp.bfloat16
    )
    gate_grad = jnp.einsum("td,tkd->tk", cotangent, picked, preferred_element_type=jnp.float32)
    slot_grads = arrived.reshape(experts * capacity, features)
    hidden_grad = lax.dot_general(
        slot_grads, weight, (((1,), (1,)), ((), ())), preferred_element_type=jnp.float32
    )
    hidden_grad = hidden_grad.astype(jnp.bfloat16).reshape(hidden_in.shape)
    summed = lax.psum_scatter(
        lax.dot_general(
            rows_in, slot_grads, (((0,), (0,)), ((), ())), preferred_element_type=jnp.float32
        ).astype(jnp.bfloat16),
        "dp",
        scatter_dimension=0,
        tiled=True,
    )
    weight_grad = summed[None]
    return (combined, gate_grad, hidden_grad, weight_grad)


def solution(mesh):
    in_specs = (
        P("expert", "dp", None, None),
        P("expert", None, None),
        P(("dp", "expert"), None),
        P(("dp", "expert"), None),
        P(("dp", "expert"), None),
    )
    out_specs = (
        P(("dp", "expert"), None),
        P(("dp", "expert"), None),
        P("expert", "dp", None, None),
        P("expert", "dp", None),
    )
    return jax.shard_map(local, mesh=mesh, in_specs=in_specs, out_specs=out_specs, check_vma=False)
```

profile of v0, /device:TPU:0, one launch (start us, length us, event | category | flops | bytes accessed | tf_op | source)
XLA Modules:
  0.0 324.8 jit_solution(10588153007036079563)
XLA Ops:
  7.2 0.9 copy.13
  8.2 0.1 eq.25
  8.3 0.7 broadcast_multiply_fusion
  9.0 1.1 reduce-window.6
  10.1 0.2 slice_reduce_fusion
  10.4 0.1 copy.12
  10.5 0.1 mul.48
  10.6 0.8 copy.11
  11.5 5.2 %mul.53 = f32[128,4,3584]{2,1,0:T(4,128)} broadcast(bf16[128,3584]{1,0:T(8,128)(2,1)} %param.9), dimensions={0,2} | broadcast | bytes 8257536 | tf_op jit(solution)/shard_map/mul | solution.py:27
  16.7 9.0 %mul.54 = f32[512,3584]{1,0:T(8,128)} reshape(f32[128,4,3584]{2,1,0:T(4,128)} %mul.53) | data formatting | bytes 14680064 | tf_op jit(solution)/shard_map/mul | solution.py:27
  25.8 10.9 %scatter_custom_fusion = bf16[640,3584]{1,0:T(8,128)(2,1)} fusion(s32[512]{0:T(512)S(1)} %bitcast.46, f32[512,3584]{1,0:T(8,128)} %mul.54, f32[512]{0:T(512)S(1)} %mul.51, bf16[]{:T(256)} %constant.14.clone.1), kind=kCustom, calls=%fused_computation.11 | custom fusion | flops 3670016 | bytes 11929602 | tf_op jit(solution)/shard_map/scatter | solution.py:31
  36.7 109.2 %all_to_all.10 = bf16[8,80,3584]{2,1,0:T(8,128)(2,1)S(1)} all-to-all(bf16[8,80,3584]{2,1,0:T(8,128)(2,1)} %bitcast.40), channel_id=1, replica_groups=mesh['dp'=4,'expert'=8] {'expert'}, dimensions={0} | all-to-all | bytes 9175040 | tf_op jit(solution)/shard_map/all_to_all | solution.py:34
  145.9 2.2 copy-done.1
  148.1 8.0 %fusion.4 = bf16[1024,3584]{0,1:T(8,128)(2,1)} fusion(bf16[640,3584]{1,0:T(8,128)(2,1)S(1)} %bitcast.41, bf16[1,1,640,1024]{3,2,1,0:T(8,128)(2,1)S(1)} %copy-done), kind=kOutput, calls=%fused_computation.9 | convolution fusion | flops 4701290496 | bytes 13238272 | tf_op jit(solution)/shard_map/dot_general | solution.py:47
  156.1 9.5 %fusion.5 = bf16[640,3584]{1,0:T(8,128)(2,1)} fusion(bf16[1,1024,3584]{2,1,0:T(8,128)(2,1)} %param.6, bf16[1,1,640,1024]{3,2,1,0:T(8,128)(2,1)S(1)} %copy-done), kind=kOutput, calls=%fused_computation.10 | convolution fusion | flops 4699914240 | bytes 13238272 | tf_op jit(solution)/shard_map/dot_general | solution.py:25
  165.7 4.6 %all-to-all-start = ((bf16[8,80,3584]{2,1,0:T(8,128)(2,1)}), bf16[8,80,3584]{2,1,0:T(8,128)(2,1)}, u32[]{:S(2)}, u32[]{:S(2)}) async-start(bf16[8,80,3584]{2,1,0:T(8,128)(2,1)} %bitcast.43), calls=%async_computation | async-start | bytes 9175040 | tf_op jit(solution)/shard_map/all_to_all | solution.py:33
  170.3 100.5 %all-to-all-done = bf16[8,80,3584]{2,1,0:T(8,128)(2,1)} async-done(((bf16[8,80,3584]{2,1,0:T(8,128)(2,1)}), bf16[8,80,3584]{2,1,0:T(8,128)(2,1)}, u32[]{:S(2)}, u32[]{:S(2)}) %all-to-all-start) | async-done | bytes 4587552 | tf_op jit(solution)/shard_map/all_to_all | solution.py:33
  270.8 10.8 %gather_fusion = bf16[512,3584]{1,0:T(8,128)(2,1)} fusion(bf16[640,3584]{1,0:T(8,128)(2,1)} %bitcast.3, s32[1024]{0:T(1024)S(1)} %pad_clamp_fusion), kind=kCustom, calls=%fused_computation | custom fusion | bytes 7342080 | tf_op jit(solution)/shard_map/gather | solution.py:35
  281.5 7.1 %reshape.80 = bf16[128,4,3584]{2,1,0:T(4,128)(2,1)} reshape(bf16[512,3584]{1,0:T(8,128)(2,1)} %gather_fusion) | data formatting | bytes 7340032 | tf_op jit(solution)/shard_map/reshape | solution.py:36
  288.6 6.2 %fusion.11 = f32[128,1,4]{2,1,0:T(1,128)S(1)} fusion(bf16[128,4,3584]{2,1,0:T(4,128)(2,1)} %reshape.80, bf16[128,3584,1]{1,0,2:T(8,128)(2,1)S(1)} %bitcast.45), kind=kOutput, calls=%fused_computation.14 | convolution fusion | flops 3670016 | bytes 4589568 | tf_op jit(solution)/shard_map/td,tkd->tk/dot_general | solution.py:40
  294.8 0.7 copy.18
  295.4 8.3 %multiply_reduce_fusion = bf16[128,3584]{1,0:T(8,128)(2,1)} fusion(bf16[128,4,3584]{2,1,0:T(4,128)(2,1)} %reshape.80, f32[128,4]{1,0:T(8,128)S(1)} %copy.11), kind=kLoop, calls=%fused_computation.8 | loop fusion | flops 5046272 | bytes 4589568 | tf_op jit(solution)/shard_map/reduce_sum | solution.py:37
  303.7 10.5 %fusion.16 = bf16[1,1,640,1024]{3,2,1,0:T(8,128)(2,1)} fusion(bf16[640,3584]{1,0:T(8,128)(2,1)} %bitcast.42, bf16[1,1024,3584]{2,1,0:T(8,128)(2,1)} %param.6), kind=kOutput, calls=%fused_computation.17 | convolution fusion | flops 4698275840 | bytes 13238272 | tf_op jit(solution)/shard_map/dot_general | solution.py:42
  314.2 3.8 %copy.16 = bf16[1,256,3584]{2,1,0:T(8,128)(2,1)} copy(bf16[1,256,3584]{1,2,0:T(8,128)(2,1)} %bitcast.44) | data formatting | bytes 3670016
  (16 shorter events, 0.4 us)
Async XLA Ops:
  7.2 140.9 %copy-start = (bf16[1,1,640,1024]{3,2,1,0:T(8,128)(2,1)S(1)}, bf16[1,1,640,1024]{3,2,1,0:T(8,128)(2,1)}, u32[]{:S(2)}) copy-start(bf16[1,1,640,1024]{3,2,1,0:T(8,128)(2,1)} %param.5) | copy-start | bytes 3932164
  7.2 307.0 %reduce-scatter.2.cloned.1.call-start = ((), (), s32[]{:S(2)}) async-start(), calls=%async_computation.3 | async-start | bytes 9175040 | tf_op jit(solution)/shard_map/reduce_scatter | solution.py:46
  145.9 2.2 copy-start.1
  165.7 105.1 %all-to-all-start = ((bf16[8,80,3584]{2,1,0:T(8,128)(2,1)}), bf16[8,80,3584]{2,1,0:T(8,128)(2,1)}, u32[]{:S(2)}, u32[]{:S(2)}) async-start(bf16[8,80,3584]{2,1,0:T(8,128)(2,1)} %bitcast.43), calls=%async_computation | async-start | bytes 9175040 | tf_op jit(solution)/shard_map/all_to_all | solution.py:33
  281.5 7.1 %copy-start.2 = (bf16[128,3584]{1,0:T(8,128)(2,1)S(1)}, bf16[128,3584]{1,0:T(8,128)(2,1)}, u32[]{:S(2)}) copy-start(bf16[128,3584]{1,0:T(8,128)(2,1)} %param.9) | copy-start | bytes 2752516
Sparse Core Ops, SparseCore 0:
  156.2 64.1 reduce-scatter.1
where the time goes:
time: 326 us; the launch traced here: 325 us
  blocking collectives  109 us (33%)
  waiting for transfers between devices  100 us (31%)
  local copies, waits for them, and re-layouts  41.1 us (13%)
  matrix products  34.2 us (10%)
  other arithmetic  21.1 us (6%)
  between operations  14.1 us (4%)
  starting transfers between devices  4.65 us (1%)
    all_to_all x1, blocking collectives, local(): lax.all_to_all(outgoing, 'expert', split_axis=0, concat_axis=0, tiled=True)  109 us
    all_to_all x1, waiting for transfers between devices, local(): lax.all_to_all(by_source, 'expert', split_axis=0, concat_axis=0, tiled=True)  100 us
    mul x2, local copies, waits for them, and re-layouts, local(): gate_prob[:, :, None] * cotangent.astype(jnp.float32)[:, None, :]  14.2 us
    scatter x1, other arithmetic, local(): outgoing.at[slot_index]  10.9 us
    gather x1, local copies, waits for them, and re-layouts, local(): picked = returned.reshape(experts * capacity, features)[slot_index]  10.8 us
    dot_general x1, matrix products, local(): lax.dot_general(slot_grads, weight, (((1,), (1,)), ((), ())), preferred_e...  10.5 us
    dot_general x1, matrix products, local(): jnp.dot(rows_in, weight, preferred_element_type=jnp.float32)  9.55 us
    reduce_sum x1, other arithmetic, local(): jnp.sum(gate_prob[:, :, None] * picked.astype(jnp.float32), axis=1)  8.26 us
  transfers between devices with their start and end apart: 2, of which 1 were waited for; matrix products, arithmetic and copies ran while one was open for 16% of the time, Pallas kernels for 0%

commit v1 on v0

v1 whole, which is shorter than its diff:
```python
import jax
import jax.numpy as jnp
from jax import lax
from jax.sharding import PartitionSpec as P

BF16 = jnp.bfloat16
F32 = jnp.float32
CHUNKS = 2


def split_expert(n):
    nx = 1
    while nx * nx * 4 <= n:
        nx *= 2
    while n % nx:
        nx -= 1
    return n // nx, nx


def dot(a, b):
    return jnp.dot(a, b, preferred_element_type=F32)


def build(n_dp, n_expert):
    nz, nx = split_expert(n_expert)
    nc = 2 if n_dp % 2 == 0 else 1
    ny = n_dp // nc

    def along_z(move):
        return [
            (z * nx + x, move(z) * nx + x)
            for z in range(nz)
            for x in range(nx)
            if move(z) is not None
        ]

    def shift_z(r):
        return along_z(lambda z: (z + r) % nz)

    def line(step, first, last):
        return along_z(lambda z: z + step if first <= z <= last and 0 <= z + step < nz else None)

    def shift_x(q):
        return [(z * nx + x, z * nx + (x + q) % nx) for z in range(nz) for x in range(nx)]

    def shift_y(o):
        return [(y * nc + c, (y + o) % ny * nc + c) for y in range(ny) for c in range(nc)]

    swap_core = [(y * nc + c, y * nc + (c + 1) % nc) for y in range(ny) for c in range(nc)]

    def over_expert(a, pairs):
        return lax.ppermute(a, "expert", pairs)

    def over_dp(a, pairs):
        return lax.ppermute(a, "dp", pairs)

    def local(hidden_in, down_weight, routes, gate_prob, cotangent):
        me = lax.axis_index("expert")
        z, x = me // nx, me % nx
        dp = lax.axis_index("dp")
        y, core = dp // nc, dp % nc
        cap = hidden_in.shape[2] // n_expert
        ff = hidden_in.shape[3]
        tok, top = routes.shape
        features = down_weight.shape[2]
        width = features // CHUNKS
        weight = down_weight[0]

        table = jnp.concatenate([routes.astype(F32), gate_prob], axis=1).T
        tables = jnp.stack([table] + [over_expert(table, shift_z(r)) for r in range(1, nz)])
        line_routes = tables[:, :top].astype(jnp.int32)
        line_gates = tables[:, top:]
        here = z * nx + (x + jnp.arange(nx, dtype=jnp.int32)) % nx

        def slots_of(routed, ids):
            named = routed[..., None, :, :] == ids[:, None, None]
            match = named.any(axis=-2)
            count = match.astype(jnp.int32)
            before = jnp.cumsum(count, axis=-1) - count
            slot = jnp.arange(cap, dtype=jnp.int32)[:, None]
            onehot = match[..., None, :] & (before[..., None, :] == slot)
            return onehot, named

        onehot, named = slots_of(line_routes, here)
        token_gate = jnp.sum(jnp.where(named, line_gates[:, None], 0.0), axis=-2)
        slot_gate = jnp.sum(jnp.where(onehot, token_gate[..., None, :], 0.0), axis=-1)
        pick = onehot.astype(BF16).reshape(nz, nx * cap, tok)
        spread = jnp.where(onehot, token_gate[..., None, :], 0.0).astype(BF16)
        spread = spread.reshape(nz, nx * cap, tok)
        slot_gate = slot_gate.reshape(nz, nx * cap, 1)

        blocks = hidden_in.reshape(nz, nx, cap, ff)
        order_z = (z - jnp.arange(nz)) % nz
        order_x = (x + jnp.arange(nx)) % nx
        hidden = blocks[order_z][:, order_x].transpose(1, 0, 2, 3).reshape(-1, ff)

        rows = ff // n_dp
        hidden_t = hidden.T.reshape(ny, nc, rows, -1)
        hidden_t = hidden_t[(y + 1 + jnp.arange(ny)) % ny][:, (core + 1 + jnp.arange(nc)) % nc]
        hidden_t = hidden_t.transpose(1, 0, 2, 3).reshape(nc, ny * rows, -1)

        line_rows = nz * cap

        def dispatch(cot):
            low, high = [cot], [cot]
            for k in range(1, nz):
                low.append(over_expert(low[-1], line(1, k - 1, nz - 2)))
                high.append(over_expert(high[-1], line(-1, 1, nz - k)))
            held = [cot] + [jnp.where(z >= r, low[r], high[nz - r]) for r in range(1, nz)]
            held = jnp.stack(held)
            packed = lax.dot_general(
                pick, held, (((2,), (1,)), ((0,), (0,))), preferred_element_type=F32
            )
            packed = (packed * slot_gate).astype(BF16).reshape(nz, nx, cap, -1)
            out = [packed[:, 0].reshape(line_rows, -1)]
            for q in range(1, nx):
                out.append(over_expert(packed[:, q].reshape(line_rows, -1), shift_x(q)))
            return [out[-q % nx] for q in range(nx)]

        def combine(weight_c):
            produced = dot(hidden, weight_c).astype(BF16).reshape(nx, line_rows, -1)
            got = [produced[0]]
            for q in range(1, nx):
                got.append(over_expert(produced[q], shift_x(q)))
            rows_in = jnp.stack([got[-q % nx].reshape(nz, cap, -1) for q in range(nx)], axis=1)
            rows_in = rows_in.reshape(nz, nx * cap, -1)
            part = lax.dot_general(
                spread, rows_in, (((1,), (1,)), ((0,), (0,))), preferred_element_type=F32
            ).astype(BF16)
            up, down = None, None
            for k in range(1, nz):
                mine = part[k] if up is None else part[k] + up
                up = over_expert(mine, line(1, 0, k - 1))
                mine = part[nz - k] if down is None else part[nz - k] + down
                down = over_expert(mine, line(-1, nz - k, nz - 1))
            total = part[0].astype(F32)
            for other in (up, down):
                if other is not None:
                    total = total + other.astype(F32)
            return total.astype(BF16)

        def weight_part(slot_rows):
            give = dot(hidden_t[0], slot_rows).astype(BF16)
            if nc == 2:
                got = over_dp(give, swap_core)
                keep = dot(hidden_t[1], slot_rows).astype(BF16)
                keep = (keep.astype(F32) + got.astype(F32)).astype(BF16)
            else:
                keep = give
            keep = keep.reshape(ny, rows, -1)
            total = keep[ny - 1].astype(F32)
            for o in range(1, ny):
                total = total + over_dp(keep[o - 1], shift_y(o)).astype(F32)
            return total.astype(BF16)

        combined, weight_grad, slot_grads = [], [], []
        for c in range(CHUNKS):
            columns = slice(c * width, (c + 1) * width)
            slot_rows = jnp.concatenate(dispatch(cotangent[:, columns]), axis=0)
            slot_grads.append(slot_rows)
            combined.append(combine(weight[:, columns]))
            weight_grad.append(weight_part(slot_rows))

        hidden_grad = 0.0
        for c in range(CHUNKS):
            columns = slice(c * width, (c + 1) * width)
            hidden_grad = hidden_grad + lax.dot_general(
                slot_grads[c], weight[:, columns], (((1,), (1,)), ((), ())),
                preferred_element_type=F32,
            )
        scalars = jnp.sum(hidden_grad * hidden.astype(F32), axis=1).reshape(nx, line_rows)
        out = hidden_grad.astype(BF16).reshape(nx, nz, cap, ff)
        out = out[(jnp.arange(nx) - x) % nx][:, (z - jnp.arange(nz)) % nz]
        out = out.transpose(1, 0, 2, 3).reshape(hidden_in.shape)

        back = [scalars[0]] + [over_expert(scalars[q], shift_x(q)) for q in range(1, nx)]
        back = jnp.stack(back).reshape(nx, nz, cap)
        home = [back[:, 0]] + [over_expert(back[:, r], shift_z(-r)) for r in range(1, nz)]
        home = jnp.stack(home).reshape(n_expert, cap)
        far_z = (z + jnp.arange(nz, dtype=jnp.int32)) % nz
        far_x = (x - jnp.arange(nx, dtype=jnp.int32)) % nx
        ids = (far_z[:, None] * nx + far_x[None, :]).reshape(-1)
        mine, said = slots_of(routes.T, ids)
        by_token = jnp.sum(jnp.where(mine, home[:, :, None], 0.0), axis=1)
        gate_grad = jnp.sum(jnp.where(said, by_token[:, None], 0.0), axis=0).T / gate_prob
        return (
            jnp.concatenate(combined, axis=1),
            gate_grad,
            out,
            jnp.concatenate(weight_grad, axis=1)[None],
        )

    return local


def solution(mesh):
    in_specs = (
        P("expert", "dp", None, None),
        P("expert", None, None),
        P(("dp", "expert"), None),
        P(("dp", "expert"), None),
        P(("dp", "expert"), None),
    )
    out_specs = (
        P(("dp", "expert"), None),
        P(("dp", "expert"), None),
        P("expert", "dp", None, None),
        P("expert", "dp", None),
    )
    local = build(mesh.shape["dp"], mesh.shape["expert"])
    return jax.shard_map(local, mesh=mesh, in_specs=in_specs, out_specs=out_specs, check_vma=False)
```

time: 326 us -> 239 us (0.73)
  blocking collectives: 109 us -> 0 us
  starting transfers between devices: 4.65 us -> 77.8 us
  local copies, waits for them, and re-layouts: 41.1 us -> 19.8 us
  waiting for transfers between devices: 100 us -> 78.7 us
  between operations: 14.1 us -> 1.56 us
  other arithmetic: 21.1 us -> 25.3 us
    all_to_all x1 -> x0, blocking collectives: 109 us -> none  [local(): lax.all_to_all(outgoing, 'expert', split_axis=0, concat_axis=0, tiled=True)]
    all_to_all x1 -> x0, waiting for transfers between devices: 100 us -> none  [local(): lax.all_to_all(by_source, 'expert', split_axis=0, concat_axis=0, tiled=True)]
    ppermute x0 -> x39, waiting for transfers between devices: none -> 78.7 us  [the longest x35 44.8 us: over_expert(): return lax.ppermute(a, 'expert', pairs)]
    ppermute x0 -> x39, starting transfers between devices: none -> 77.8 us  [the longest x35 74.2 us: over_expert(): return lax.ppermute(a, 'expert', pairs)]
    mul x5 -> x1, local copies, waits for them, and re-layouts: 14.5 us -> 0.09 us  [dispatch(): packed = (packed * slot_gate).astype(BF16).reshape(nz, nx, cap, -1)]
    scatter x1 -> x0, other arithmetic: 10.9 us -> none  [local(): outgoing.at[slot_index]]
    convert_element_type x1 -> x11, other arithmetic: 0.01 us -> 8.22 us  [the longest x2 3.92 us: weight_part(): keep = (keep.astype(F32) + got.astype(F32)).astype(BF16)]
    reduce_sum x2 -> x4, other arithmetic: 8.35 us -> 0.56 us  [the longest x1 0.23 us: local(): jnp.sum(jnp.where(onehot, token_gate[..., None, :], 0.0), axis=-1)]
  transfers between devices with their start and end apart: 2 -> 39, of which waited for: 1 -> 12; matrix products, arithmetic and copies ran while one was open for 16% -> 32% of each run, Pallas kernels for 0% -> 0%
where the time goes in v1:
time: 239 us; the launch traced here: 238 us
  waiting for transfers between devices  78.7 us (33%)
  starting transfers between devices  77.8 us (33%)
  matrix products  34.7 us (15%)
  other arithmetic  25.3 us (11%)
  local copies, waits for them, and re-layouts  19.8 us (8%)
    ppermute x35, starting transfers between devices, over_expert(): return lax.ppermute(a, 'expert', pairs)  74.2 us
    ppermute x35, waiting for transfers between devices, over_expert(): return lax.ppermute(a, 'expert', pairs)  44.8 us
    ppermute x4, waiting for transfers between devices, over_dp(): return lax.ppermute(a, 'dp', pairs)  33.9 us
    dot_general x6, matrix products, dot(): return jnp.dot(a, b, preferred_element_type=F32)  25.4 us
    dot_general x2, matrix products, local(): lax.dot_general(slot_grads[c], weight[:, columns], (((1,), (1,)), ((), ()...  6.34 us
  transfers between devices with their start and end apart: 39, of which 12 were waited for; matrix products, arithmetic and copies ran while one was open for 32% of the time, Pallas kernels for 0%

profile of v1, /device:TPU:0, one launch (start us, length us, event | category | flops | bytes accessed | tf_op | source)
XLA Modules:
  0.0 237.8 jit_solution(4183506844708295139)
XLA Ops:
  2.7 3.0 %collective-permute-start = (f32[8,128]{1,0:T(8,128)}, f32[8,128]{1,0:T(8,128)}, u32[]{:S(2)}, u32[]{:S(2)}) collective-permute-start(f32[8,128]{1,0:T(8,128)} %get-tuple-element.41), channel_id=1, source_target_pairs={{0,2},{1,3},{2,4},{3,5},{4,6},{5,7},{6,0},{7,1},{8,10},{9,11},{10,... | collective-permute-start | bytes 12296 | tf_op jit(solution)/shard_map/ppermute | solution.py:52
  5.7 2.6 %collective-permute-start.1 = (f32[8,128]{1,0:T(8,128)}, f32[8,128]{1,0:T(8,128)}, u32[]{:S(2)}, u32[]{:S(2)}) collective-permute-start(f32[8,128]{1,0:T(8,128)} %get-tuple-element.41), channel_id=1, source_target_pairs={{0,4},{1,5},{2,6},{3,7},{4,0},{5,1},{6,2},{7,3},{8,12},{9,13},{10,... | collective-permute-start | bytes 12296 | tf_op jit(solution)/shard_map/ppermute | solution.py:52
  13.3 4.6 %collective-permute-start.17 = (bf16[128,1792]{1,0:T(8,128)(2,1)S(1)}, bf16[128,1792]{1,0:T(8,128)(2,1)S(1)}, u32[]{:S(2)}, u32[]{:S(2)}) collective-permute-start(bf16[128,1792]{1,0:T(8,128)(2,1)S(1)} %get-tuple-element.31), channel_id=1, source_target_pairs={{0,2},{1,3},{2,4},{3,5},{4,6},{5,7},{8,10},{9,11},{10,12},{11,13},... | collective-permute-start | bytes 1376264 | tf_op jit(solution)/shard_map/ppermute | solution.py:52
  20.3 6.0 %fusion.8 = bf16[640,1792]{1,0:T(8,128)(2,1)} fusion(bf16[640,1024]{1,0:T(8,128)(2,1)S(1)} %bitcast.141, bf16[1024,3584]{1,0:T(8,128)(2,1)} %bitcast.170), kind=kOutput, calls=%fused_computation.18 | convolution fusion | flops 2349957120 | bytes 7274496 | tf_op jit(solution)/shard_map/dot_general | solution.py:21
  26.3 5.9 %fusion.11 = bf16[640,1792]{1,0:T(8,128)(2,1)} fusion(bf16[640,1024]{1,0:T(8,128)(2,1)S(1)} %bitcast.142, bf16[1024,3584]{1,0:T(8,128)(2,1)} %bitcast.171), kind=kOutput, calls=%fused_computation.19 | convolution fusion | flops 2349957120 | bytes 7274496 | tf_op jit(solution)/shard_map/dot_general | solution.py:21
  39.9 2.9 %fusion.84 = (bf16[320,1792]{1,0:T(8,128)(2,1)S(1)}, bf16[320,1792]{1,0:T(8,128)(2,1)}) fusion(bf16[640,1792]{1,0:T(8,128)(2,1)} %fusion.8), kind=kLoop, calls=%fused_computation.180 | loop fusion | bytes 4587520 | tf_op jit(solution)/shard_map/slice | solution.py:122
  46.3 5.3 %collective-permute-start.24 = (bf16[128,1792]{1,0:T(8,128)(2,1)}, bf16[128,1792]{1,0:T(8,128)(2,1)}, u32[]{:S(2)}, u32[]{:S(2)}) collective-permute-start(bf16[128,1792]{1,0:T(8,128)(2,1)} %get-tuple-element.30), channel_id=1, source_target_pairs={{0,2},{1,3},{2,4},{3,5},{4,6},{5,7},{8,10},{9,11},{10,12},{11,13},... | collective-permute-start | bytes 1376264 | tf_op jit(solution)/shard_map/ppermute | solution.py:52
  62.3 8.6 %collective-permute-done.19 = bf16[128,1792]{1,0:T(8,128)(2,1)} collective-permute-done((bf16[128,1792]{1,0:T(8,128)(2,1)}, bf16[128,1792]{1,0:T(8,128)(2,1)}, u32[]{:S(2)}, u32[]{:S(2)}) %collective-permute-start.19) | collective-permute-done | bytes 458784 | tf_op jit(solution)/shard_map/ppermute | solution.py:52
  73.3 4.3 %collective-permute-done.26 = bf16[128,1792]{1,0:T(8,128)(2,1)S(1)} collective-permute-done((bf16[128,1792]{1,0:T(8,128)(2,1)}, bf16[128,1792]{1,0:T(8,128)(2,1)S(1)}, u32[]{:S(2)}, u32[]{:S(2)}) %collective-permute-start.26) | collective-permute-done | bytes 458784 | tf_op jit(solution)/shard_map/ppermute | solution.py:52
  83.9 17.6 %collective-permute-done.10 = bf16[320,1792]{1,0:T(8,128)(2,1)S(1)} collective-permute-done((bf16[320,1792]{1,0:T(8,128)(2,1)}, bf16[320,1792]{1,0:T(8,128)(2,1)S(1)}, u32[]{:S(2)}, u32[]{:S(2)}) %collective-permute-start.10) | collective-permute-done | bytes 1146912 | tf_op jit(solution)/shard_map/ppermute | solution.py:52
  115.9 4.4 %collective-permute-start.5 = (bf16[128,1792]{1,0:T(8,128)(2,1)S(1)}, bf16[128,1792]{1,0:T(8,128)(2,1)S(1)}, u32[]{:S(2)}, u32[]{:S(2)}) collective-permute-start(bf16[128,1792]{1,0:T(8,128)(2,1)S(1)} %get-tuple-element.16), channel_id=1, source_target_pairs={{0,2},{1,3},{2,4},{3,5},{8,10},{9,11},{10,12},{11,13},{16,18},{17,... | collective-permute-start | bytes 1376264 | tf_op jit(solution)/shard_map/ppermute | solution.py:52
  120.3 3.8 %collective-permute-done.11 = bf16[128,1792]{1,0:T(8,128)(2,1)S(1)} collective-permute-done((bf16[128,1792]{1,0:T(8,128)(2,1)S(1)}, bf16[128,1792]{1,0:T(8,128)(2,1)S(1)}, u32[]{:S(2)}, u32[]{:S(2)}) %collective-permute-start.11) | collective-permute-done | bytes 458784 | tf_op jit(solution)/shard_map/ppermute | solution.py:52
  124.9 5.3 %collective-permute-start.12 = (bf16[128,1792]{1,0:T(8,128)(2,1)S(1)}, bf16[128,1792]{1,0:T(8,128)(2,1)S(1)}, u32[]{:S(2)}, u32[]{:S(2)}) collective-permute-start(bf16[128,1792]{1,0:T(8,128)(2,1)S(1)} %get-tuple-element.22), channel_id=1, source_target_pairs={{0,2},{1,3},{2,4},{3,5},{8,10},{9,11},{10,12},{11,13},{16,18},{17,... | collective-permute-start | bytes 1376264 | tf_op jit(solution)/shard_map/ppermute | solution.py:52
  130.2 3.7 %collective-permute-done.5 = bf16[128,1792]{1,0:T(8,128)(2,1)S(1)} collective-permute-done((bf16[128,1792]{1,0:T(8,128)(2,1)S(1)}, bf16[128,1792]{1,0:T(8,128)(2,1)S(1)}, u32[]{:S(2)}, u32[]{:S(2)}) %collective-permute-start.5) | collective-permute-done | bytes 458784 | tf_op jit(solution)/shard_map/ppermute | solution.py:52
  135.7 9.3 %collective-permute-start.6 = (bf16[128,1792]{1,0:T(8,128)(2,1)}, bf16[128,1792]{1,0:T(8,128)(2,1)}, u32[]{:S(2)}, u32[]{:S(2)}) collective-permute-start(bf16[128,1792]{1,0:T(8,128)(2,1)} %get-tuple-element.14), channel_id=1, source_target_pairs={{0,2},{1,3},{2,4},{3,5},{4,6},{5,7},{8,10},{9,11},{10,12},{11,13},... | collective-permute-start | bytes 1376264 | tf_op jit(solution)/shard_map/ppermute | solution.py:52
  147.7 6.5 %collective-permute-start.13 = (bf16[128,1792]{1,0:T(8,128)(2,1)}, bf16[128,1792]{1,0:T(8,128)(2,1)}, u32[]{:S(2)}, u32[]{:S(2)}) collective-permute-start(bf16[128,1792]{1,0:T(8,128)(2,1)} %get-tuple-element.20), channel_id=1, source_target_pairs={{0,2},{1,3},{2,4},{3,5},{4,6},{5,7},{8,10},{9,11},{10,12},{11,13},... | collective-permute-start | bytes 1376264 | tf_op jit(solution)/shard_map/ppermute | solution.py:52
  155.5 2.9 %convolution_convert_fusion.4 = bf16[512,1792]{1,0:T(8,128)(2,1)} fusion(bf16[512,640]{1,0:T(8,128)(2,1)S(1)} %bitcast.163, bf16[320,1792]{1,0:T(8,128)(2,1)S(1)} %collective-permute-done.23, bf16[320,1792]{1,0:T(8,128)(2,1)S(1)} %bitcast.151), kind=kOutput, calls=%fused_computation.24 | convolution fusion | flops 1179910144 | bytes 4784128 | tf_op jit(solution)/shard_map/dot_general | solution.py:21
  159.5 2.6 %fusion = f32[640,1024]{1,0:T(8,128)S(1)} fusion(bf16[1024,3584]{1,0:T(8,128)(2,1)S(1)} %bitcast.174, bf16[320,1792]{1,0:T(8,128)(2,1)S(1)} %collective-permute-done.30, bf16[320,1792]{1,0:T(8,128)(2,1)S(1)} %bitcast.154), kind=kOutput, calls=%fused_computation.10 | convolution fusion | flops 2353397760 | bytes 8585216 | tf_op jit(solution)/shard_map/dot_general | solution.py:167
  162.1 3.8 %fusion.81 = (bf16[640,1024]{1,0:T(8,128)(2,1)}, f32[640]{0:T(1024)S(1)}) fusion(bf16[2,4,80,1024]{3,2,1,0:T(8,128)(2,1)S(1)} %gather_fusion.1, f32[640,1024]{1,0:T(8,128)S(1)} %fusion, bf16[1024,3584]{1,0:T(8,128)(2,1)S(1)} %bitcast.175, bf16[320,1792]{1,0:T(8,128)(2,1)S(1)} %collective-permute-done.23, bf16[320,1792]{1,0:T(8,128)(2,1)S(1)} %bitcast.152), kind=kOutput, calls=%fused_computation.177 | convolution fusion | flops 2356674048 | bytes 11209216 | tf_op jit(solution)/shard_map/dot_general | solution.py:167
  169.8 4.8 %convolution_convert_fusion.2 = bf16[512,1792]{1,0:T(8,128)(2,1)} fusion(bf16[512,640]{1,0:T(8,128)(2,1)} %bitcast.162, bf16[320,1792]{1,0:T(8,128)(2,1)} %copy-done.27, bf16[320,1792]{1,0:T(8,128)(2,1)} %bitcast.155), kind=kOutput, calls=%fused_computation.22 | convolution fusion | flops 1179910144 | bytes 4784128 | tf_op jit(solution)/shard_map/dot_general | solution.py:21
  174.6 2.9 %convolution_convert_fusion.5 = bf16[512,1792]{1,0:T(8,128)(2,1)} fusion(bf16[512,640]{1,0:T(8,128)(2,1)S(1)} %bitcast.160, bf16[320,1792]{1,0:T(8,128)(2,1)S(1)} %copy-done.26, bf16[320,1792]{1,0:T(8,128)(2,1)S(1)} %bitcast.153), kind=kOutput, calls=%fused_computation.25 | convolution fusion | flops 1179910144 | bytes 4784128 | tf_op jit(solution)/shard_map/dot_general | solution.py:21
  177.5 2.9 %convolution_convert_fusion.3 = bf16[512,1792]{1,0:T(8,128)(2,1)} fusion(bf16[512,640]{1,0:T(8,128)(2,1)S(1)} %bitcast.161, bf16[320,1792]{1,0:T(8,128)(2,1)S(1)} %copy-done.28, bf16[320,1792]{1,0:T(8,128)(2,1)S(1)} %bitcast.156), kind=kOutput, calls=%fused_computation.23 | convolution fusion | flops 1179910144 | bytes 4784128 | tf_op jit(solution)/shard_map/dot_general | solution.py:21
  202.0 17.4 %collective-permute-done.36 = bf16[256,1792]{1,0:T(8,128)(2,1)S(1)} collective-permute-done((bf16[256,1792]{1,0:T(8,128)(2,1)S(1)}, bf16[256,1792]{1,0:T(8,128)(2,1)S(1)}, u32[]{:S(2)}, u32[]{:S(2)}) %collective-permute-start.36) | collective-permute-done | bytes 917536 | tf_op jit(solution)/shard_map/ppermute | solution.py:55
  219.7 16.5 %collective-permute-done.38 = bf16[256,1792]{1,0:T(8,128)(2,1)S(1)} collective-permute-done((bf16[256,1792]{1,0:T(8,128)(2,1)S(1)}, bf16[256,1792]{1,0:T(8,128)(2,1)S(1)}, u32[]{:S(2)}, u32[]{:S(2)}) %collective-permute-start.38) | collective-permute-done | bytes 917536 | tf_op jit(solution)/shard_map/ppermute | solution.py:55
  (209 shorter events, 88.6 us)
Async XLA Ops:
  2.7 42.3 %collective-permute-start = (f32[8,128]{1,0:T(8,128)}, f32[8,128]{1,0:T(8,128)}, u32[]{:S(2)}, u32[]{:S(2)}) collective-permute-start(f32[8,128]{1,0:T(8,128)} %get-tuple-element.41), channel_id=1, source_target_pairs={{0,2},{1,3},{2,4},{3,5},{4,6},{5,7},{6,0},{7,1},{8,10},{9,11},{10,... | collective-permute-start | bytes 12296 | tf_op jit(solution)/shard_map/ppermute | solution.py:52
  5.7 40.6 %collective-permute-start.1 = (f32[8,128]{1,0:T(8,128)}, f32[8,128]{1,0:T(8,128)}, u32[]{:S(2)}, u32[]{:S(2)}) collective-permute-start(f32[8,128]{1,0:T(8,128)} %get-tuple-element.41), channel_id=1, source_target_pairs={{0,4},{1,5},{2,6},{3,7},{4,0},{5,1},{6,2},{7,3},{8,12},{9,13},{10,... | collective-permute-start | bytes 12296 | tf_op jit(solution)/shard_map/ppermute | solution.py:52
  8.3 43.3 %collective-permute-start.2 = (f32[8,128]{1,0:T(8,128)}, f32[8,128]{1,0:T(8,128)}, u32[]{:S(2)}, u32[]{:S(2)}) collective-permute-start(f32[8,128]{1,0:T(8,128)} %get-tuple-element.41), channel_id=1, source_target_pairs={{0,6},{1,7},{2,0},{3,1},{4,2},{5,3},{6,4},{7,5},{8,14},{9,15},{10,... | collective-permute-start | bytes 12296 | tf_op jit(solution)/shard_map/ppermute | solution.py:52
  12.0 43.2 %collective-permute-start.18 = (bf16[128,1792]{1,0:T(8,128)(2,1)S(1)}, bf16[128,1792]{1,0:T(8,128)(2,1)}, u32[]{:S(2)}, u32[]{:S(2)}) collective-permute-start(bf16[128,1792]{1,0:T(8,128)(2,1)S(1)} %get-tuple-element.31), channel_id=1, source_target_pairs={{2,0},{3,1},{4,2},{5,3},{6,4},{7,5},{10,8},{11,9},{12,10},{13,11},... | collective-permute-start | bytes 1376264 | tf_op jit(solution)/shard_map/ppermute | solution.py:52
  13.3 43.2 %collective-permute-start.17 = (bf16[128,1792]{1,0:T(8,128)(2,1)S(1)}, bf16[128,1792]{1,0:T(8,128)(2,1)S(1)}, u32[]{:S(2)}, u32[]{:S(2)}) collective-permute-start(bf16[128,1792]{1,0:T(8,128)(2,1)S(1)} %get-tuple-element.31), channel_id=1, source_target_pairs={{0,2},{1,3},{2,4},{3,5},{4,6},{5,7},{8,10},{9,11},{10,12},{11,13},... | collective-permute-start | bytes 1376264 | tf_op jit(solution)/shard_map/ppermute | solution.py:52
  51.6 28.5 %collective-permute-start.3 = (bf16[320,1792]{1,0:T(8,128)(2,1)}, bf16[320,1792]{1,0:T(8,128)(2,1)}, u32[]{:S(2)}, u32[]{:S(2)}) collective-permute-start(bf16[320,1792]{1,0:T(8,128)(2,1)} %get-tuple-element.11), channel_id=1, source_target_pairs={{0,1},{1,0},{2,3},{3,2},{4,5},{5,4},{6,7},{7,6},{8,9},{9,8},{10,11... | collective-permute-start | bytes 3440648 | tf_op jit(solution)/shard_map/ppermute | solution.py:52
  58.6 42.9 %collective-permute-start.10 = (bf16[320,1792]{1,0:T(8,128)(2,1)}, bf16[320,1792]{1,0:T(8,128)(2,1)S(1)}, u32[]{:S(2)}, u32[]{:S(2)}) collective-permute-start(bf16[320,1792]{1,0:T(8,128)(2,1)} %get-tuple-element.13), channel_id=1, source_target_pairs={{0,1},{1,0},{2,3},{3,2},{4,5},{5,4},{6,7},{7,6},{8,9},{9,8},{10,11... | collective-permute-start | bytes 3440648 | tf_op jit(solution)/shard_map/ppermute | solution.py:52
  71.5 33.0 %collective-permute-start.22 = (bf16[128,1792]{1,0:T(8,128)(2,1)}, bf16[128,1792]{1,0:T(8,128)(2,1)S(1)}, u32[]{:S(2)}, u32[]{:S(2)}) collective-permute-start(bf16[128,1792]{1,0:T(8,128)(2,1)} %collective-permute-done.21), channel_id=1, source_target_pairs={{4,6},{5,7},{12,14},{13,15},{20,22},{21,23},{28,30},{29,31}} | collective-permute-start | bytes 1376264 | tf_op jit(solution)/shard_map/ppermute | solution.py:52
  77.6 28.9 %collective-permute-start.20 = (bf16[128,1792]{1,0:T(8,128)(2,1)}, bf16[128,1792]{1,0:T(8,128)(2,1)S(1)}, u32[]{:S(2)}, u32[]{:S(2)}) collective-permute-start(bf16[128,1792]{1,0:T(8,128)(2,1)} %collective-permute-done.19), channel_id=1, source_target_pairs={{2,0},{3,1},{10,8},{11,9},{18,16},{19,17},{26,24},{27,25}} | collective-permute-start | bytes 1376264 | tf_op jit(solution)/shard_map/ppermute | solution.py:52
  78.9 29.9 %collective-permute-start.29 = (bf16[128,1792]{1,0:T(8,128)(2,1)S(1)}, bf16[128,1792]{1,0:T(8,128)(2,1)S(1)}, u32[]{:S(2)}, u32[]{:S(2)}) collective-permute-start(bf16[128,1792]{1,0:T(8,128)(2,1)S(1)} %collective-permute-done.28), channel_id=1, source_target_pairs={{4,6},{5,7},{12,14},{13,15},{20,22},{21,23},{28,30},{29,31}} | collective-permute-start | bytes 1376264 | tf_op jit(solution)/shard_map/ppermute | solution.py:52
  80.2 30.8 %collective-permute-start.27 = (bf16[128,1792]{1,0:T(8,128)(2,1)S(1)}, bf16[128,1792]{1,0:T(8,128)(2,1)S(1)}, u32[]{:S(2)}, u32[]{:S(2)}) collective-permute-start(bf16[128,1792]{1,0:T(8,128)(2,1)S(1)} %collective-permute-done.26), channel_id=1, source_target_pairs={{2,0},{3,1},{10,8},{11,9},{18,16},{19,17},{26,24},{27,25}} | collective-permute-start | bytes 1376264 | tf_op jit(solution)/shard_map/ppermute | solution.py:52
  106.5 17.6 %collective-permute-start.11 = (bf16[128,1792]{1,0:T(8,128)(2,1)S(1)}, bf16[128,1792]{1,0:T(8,128)(2,1)S(1)}, u32[]{:S(2)}, u32[]{:S(2)}) collective-permute-start(bf16[128,1792]{1,0:T(8,128)(2,1)S(1)} %get-tuple-element.24), channel_id=1, source_target_pairs={{0,2},{1,3},{8,10},{9,11},{16,18},{17,19},{24,26},{25,27}} | collective-permute-start | bytes 1376264 | tf_op jit(solution)/shard_map/ppermute | solution.py:52
  111.0 43.2 %collective-permute-start.23 = (bf16[320,1792]{1,0:T(8,128)(2,1)S(1)}, bf16[320,1792]{1,0:T(8,128)(2,1)S(1)}, u32[]{:S(2)}, u32[]{:S(2)}) collective-permute-start(bf16[320,1792]{1,0:T(8,128)(2,1)S(1)} %bitcast.157), channel_id=1, source_target_pairs={{0,1},{1,0},{2,3},{3,2},{4,5},{5,4},{6,7},{7,6},{8,9},{9,8},{10,11... | collective-permute-start | bytes 3440648 | tf_op jit(solution)/shard_map/ppermute | solution.py:52
  114.3 45.2 %collective-permute-start.30 = (bf16[320,1792]{1,0:T(8,128)(2,1)S(1)}, bf16[320,1792]{1,0:T(8,128)(2,1)S(1)}, u32[]{:S(2)}, u32[]{:S(2)}) collective-permute-start(bf16[320,1792]{1,0:T(8,128)(2,1)S(1)} %bitcast.158), channel_id=1, source_target_pairs={{0,1},{1,0},{2,3},{3,2},{4,5},{5,4},{6,7},{7,6},{8,9},{9,8},{10,11... | collective-permute-start | bytes 3440648 | tf_op jit(solution)/shard_map/ppermute | solution.py:52
  115.9 18.1 %collective-permute-start.5 = (bf16[128,1792]{1,0:T(8,128)(2,1)S(1)}, bf16[128,1792]{1,0:T(8,128)(2,1)S(1)}, u32[]{:S(2)}, u32[]{:S(2)}) collective-permute-start(bf16[128,1792]{1,0:T(8,128)(2,1)S(1)} %get-tuple-element.16), channel_id=1, source_target_pairs={{0,2},{1,3},{2,4},{3,5},{8,10},{9,11},{10,12},{11,13},{16,18},{17,... | collective-permute-start | bytes 1376264 | tf_op jit(solution)/shard_map/ppermute | solution.py:52
  124.9 20.1 %collective-permute-start.12 = (bf16[128,1792]{1,0:T(8,128)(2,1)S(1)}, bf16[128,1792]{1,0:T(8,128)(2,1)S(1)}, u32[]{:S(2)}, u32[]{:S(2)}) collective-permute-start(bf16[128,1792]{1,0:T(8,128)(2,1)S(1)} %get-tuple-element.22), channel_id=1, source_target_pairs={{0,2},{1,3},{2,4},{3,5},{8,10},{9,11},{10,12},{11,13},{16,18},{17,... | collective-permute-start | bytes 1376264 | tf_op jit(solution)/shard_map/ppermute | solution.py:52
  135.7 44.8 %collective-permute-start.6 = (bf16[128,1792]{1,0:T(8,128)(2,1)}, bf16[128,1792]{1,0:T(8,128)(2,1)}, u32[]{:S(2)}, u32[]{:S(2)}) collective-permute-start(bf16[128,1792]{1,0:T(8,128)(2,1)} %get-tuple-element.14), channel_id=1, source_target_pairs={{0,2},{1,3},{2,4},{3,5},{4,6},{5,7},{8,10},{9,11},{10,12},{11,13},... | collective-permute-start | bytes 1376264 | tf_op jit(solution)/shard_map/ppermute | solution.py:52
  145.0 36.1 %collective-permute-start.9 = (bf16[128,1792]{1,0:T(8,128)(2,1)}, bf16[128,1792]{1,0:T(8,128)(2,1)}, u32[]{:S(2)}, u32[]{:S(2)}) collective-permute-start(bf16[128,1792]{1,0:T(8,128)(2,1)} %get-tuple-element.15), channel_id=1, source_target_pairs={{2,0},{3,1},{4,2},{5,3},{6,4},{7,5},{10,8},{11,9},{12,10},{13,11},... | collective-permute-start | bytes 1376264 | tf_op jit(solution)/shard_map/ppermute | solution.py:52
  147.7 36.3 %collective-permute-start.13 = (bf16[128,1792]{1,0:T(8,128)(2,1)}, bf16[128,1792]{1,0:T(8,128)(2,1)}, u32[]{:S(2)}, u32[]{:S(2)}) collective-permute-start(bf16[128,1792]{1,0:T(8,128)(2,1)} %get-tuple-element.20), channel_id=1, source_target_pairs={{0,2},{1,3},{2,4},{3,5},{4,6},{5,7},{8,10},{9,11},{10,12},{11,13},... | collective-permute-start | bytes 1376264 | tf_op jit(solution)/shard_map/ppermute | solution.py:52
  154.2 29.7 %collective-permute-start.16 = (bf16[128,1792]{1,0:T(8,128)(2,1)}, bf16[128,1792]{1,0:T(8,128)(2,1)}, u32[]{:S(2)}, u32[]{:S(2)}) collective-permute-start(bf16[128,1792]{1,0:T(8,128)(2,1)} %get-tuple-element.21), channel_id=1, source_target_pairs={{2,0},{3,1},{4,2},{5,3},{6,4},{7,5},{10,8},{11,9},{12,10},{13,11},... | collective-permute-start | bytes 1376264 | tf_op jit(solution)/shard_map/ppermute | solution.py:52
  159.5 34.6 %collective-permute-start.35 = (bf16[512,1792]{1,0:T(8,128)(2,1)}, bf16[512,1792]{1,0:T(8,128)(2,1)}, u32[]{:S(2)}, u32[]{:S(2)}) collective-permute-start(bf16[512,1792]{1,0:T(8,128)(2,1)} %convolution_convert_fusion.4), channel_id=1, source_target_pairs={{0,8},{8,0},{16,24},{24,16},{1,9},{9,1},{17,25},{25,17},{2,10},{10... | collective-permute-start | bytes 5505032 | tf_op jit(solution)/shard_map/ppermute | solution.py:55
  180.5 17.1 %collective-permute-start.37 = (bf16[512,1792]{1,0:T(8,128)(2,1)}, bf16[512,1792]{1,0:T(8,128)(2,1)}, u32[]{:S(2)}, u32[]{:S(2)}) collective-permute-start(bf16[512,1792]{1,0:T(8,128)(2,1)} %convolution_convert_fusion.2), channel_id=1, source_target_pairs={{0,8},{8,0},{16,24},{24,16},{1,9},{9,1},{17,25},{25,17},{2,10},{10... | collective-permute-start | bytes 5505032 | tf_op jit(solution)/shard_map/ppermute | solution.py:55
  196.1 23.4 %collective-permute-start.36 = (bf16[256,1792]{1,0:T(8,128)(2,1)S(1)}, bf16[256,1792]{1,0:T(8,128)(2,1)S(1)}, u32[]{:S(2)}, u32[]{:S(2)}) collective-permute-start(bf16[256,1792]{1,0:T(8,128)(2,1)S(1)} %slice.205), channel_id=1, source_target_pairs={{0,16},{8,24},{16,0},{24,8},{1,17},{9,25},{17,1},{25,9},{2,18},{10... | collective-permute-start | bytes 2752520 | tf_op jit(solution)/shard_map/ppermute | solution.py:55
  199.8 36.4 %collective-permute-start.38 = (bf16[256,1792]{1,0:T(8,128)(2,1)S(1)}, bf16[256,1792]{1,0:T(8,128)(2,1)S(1)}, u32[]{:S(2)}, u32[]{:S(2)}) collective-permute-start(bf16[256,1792]{1,0:T(8,128)(2,1)S(1)} %slice.207), channel_id=1, source_target_pairs={{0,16},{8,24},{16,0},{24,8},{1,17},{9,25},{17,1},{25,9},{2,18},{10... | collective-permute-start | bytes 2752520 | tf_op jit(solution)/shard_map/ppermute | solution.py:55
  (46 other events, 518.5 us)

commit v2 on v1

--- a/solution.py
+++ b/solution.py
@@ -1,11 +1,19 @@
+import math
+
 import jax
 import jax.numpy as jnp
 from jax import lax
+from jax.experimental import pallas as pl
+from jax.experimental.pallas import tpu as pltpu
 from jax.sharding import PartitionSpec as P
 
 BF16 = jnp.bfloat16
 F32 = jnp.float32
 CHUNKS = 2
+COST = 10**11
+COSTS = {'kept2': 1}
+LIMIT = 24
+LIMITS = {'hidden': 60, 'made': 60}
 
 
 def split_expert(n):
@@ -21,7 +29,7 @@
     return jnp.dot(a, b, preferred_element_type=F32)
 
 
-def build(n_dp, n_expert):
+def build_line(n_dp, n_expert):
     nz, nx = split_expert(n_expert)
     nc = 2 if n_dp % 2 == 0 else 1
     ny = n_dp // nc
@@ -193,6 +201,468 @@
     return local
 
 
+def nothing(*refs):
+    pass
+
+
+def after(x, *deps):
+    anywhere = pl.BlockSpec(memory_space=pl.ANY)
+    return pl.pallas_call(
+        nothing,
+        out_shape=jax.ShapeDtypeStruct(x.shape, x.dtype),
+        in_specs=[anywhere] * (1 + len(deps)),
+        out_specs=anywhere,
+        input_output_aliases={0: 0},
+        name="after",
+    )(x, *deps)
+
+
+def call(kernel, grid, ins, outs, scratch, scalars, deps, cost):
+    n_in, n_dep = len(ins), len(deps)
+    n_scalar = 0 if scalars is None else 1
+
+    def body(*refs):
+        first = n_scalar + n_in
+        kernel(*refs[:first], *refs[first + n_dep:])
+
+    specs = [pl.BlockSpec(block, index) for _, block, index in ins]
+    specs += [pl.BlockSpec(memory_space=pl.ANY)] * n_dep
+    return pl.pallas_call(
+        body,
+        out_shape=[jax.ShapeDtypeStruct(shape, dtype) for shape, dtype, _, _ in outs],
+        grid_spec=pltpu.PrefetchScalarGridSpec(
+            num_scalar_prefetch=n_scalar,
+            grid=grid,
+            in_specs=specs,
+            out_specs=[pl.BlockSpec(block, index) for _, _, block, index in outs],
+            scratch_shapes=list(scratch),
+        ),
+        compiler_params=pltpu.CompilerParams(vmem_limit_bytes=LIMITS.get(kernel.__name__, LIMIT) << 20),
+        cost_estimate=pl.CostEstimate(flops=cost, bytes_accessed=cost // 300, transcendentals=0),
+        name=kernel.__name__,
+    )(*([] if scalars is None else [scalars]), *[a for a, _, _ in ins], *deps)
+
+
+def build_tree(n_dp, n_expert):
+    nz, nx, nc, ny = 4, 2, 2, 2
+
+    def along_z(pairs):
+        return [(a * nx + x, b * nx + x) for a, b in pairs for x in range(nx)]
+
+    buddy = along_z([(0, 1), (1, 0), (2, 3), (3, 2)])
+    middle = along_z([(1, 2), (2, 1)])
+    skip = along_z([(0, 2), (2, 0), (1, 3), (3, 1)])
+    mirror = along_z([(0, 3), (3, 0), (1, 2), (2, 1)])
+    inward = along_z([(0, 1), (3, 2)])
+    outward = along_z([(1, 0), (2, 3)])
+    swap_x = [(e, e ^ 1) for e in range(n_expert)]
+    swap_core = [(d, d ^ 1) for d in range(n_dp)]
+    swap_y = [(d, d ^ 2) for d in range(n_dp)]
+
+    def over_expert(a, pairs):
+        return lax.ppermute(a, "expert", pairs)
+
+    def over_dp(a, pairs):
+        return lax.ppermute(a, "dp", pairs)
+
+    def local(hidden_in, down_weight, routes, gate_prob, cotangent):
+        me = lax.axis_index("expert")
+        z, x = me // nx, me % nx
+        dp = lax.axis_index("dp")
+        cap = hidden_in.shape[2] // n_expert
+        ff = hidden_in.shape[3]
+        tok, top = routes.shape
+        features = down_weight.shape[2]
+        tile = 512
+        tiles = features // tile
+        first = tiles // 2
+        begin, count = (0, first), (first, tiles - first)
+        widths = [n * tile for n in count]
+        spans = [(b * tile, (b + n) * tile) for b, n in zip(begin, count)]
+        half = 2 * cap
+        part = ff // n_dp
+        last, named = [], []
+
+        def chain(kernel, grid, ins, outs, scratch=(), deps=(), flops=0):
+            named.append(kernel.__name__)
+            cost = COSTS.get(f"{named[-1]}{named.count(named[-1])}", COST)
+            got = call(kernel, grid, ins, outs, scratch, scalars, tuple(last) + tuple(deps), cost)
+            last[:] = [got[0]]
+            return got
+
+        def hold(a, *deps):
+            a = after(a, *last, *deps)
+            last[:] = [a]
+            return a
+        blocks_in = hidden_in.reshape(n_expert, cap, ff)
+        is_middle = (z == 1) | (z == 2)
+        low = z < 2
+        order_z = jnp.stack([z, z ^ 1, jnp.where(low, 2, 1), jnp.where(low, 3, 0)])
+        order_x = jnp.stack([x, x ^ 1])
+        order = (order_z[None, :] * nx + order_x[:, None]).reshape(-1)
+        parts = jnp.stack([dp ^ 3, dp ^ 1, dp ^ 2, dp])
+        scalars = jnp.concatenate(
+            [order, parts, jnp.stack([is_middle.astype(jnp.int32), z * nx + x, z * nx + (x ^ 1)])]
+        ).astype(jnp.int32)
+        at_parts, at_middle, at_here = n_expert, n_expert + n_dp, n_expert + n_dp + 1
+
+        buddies = over_expert(cotangent, buddy)
+        mids = over_expert(cotangent, middle)
+        table = jnp.concatenate([routes.astype(F32), gate_prob], axis=1).T
+        pair = jnp.concatenate([table, over_expert(table, buddy)])
+        far_pair = over_expert(pair, skip)
+
+        def whole(a):
+            return (a, a.shape, lambda *_: (0,) * a.ndim)
+
+        def sliced(body, fixed):
+            def run(s, *refs):
+                kept, moving = refs[:fixed], refs[fixed:]
+                for k in range(moving[-1].shape[-1] // tile):
+                    body(s, *kept, *(ref.at[:, k * tile:(k + 1) * tile] for ref in moving))
+
+            run.__name__ = body.__name__
+            return run
+
+        def strip_of(a):
+            return (a, a.shape, lambda *_: (0, 0))
+
+        def strip_out(rows, c, dtype=BF16):
+            return ((rows, widths[c]), dtype, (rows, widths[c]), lambda *_: (0, 0))
+
+        def columns(a, first=0):
+            return (a, (a.shape[0], tile), lambda j, *_: (0, first + j))
+
+        def wide(rows, c, dtype=BF16):
+            return ((rows, widths[c]), dtype, (rows, tile), lambda j, *_: (0, j))
+
+        def full(rows, dtype=BF16):
+            return ((rows, features), dtype, (rows, tile), lambda j, *_: (0, j))
+
+        broad = features // 4
+
+        def broadly(rows):
+            return ((rows, features), BF16, (rows, broad), lambda j, *_: (0, j))
+
+        def product(q):
+            def made(s, *refs):
+                *given, w, near_ref, far_ref, last_ref, rows = refs
+
+                @pl.when(pl.program_id(0) == 0)
+                def _():
+                    for i, ref in enumerate(given):
+                        rows[i * cap:(i + 1) * cap] = ref[0]
+
+                out = dot(rows[...], w[0]).astype(BF16)
+                near_ref[...] = out[:half]
+                far_ref[...] = out[half:half + cap]
+                last_ref[...] = out[half + cap:]
+
+            ins = [
+                (blocks_in, (1, cap, ff), lambda j, s, i=i: (s[q * nz + i], 0, 0)) for i in range(nz)
+            ]
+            ins.append((down_weight, (1, ff, broad), lambda j, s: (0, 0, j)))
+            return chain(
+                made, (features // broad,), ins, [broadly(half), broadly(cap), broadly(cap)],
+                [pltpu.VMEM((nz * cap, ff), BF16)],
+            )
+
+        there_near, there_far, there_last = product(1)
+        rs_last = over_expert(there_last, swap_x)
+        rs_far = over_expert(there_far, swap_x)
+        rs_near = over_expert(there_near, swap_x)
+
+        here_near, here_far, here_last = product(0)
+
+        def onehot(pos_ref, row):
+            slot = lax.broadcasted_iota(jnp.int32, (cap, tok), 0)
+            return slot == pos_ref[row:row + 1, :]
+
+        def pack_rows(pos_ref, gate_ref, first, held, send_ref, keep_ref):
+            for i, block in enumerate(held):
+                for q, ref in enumerate((keep_ref, send_ref)):
+                    row = (first + i) * nx + q
+                    hot = onehot(pos_ref, row)
+                    scale = jnp.sum(
+                        jnp.where(hot, gate_ref[row:row + 1, :], 0.0), axis=1, keepdims=True
+                    )
+                    rows = dot(hot.astype(BF16), block)
+                    ref[i * cap:(i + 1) * cap] = (rows * scale).astype(BF16)
+
+        def spread_rows(pos_ref, gate_ref, row, here, there):
+            total = None
+            for q, rows in enumerate((here, there)):
+                at = row * nx + q
+                weighted = jnp.where(onehot(pos_ref, at), gate_ref[at:at + 1, :], 0.0).astype(BF16)
+                term = lax.dot_general(
+                    weighted, rows, (((0,), (0,)), ((), ())), preferred_element_type=F32
+                )
+                total = term if total is None else total + term
+            return total
+
+        def entire(rows, dtype=BF16, cols=None):
+            shape = (rows, features if cols is None else cols)
+            return (shape, dtype, shape, lambda *_: (0, 0))
+
+        def packed_near(s, pos_ref, gate_ref, own, other, send_ref, keep_ref):
+            pack_rows(pos_ref, gate_ref, 0, (own[...], other[...]), send_ref, keep_ref)
+
+        def packed_far(s, pos_ref, gate_ref, m0, o0, m1, o1, first_ref, second_ref, keep_ref):
+            middle_here = s[at_middle] == 1
+            for k in range(tiles):
+                at = slice(k * tile, (k + 1) * tile)
+                held = [
+                    jnp.where(middle_here, a[:, at], b[:, at]) for a, b in ((m0, o0), (m1, o1))
+                ]
+                send, moved = (first_ref, 0) if k < first else (second_ref, first)
+                send = send.at[:, (k - moved) * tile:(k - moved + 1) * tile]
+                pack_rows(pos_ref, gate_ref, 2, held, send, keep_ref.at[:, at])
+
+        def shared_far(s, pos_ref, gate_ref, here2, there2, here3, there3, far_ref, last_ref):
+            for row, here, there, ref in ((2, here2, there2, far_ref), (3, here3, there3, last_ref)):
+                total = spread_rows(pos_ref, gate_ref, row, here[...], there[...])
+                ref[...] = total.astype(BF16)
+
+        def shared_near(s, pos_ref, gate_ref, here, there, sum_ref, keep_ref, send_ref):
+            for i, ref in enumerate((keep_ref, send_ref)):
+                lines = slice(i * cap, (i + 1) * cap)
+                total = spread_rows(pos_ref, gate_ref, i, here[lines], there[lines])
+                if i == 1:
+                    total = total + sum_ref[...].astype(F32)
+                ref[...] = total.astype(ref.dtype)
+
+        def plus(a, b):
+            def add(s, a_ref, b_ref, out_ref):
+                out_ref[...] = a_ref[...] + b_ref[...]
+
+            return chain(add, (1,), [whole(a), whole(b)], [entire(tok)])[0]
+
+        def turned(s, *refs):
+            *given, out_ref, rows = refs
+
+            @pl.when(pl.program_id(0) == 0)
+            def _():
+                for i, ref in enumerate(given):
+                    rows[i * cap:(i + 1) * cap] = ref[0]
+
+            first = pl.multiple_of(s[at_parts + pl.program_id(0)] * part, part)
+            out_ref[...] = rows[:, pl.ds(first, part)].T
+
+        slots = n_expert * cap
+        (hidden_t,) = chain(
+            turned, (n_dp,),
+            [(blocks_in, (1, cap, ff), lambda j, s, i=i: (s[i], 0, 0)) for i in range(n_expert)],
+            [((ff, slots), BF16, (part, slots), lambda j, *_: (j, 0))],
+            [pltpu.VMEM((slots, ff), BF16)],
+        )
+
+        def positions(s, near_ref, far_ref, pos_ref, gate_ref):
+            middle_here = s[at_middle] == 1
+            rows = 2 * top
+            held = [
+                near_ref[:rows],
+                near_ref[rows:],
+                jnp.where(middle_here, far_ref[rows:], far_ref[:rows]),
+                jnp.where(middle_here, far_ref[:rows], far_ref[rows:]),
+            ]
+            match, gates = [], []
+            for t in held:
+                for q in range(nx):
+                    named = t[:top] == s[at_here + q].astype(F32)
+                    match.append(jnp.sum(named.astype(F32), axis=0, keepdims=True))
+                    gates.append(jnp.sum(jnp.where(named, t[top:], 0.0), axis=0, keepdims=True))
+            match = jnp.concatenate(match, axis=0)
+            earlier = lax.broadcasted_iota(jnp.int32, (tok, tok), 0) < lax.broadcasted_iota(
+                jnp.int32, (tok, tok), 1
+            )
+            before = dot(match.astype(BF16), earlier.astype(BF16))
+            pos_ref[...] = jnp.where(match > 0, before, -1.0).astype(jnp.int32)
+            gate_ref[...] = jnp.concatenate(gates, axis=0)
+
+        small = (nz * nx, tok)
+        pos, gate = chain(
+            positions, (1,), [whole(pair), whole(far_pair)],
+            [(small, jnp.int32, small, lambda *_: (0, 0)), (small, F32, small, lambda *_: (0, 0))],
+        )
+        def pieces(c):
+            whole_width = [columns(a, begin[c]) for a in (own_near, own_far, ag_near)]
+            return whole_width + [columns(ag_far[c])]
+
+        share_rows = ny * part
+
+        def stack_pieces(given, rows):
+            for i, ref in enumerate(given):
+                rows[i * half:(i + 1) * half] = ref[...]
+
+        def weight_give(c):
+            def gave(s, *refs):
+                *given, turned_ref, out_ref, rows_ref = refs
+                stack_pieces(given, rows_ref)
+                out_ref[...] = dot(turned_ref[...], rows_ref[...]).astype(BF16)
+
+            return chain(
+                gave, (count[c],),
+                pieces(c) + [(hidden_t, (share_rows, slots), lambda *_: (0, 0))],
+                [wide(share_rows, c), wide(slots, c)],
+            )
+
+        def weight_keep(rows, c, got):
+            def kept(s, rows_ref, turned_ref, got_ref, send_ref, keep_ref):
+                out = dot(turned_ref[...], rows_ref[...]).astype(BF16).astype(F32)
+                out = out + got_ref[...].astype(F32)
+                send_ref[...] = out[:part].astype(BF16)
+                keep_ref[...] = out[part:]
+
+            return chain(
+                kept, (count[c],),
+                [columns(rows), (hidden_t, (share_rows, slots), lambda *_: (1, 0)), columns(got)],
+                [wide(part, c), wide(part, c, F32)],
+            )
+
+        def hidden_all(rows_a, rows_b, deps):
+            strip = 256
+
+            def hidden(s, a_ref, b_ref, w, h, out_ref, scalar_ref):
+                j = pl.program_id(0)
+                total = None
+                for ref, (first, end) in zip((a_ref, b_ref), spans):
+                    term = lax.dot_general(
+                        ref[...], w[0, :, first:end], (((1,), (1,)), ((), ())),
+                        preferred_element_type=F32,
+                    )
+                    total = term if total is None else total + term
+                for i in range(n_expert):
+                    mine = total[i * cap:(i + 1) * cap]
+                    out_ref[s[i]] = mine.astype(BF16)
+                    term = jnp.sum(mine * h[s[i]].astype(F32), axis=1, keepdims=True)
+                    term = jnp.broadcast_to(term, (cap, 128))
+
+                    @pl.when(j == 0)
+                    def _():
+                        scalar_ref[i] = term
+
+                    @pl.when(j > 0)
+                    def _():
+                        scalar_ref[i] += term
+
+            strips = (n_expert, cap, strip)
+            return chain(
+                hidden, (ff // strip,),
+                [
+                    whole(rows_a), whole(rows_b),
+                    (down_weight, (1, strip, features), lambda j, s: (0, j, 0)),
+                    (blocks_in, strips, lambda j, s: (0, 0, j)),
+                ],
+                [
+                    (blocks_in.shape, BF16, strips, lambda j, s: (0, 0, j)),
+                    ((n_expert, cap, 128), F32, (n_expert, cap, 128), lambda *_: (0, 0, 0)),
+                ],
+                (), deps,
+            )
+
+        mids = hold(mids, buddies)
+        mid_last = over_expert(buddies, middle)
+        out_far = over_expert(mids, outward)
+        send, own_near = chain(
+            sliced(packed_near, 2), (1,),
+            [whole(a) for a in (pos, gate, cotangent, buddies)], [entire(half), entire(half)],
+        )
+        ag_near = over_expert(send, swap_x)
+        sum_far, sum_last = chain(
+            sliced(shared_far, 2), (1,),
+            [whole(a) for a in (pos, gate, here_far, rs_far, here_last, rs_last)],
+            [entire(tok), entire(tok)],
+        )
+        one = over_expert(sum_last, inward)
+        mid_last = hold(mid_last, out_far)
+        out_last = over_expert(mid_last, outward)
+        two = over_expert(plus(sum_last, one), middle)
+        sum_far = hold(sum_far, one)
+        one_far = over_expert(sum_far, inward)
+        send_a, send_b, own_far = chain(
+            packed_far, (1,),
+            [whole(a) for a in (pos, gate, mids, out_far, mid_last, out_last)],
+            [entire(half, BF16, widths[0]), entire(half, BF16, widths[1]), entire(half)],
+        )
+        ag_far = [over_expert(send_a, swap_x), over_expert(send_b, swap_x)]
+        two_far = over_expert(plus(sum_far, one_far), middle)
+        give, rows_a = weight_give(0)
+        got = over_dp(give, swap_core)
+        keep, give = chain(
+            sliced(shared_near, 2), (1,),
+            [whole(a) for a in (pos, gate, here_near, rs_near, two)],
+            [entire(tok, F32), entire(tok)],
+        )
+        three = over_expert(give, buddy)
+        send_a, keep_a = weight_keep(rows_a, 0, got)
+        got_a = over_dp(send_a, swap_y)
+        give, rows_b = weight_give(1)
+        got = over_dp(give, swap_core)
+        hidden_grad, scalar_rows = hidden_all(rows_a, rows_b, ())
+        two_far = hold(two_far)
+        send_b, keep_b = weight_keep(rows_b, 1, got)
+        got_b = over_dp(send_b, swap_y)
+        scalar_rows = hold(scalar_rows)
+        three = hold(three)
+        got_a = hold(got_a)
+
+        def add_three(s, a, b, c, out_ref):
+            total = a[...] + b[...].astype(F32) + c[...].astype(F32)
+            out_ref[...] = total.astype(BF16)
+
+        (combined,) = chain(
+            add_three, (1,), [whole(a) for a in (keep, three, two_far)], [entire(tok)]
+        )
+
+        def add_chunks(s, *refs):
+            *given, out_ref = refs
+            for c in range(2):
+                total = given[2 * c][...] + given[2 * c + 1][...].astype(F32)
+                out_ref[0, :, spans[c][0]:spans[c][1]] = total.astype(BF16)
+
+        strip = part // 2
+        (weight_grad,) = chain(
+            add_chunks, (2,),
+            [(a, (strip, a.shape[1]), lambda j, *_: (j, 0)) for a in (keep_a, got_a, keep_b, got_b)],
+            [((1, part, features), BF16, (1, strip, features), lambda j, *_: (0, j, 0))],
+        )
+
+        back = scalar_rows[:, :, 0].reshape(nx, nz, cap)
+        back = jnp.stack([back[0], over_expert(back[1], swap_x)], axis=1)
+        home = jnp.stack(
+            [
+                back[0],
+                over_expert(back[1], buddy),
+                over_expert(jnp.where(is_middle, back[3], back[2]), skip),
+                over_expert(jnp.where(is_middle, back[2], back[3]), mirror),
+            ]
+        ).reshape(n_expert, cap)
+        from_z = jnp.stack([z, z ^ 1, z ^ 2, 3 - z])
+        ids = (from_z[:, None] * nx + order_x[None, :]).reshape(-1)
+        said = routes.T[None] == ids[:, None, None]
+        match = said.any(axis=1)
+        count = match.astype(jnp.int32)
+        before = jnp.cumsum(count, axis=1) - count
+        slot = jnp.arange(cap, dtype=jnp.int32)[:, None]
+        mine = match[:, None, :] & (before[:, None, :] == slot)
+        by_token = jnp.sum(jnp.where(mine, home[:, :, None], 0.0), axis=1)
+        gate_grad = jnp.sum(jnp.where(said, by_token[:, None], 0.0), axis=0).T / gate_prob
+        return (
+            combined,
+            gate_grad,
+            hidden_grad.reshape(hidden_in.shape),
+            weight_grad,
+        )
+
+    return local
+
+
+def build(n_dp, n_expert):
+    if split_expert(n_expert) == (4, 2) and n_dp == 4:
+        return build_tree(n_dp, n_expert)
+    return build_line(n_dp, n_expert)
+
+
 def solution(mesh):
     in_specs = (
         P("expert", "dp", None, None),

time: 239 us -> 193 us (0.81)
  Pallas kernels: 0 us -> 71.3 us
  starting transfers between devices: 77.8 us -> 39.6 us
  matrix products: 34.7 us -> 0 us
  waiting for transfers between devices: 78.7 us -> 57.5 us
  other arithmetic: 25.3 us -> 4.81 us
    pallas_call x0 -> x24, Pallas kernels: none -> 71.3 us  [the longest x17 71.3 us: call(): pl.pallas_call(body, out_shape=[jax.ShapeDtypeStruct(shape, dtype) for sh...]
    ppermute x35 -> x22, starting transfers between devices: 74.2 us -> 37.2 us  [over_expert(): return lax.ppermute(a, 'expert', pairs)]
    dot_general x12 -> x0, matrix products: 34.7 us -> none  [the longest x6 25.4 us: dot(): return jnp.dot(a, b, preferred_element_type=F32)]
    ppermute x4, waiting for transfers between devices: 33.9 us -> 12.6 us  [over_dp(): return lax.ppermute(a, 'dp', pairs)]
    unnamed x62 -> x86, local copies, waits for them, and re-layouts: 0.7 us -> 15.6 us
    gather x6 -> x0, local copies, waits for them, and re-layouts: 9 us -> none  [the longest x2 3.88 us: local(): out = out[(jnp.arange(nx) - x) % nx][:, (z - jnp.arange(nz)) % nz]]
    another operation x14 -> x4, other arithmetic: 8.62 us -> 0.96 us  [the longest x1 0.87 us: local(): before = jnp.cumsum(count, axis=1) - count]
    convert_element_type x10 -> x1, other arithmetic: 7.43 us -> 0.01 us  [local(): count = match.astype(jnp.int32)]
  transfers between devices with their start and end apart: 39 -> 26, of which waited for: 12 -> 10; matrix products, arithmetic and copies ran while one was open for 32% -> 4% of each run, Pallas kernels for 0% -> 36%
where the time goes in v2:
time: 193 us; the launch traced here: 192 us
  Pallas kernels  71.3 us (37%)
  waiting for transfers between devices  57.5 us (30%)
  starting transfers between devices  39.6 us (21%)
  local copies, waits for them, and re-layouts  17.8 us (9%)
  other arithmetic  4.81 us (2%)
    pallas_call x17, Pallas kernels, call(): pl.pallas_call(body, out_shape=[jax.ShapeDtypeStruct(shape, dtype) for sh...  71.3 us
    ppermute x22, waiting for transfers between devices, over_expert(): return lax.ppermute(a, 'expert', pairs)  44.9 us
    ppermute x22, starting transfers between devices, over_expert(): return lax.ppermute(a, 'expert', pairs)  37.2 us
    unnamed x86, local copies, waits for them, and re-layouts  15.6 us
    ppermute x4, waiting for transfers between devices, over_dp(): return lax.ppermute(a, 'dp', pairs)  12.6 us
  transfers between devices with their start and end apart: 26, of which 10 were waited for; matrix products, arithmetic and copies ran while one was open for 4% of the time, Pallas kernels for 36%

profile of v2, /device:TPU:0, one launch (start us, length us, event | category | flops | bytes accessed | tf_op | source)
XLA Modules:
  0.0 192.0 jit_solution(1162076278006609144)
XLA Ops:
  0.6 3.1 %collective-permute-start.5 = (bf16[128,3584]{1,0:T(8,128)(2,1)}, bf16[128,3584]{1,0:T(8,128)(2,1)}, u32[]{:S(2)}, u32[]{:S(2)}) collective-permute-start(bf16[128,3584]{1,0:T(8,128)(2,1)} %refs_3_.2), channel_id=1, source_target_pairs={{0,2},{1,3},{2,0},{3,1},{4,6},{5,7},{6,4},{7,5},{8,10},{9,11},{10,... | collective-permute-start | bytes 2752520 | tf_op jit(solution)/shard_map/ppermute | solution.py:263
  7.3 3.5 %collective-permute-start = (f32[8,128]{1,0:T(8,128)}, f32[8,128]{1,0:T(8,128)}, u32[]{:S(2)}, u32[]{:S(2)}) collective-permute-start(f32[8,128]{1,0:T(8,128)} %maximum_bitcast_fusion), channel_id=1, source_target_pairs={{0,2},{1,3},{2,0},{3,1},{4,6},{5,7},{6,4},{7,5},{8,10},{9,11},{10,... | collective-permute-start | bytes 12296 | tf_op jit(solution)/shard_map/ppermute | solution.py:263
  12.2 7.5 %made.2 = (bf16[160,3584]{1,0:T(8,128)(2,1)}, bf16[80,3584]{1,0:T(8,128)(2,1)}, bf16[80,3584]{1,0:T(8,128)(2,1)}) custom-call(s32[15]{0:T(128)} %concatenate.17.refs_0_, bf16[8,80,1024]{2,1,0:T(8,128)(2,1)} %bitcast.39, bf16[8,80,1024]{2,1,0:T(8,128)(2,1)} %bitcast.40, bf16[8,80,1024]{2,1,0:T(8,128)(2,1)} %bitcast.41, bf16[8,80,1024]{2,1,0:T(8,128)(2,1)} %bitcast.42, ...), custom_call_target="tpu_custom_call" | custom-call | flops 99999997952 | bytes 333333344 | tf_op jit(solution)/shard_map/made/pallas_call | solution.py:230
  21.7 8.1 %made.3 = (bf16[160,3584]{1,0:T(8,128)(2,1)}, bf16[80,3584]{1,0:T(8,128)(2,1)}, bf16[80,3584]{1,0:T(8,128)(2,1)}) custom-call(s32[15]{0:T(128)} %concatenate.17.refs_0_, bf16[8,80,1024]{2,1,0:T(8,128)(2,1)} %bitcast.43, bf16[8,80,1024]{2,1,0:T(8,128)(2,1)} %bitcast.44, bf16[8,80,1024]{2,1,0:T(8,128)(2,1)} %bitcast.45, bf16[8,80,1024]{2,1,0:T(8,128)(2,1)} %bitcast.46, ...), custom_call_target="tpu_custom_call" | custom-call | flops 99999997952 | bytes 333333344 | tf_op jit(solution)/shard_map/made/pallas_call | solution.py:230
  39.5 3.5 %packed_near.1 = (bf16[160,3584]{1,0:T(8,128)(2,1)}, bf16[160,3584]{1,0:T(8,128)(2,1)S(1)}) custom-call(s32[15]{0:T(128)S(1)} %copy-done.12, s32[8,128]{1,0:T(8,128)S(1)} %copy-done.11, f32[8,128]{1,0:T(8,128)S(1)} %get-tuple-element.34.refs_2_, bf16[128,3584]{1,0:T(8,128)(2,1)S(1)} %copy-done.17, bf16[128,3584]{1,0:T(8,128)(2,1)} %collective-permute-done.5.refs_2_.refs_4_, ...), custom_call_target="tpu_custom_call" | custom-call | flops 99999997952 | bytes 333333344 | tf_op jit(solution)/shard_map/packed_near/pallas_call | solution.py:230
  44.1 2.1 %collective-permute-done.4.refs_6_ = bf16[80,3584]{1,0:T(8,128)(2,1)} collective-permute-done((bf16[80,3584]{1,0:T(8,128)(2,1)}, bf16[80,3584]{1,0:T(8,128)(2,1)}, u32[]{:S(2)}, u32[]{:S(2)}) %collective-permute-start.4) | collective-permute-done | bytes 573472 | tf_op jit(solution)/shard_map/ppermute | solution.py:263
  46.2 2.9 %shared_far.1 = (bf16[128,3584]{1,0:T(8,128)(2,1)S(1)}, bf16[128,3584]{1,0:T(8,128)(2,1)S(1)}) custom-call(s32[15]{0:T(128)S(1)} %copy-done.12, s32[8,128]{1,0:T(8,128)S(1)} %copy-done.11, f32[8,128]{1,0:T(8,128)S(1)} %get-tuple-element.34.refs_2_, bf16[80,3584]{1,0:T(8,128)(2,1)S(1)} %copy-done.29, bf16[80,3584]{1,0:T(8,128)(2,1)} %collective-permute-done.3.refs_4_, ...), custom_call_target="tpu_custom_call" | custom-call | flops 99999997952 | bytes 333333344 | tf_op jit(solution)/shard_map/shared_far/pallas_call | solution.py:230
  50.1 3.7 %collective-permute-start.7 = (bf16[128,3584]{1,0:T(8,128)(2,1)S(1)}, bf16[128,3584]{1,0:T(8,128)(2,1)S(1)}, u32[]{:S(2)}, u32[]{:S(2)}) collective-permute-start(bf16[128,3584]{1,0:T(8,128)(2,1)S(1)} %get-tuple-element.40.refs_1_), channel_id=1, source_target_pairs={{0,2},{1,3},{6,4},{7,5},{8,10},{9,11},{14,12},{15,13},{16,18},{17,... | collective-permute-start | bytes 2752520 | tf_op jit(solution)/shard_map/ppermute | solution.py:263
  59.6 11.5 %collective-permute-done.7.refs_2_ = bf16[128,3584]{1,0:T(8,128)(2,1)S(1)} collective-permute-done((bf16[128,3584]{1,0:T(8,128)(2,1)S(1)}, bf16[128,3584]{1,0:T(8,128)(2,1)S(1)}, u32[]{:S(2)}, u32[]{:S(2)}) %collective-permute-start.7) | collective-permute-done | bytes 917536 | tf_op jit(solution)/shard_map/ppermute | solution.py:263
  74.3 5.8 %collective-permute-start.14 = (bf16[128,3584]{1,0:T(8,128)(2,1)}, bf16[128,3584]{1,0:T(8,128)(2,1)S(1)}, u32[]{:S(2)}, u32[]{:S(2)}) collective-permute-start(bf16[128,3584]{1,0:T(8,128)(2,1)} %after.9.refs_7_.refs_1_), channel_id=1, source_target_pairs={{0,2},{1,3},{6,4},{7,5},{8,10},{9,11},{14,12},{15,13},{16,18},{17,... | collective-permute-start | bytes 2752520 | tf_op jit(solution)/shard_map/ppermute | solution.py:263
  82.1 3.9 %packed_far.1 = (bf16[160,1536]{1,0:T(8,128)(2,1)S(1)}, bf16[160,2048]{1,0:T(8,128)(2,1)}, bf16[160,3584]{1,0:T(8,128)(2,1)S(1)}) custom-call(s32[15]{0:T(128)S(1)} %copy-done.12, s32[8,128]{1,0:T(8,128)S(1)} %copy-done.11, f32[8,128]{1,0:T(8,128)S(1)} %get-tuple-element.34.refs_2_, bf16[128,3584]{1,0:T(8,128)(2,1)} %after.7.refs_5_.refs_3_, ...), custom_call_target="tpu_custom_call" | custom-call | flops 99999997952 | bytes 333333344 | tf_op jit(solution)/shard_map/packed_far/pallas_call | solution.py:230
  87.1 8.8 %collective-permute-done.14.refs_2_ = bf16[128,3584]{1,0:T(8,128)(2,1)S(1)} collective-permute-done((bf16[128,3584]{1,0:T(8,128)(2,1)}, bf16[128,3584]{1,0:T(8,128)(2,1)S(1)}, u32[]{:S(2)}, u32[]{:S(2)}) %collective-permute-start.14) | collective-permute-done | bytes 917536 | tf_op jit(solution)/shard_map/ppermute | solution.py:263
  98.7 8.3 %collective-permute-done.12.refs_3_ = bf16[160,3584]{1,0:T(8,128)(2,1)} collective-permute-done((bf16[160,3584]{1,0:T(8,128)(2,1)}, bf16[160,3584]{1,0:T(8,128)(2,1)}, u32[]{:S(2)}, u32[]{:S(2)}) %collective-permute-start.12) | collective-permute-done | bytes 1146912 | tf_op jit(solution)/shard_map/ppermute | solution.py:263
  108.6 8.8 %collective-permute-done.13.refs_4_ = bf16[160,1536]{1,0:T(8,128)(2,1)S(1)} collective-permute-done((bf16[160,1536]{1,0:T(8,128)(2,1)S(1)}, bf16[160,1536]{1,0:T(8,128)(2,1)S(1)}, u32[]{:S(2)}, u32[]{:S(2)}) %collective-permute-start.13) | collective-permute-done | bytes 491552 | tf_op jit(solution)/shard_map/ppermute | solution.py:263
  117.4 3.7 %gave.2 = (bf16[512,1536]{1,0:T(8,128)(2,1)S(1)}, bf16[640,1536]{1,0:T(8,128)(2,1)S(1)}) custom-call(s32[15]{0:T(128)S(1)} %copy-done.12, bf16[160,3584]{1,0:T(8,128)(2,1)S(1)} %copy-done.27, bf16[160,3584]{1,0:T(8,128)(2,1)S(1)} %get-tuple-element.43.refs_2_, bf16[160,3584]{1,0:T(8,128)(2,1)} %collective-permute-done.12.refs_3_, ...), custom_call_target="tpu_custom_call" | custom-call | flops 99999997952 | bytes 333333344 | tf_op jit(solution)/shard_map/gave/pallas_call | solution.py:230
  121.3 4.2 %shared_near.1 = (f32[128,3584]{1,0:T(8,128)S(1)}, bf16[128,3584]{1,0:T(8,128)(2,1)}) custom-call(s32[15]{0:T(128)S(1)} %copy-done.12, s32[8,128]{1,0:T(8,128)S(1)} %copy-done.11, f32[8,128]{1,0:T(8,128)S(1)} %copy-done.32, bf16[160,3584]{1,0:T(8,128)(2,1)S(1)} %copy-done.25, bf16[160,3584]{1,0:T(8,128)(2,1)} %collective-permute-done.2.refs_4_, ...), custom_call_target="tpu_custom_call" | custom-call | flops 99999997952 | bytes 333333344 | tf_op jit(solution)/shard_map/shared_near/pallas_call | solution.py:230
  125.5 3.3 %kept.2 = (bf16[256,1536]{1,0:T(8,128)(2,1)}, f32[256,1536]{1,0:T(8,128)S(1)}) custom-call(s32[15]{0:T(128)S(1)} %copy-done.12, bf16[640,1536]{1,0:T(8,128)(2,1)S(1)} %get-tuple-element.48.refs_1_, bf16[1024,640]{1,0:T(8,128)(2,1)S(1)} %copy-done.5, bf16[512,1536]{1,0:T(8,128)(2,1)S(1)} %collective-permute-done.17.refs_3_, ...), custom_call_target="tpu_custom_call" | custom-call | flops 99999997952 | bytes 333333344 | tf_op jit(solution)/shard_map/kept/pallas_call | solution.py:230
  130.3 5.5 %gave.3 = (bf16[512,2048]{1,0:T(8,128)(2,1)}, bf16[640,2048]{1,0:T(8,128)(2,1)S(1)}) custom-call(s32[15]{0:T(128)S(1)} %copy-done.12, bf16[160,3584]{1,0:T(8,128)(2,1)S(1)} %copy-done.28, bf16[160,3584]{1,0:T(8,128)(2,1)S(1)} %get-tuple-element.43.refs_2_, bf16[160,3584]{1,0:T(8,128)(2,1)} %collective-permute-done.12.refs_3_, ...), custom_call_target="tpu_custom_call" | custom-call | flops 99999997952 | bytes 333333344 | tf_op jit(solution)/shard_map/gave/pallas_call | solution.py:230
  137.5 12.7 %hidden.1 = (bf16[8,80,1024]{2,1,0:T(8,128)(2,1)}, f32[8,80,128]{2,1,0:T(8,128)}) custom-call(s32[15]{0:T(128)} %concatenate.17.refs_0_, bf16[640,1536]{1,0:T(8,128)(2,1)} %copy-done.19, bf16[640,2048]{1,0:T(8,128)(2,1)} %copy-done.2, bf16[1,1024,3584]{2,1,0:T(8,128)(2,1)} %refs_3_.3, bf16[8,80,1024]{2,1,0:T(8,128)(2,1)} %bitcast.47, ...), custom_call_target="tpu_custom_call" | custom-call | flops 99999997952 | bytes 333333344 | tf_op jit(solution)/shard_map/hidden/pallas_call | solution.py:230
  153.2 4.7 %kept.3 = (bf16[256,2048]{1,0:T(8,128)(2,1)S(1)}, f32[256,2048]{1,0:T(8,128)S(1)}) custom-call(s32[15]{0:T(128)S(1)} %copy-done.13, bf16[640,2048]{1,0:T(8,128)(2,1)S(1)} %copy-done.3, bf16[1024,640]{1,0:T(8,128)(2,1)S(1)} %copy-done.6, bf16[512,2048]{1,0:T(8,128)(2,1)} %collective-permute-done.18.refs_3_, bf16[128,3584]{1,0:T(8,128)(2,1)} %after.10.refs_4_.refs_3_), custom_call_target="tpu_custom_call" | custom-call | flops 1 | tf_op jit(solution)/shard_map/kept/pallas_call | solution.py:230
  165.3 2.9 %collective-permute-start.24 = (f32[2,80]{1,0:T(2,128)S(1)}, f32[2,80]{1,0:T(2,128)S(1)}, u32[]{:S(2)}, u32[]{:S(2)}) collective-permute-start(f32[2,80]{1,0:T(2,128)S(1)} %bitcast.66), channel_id=1, source_target_pairs={{0,6},{1,7},{6,0},{7,1},{2,4},{3,5},{4,2},{5,3},{8,14},{9,15},{14,... | collective-permute-start | bytes 1928 | tf_op jit(solution)/shard_map/ppermute | solution.py:263
  171.2 3.2 %add_three.1.refs_5_ = bf16[128,3584]{1,0:T(8,128)(2,1)} custom-call(s32[15]{0:T(128)S(1)} %copy-done.13, f32[128,3584]{1,0:T(8,128)S(1)} %copy-done.21, bf16[128,3584]{1,0:T(8,128)(2,1)} %after.12.refs_1_.refs_2_, bf16[128,3584]{1,0:T(8,128)(2,1)} %after.10.refs_4_.refs_3_, bf16[256,1536]{1,0:T(8,128)(2,1)} %after.13.refs_4_.refs_2_), custom_call_target="tpu_custom_call" | custom-call | flops 99999997952 | bytes 333333344 | tf_op jit(solution)/shard_map/add_three/pallas_call | solution.py:230
  175.3 12.6 %collective-permute-done.25.refs_4_ = bf16[256,2048]{1,0:T(8,128)(2,1)S(1)} collective-permute-done((bf16[256,2048]{1,0:T(8,128)(2,1)S(1)}, bf16[256,2048]{1,0:T(8,128)(2,1)S(1)}, u32[]{:S(2)}, u32[]{:S(2)}) %collective-permute-start.25) | collective-permute-done | bytes 1048608 | tf_op jit(solution)/shard_map/ppermute | solution.py:266
  189.1 2.9 %add_chunks.1 = bf16[1,256,3584]{2,1,0:T(8,128)(2,1)} custom-call(s32[15]{0:T(128)S(1)} %copy-done.13, f32[256,1536]{1,0:T(8,128)S(1)} %copy-done.23, bf16[256,1536]{1,0:T(8,128)(2,1)} %after.13.refs_4_.refs_2_, f32[256,2048]{1,0:T(8,128)S(1)} %copy-done.15, bf16[256,2048]{1,0:T(8,128)(2,1)S(1)} %collective-permute-done.25.refs_4_, ...), custom_call_target="tpu_custom_call" | custom-call | flops 99999997952 | bytes 333333344 | tf_op jit(solution)/shard_map/add_chunks/pallas_call | solution.py:230
  (160 shorter events, 53.6 us)
Async XLA Ops:
  0.6 35.7 %collective-permute-start.5 = (bf16[128,3584]{1,0:T(8,128)(2,1)}, bf16[128,3584]{1,0:T(8,128)(2,1)}, u32[]{:S(2)}, u32[]{:S(2)}) collective-permute-start(bf16[128,3584]{1,0:T(8,128)(2,1)} %refs_3_.2), channel_id=1, source_target_pairs={{0,2},{1,3},{2,0},{3,1},{4,6},{5,7},{6,4},{7,5},{8,10},{9,11},{10,... | collective-permute-start | bytes 2752520 | tf_op jit(solution)/shard_map/ppermute | solution.py:263
  3.7 32.6 %collective-permute-start.6 = (bf16[128,3584]{1,0:T(8,128)(2,1)}, bf16[128,3584]{1,0:T(8,128)(2,1)}, u32[]{:S(2)}, u32[]{:S(2)}) collective-permute-start(bf16[128,3584]{1,0:T(8,128)(2,1)} %refs_3_.2), channel_id=1, source_target_pairs={{2,4},{3,5},{4,2},{5,3},{10,12},{11,13},{12,10},{13,11},{18,20},{1... | collective-permute-start | bytes 2752520 | tf_op jit(solution)/shard_map/ppermute | solution.py:263
  7.3 22.6 %collective-permute-start = (f32[8,128]{1,0:T(8,128)}, f32[8,128]{1,0:T(8,128)}, u32[]{:S(2)}, u32[]{:S(2)}) collective-permute-start(f32[8,128]{1,0:T(8,128)} %maximum_bitcast_fusion), channel_id=1, source_target_pairs={{0,2},{1,3},{2,0},{3,1},{4,6},{5,7},{6,4},{7,5},{8,10},{9,11},{10,... | collective-permute-start | bytes 12296 | tf_op jit(solution)/shard_map/ppermute | solution.py:263
  19.7 24.3 %collective-permute-start.3 = (bf16[80,3584]{1,0:T(8,128)(2,1)}, bf16[80,3584]{1,0:T(8,128)(2,1)}, u32[]{:S(2)}, u32[]{:S(2)}) collective-permute-start(bf16[80,3584]{1,0:T(8,128)(2,1)} %get-tuple-element.36), channel_id=1, source_target_pairs={{0,1},{1,0},{2,3},{3,2},{4,5},{5,4},{6,7},{7,6},{8,9},{9,8},{10,11... | collective-permute-start | bytes 1720328 | tf_op jit(solution)/shard_map/ppermute | solution.py:263
  21.2 25.0 %collective-permute-start.4 = (bf16[80,3584]{1,0:T(8,128)(2,1)}, bf16[80,3584]{1,0:T(8,128)(2,1)}, u32[]{:S(2)}, u32[]{:S(2)}) collective-permute-start(bf16[80,3584]{1,0:T(8,128)(2,1)} %get-tuple-element.38), channel_id=1, source_target_pairs={{0,1},{1,0},{2,3},{3,2},{4,5},{5,4},{6,7},{7,6},{8,9},{9,8},{10,11... | collective-permute-start | bytes 1720328 | tf_op jit(solution)/shard_map/ppermute | solution.py:263
  30.5 4.5 %collective-permute-start.1 = (f32[16,128]{1,0:T(8,128)S(1)}, f32[16,128]{1,0:T(8,128)S(1)}, u32[]{:S(2)}, u32[]{:S(2)}) collective-permute-start(f32[16,128]{1,0:T(8,128)S(1)} %pad_maximum_fusion.refs_1_), channel_id=1, source_target_pairs={{0,4},{1,5},{4,0},{5,1},{2,6},{3,7},{6,2},{7,3},{8,12},{9,13},{12,... | collective-permute-start | bytes 24584 | tf_op jit(solution)/shard_map/ppermute | solution.py:263
  36.4 21.9 %collective-permute-start.9 = (bf16[128,3584]{1,0:T(8,128)(2,1)}, bf16[128,3584]{1,0:T(8,128)(2,1)}, u32[]{:S(2)}, u32[]{:S(2)}) collective-permute-start(bf16[128,3584]{1,0:T(8,128)(2,1)} %after.7.refs_5_.refs_3_), channel_id=1, source_target_pairs={{2,0},{3,1},{4,6},{5,7},{10,8},{11,9},{12,14},{13,15},{18,16},{19,... | collective-permute-start | bytes 2752520 | tf_op jit(solution)/shard_map/ppermute | solution.py:263
  37.8 19.9 %collective-permute-start.8 = (bf16[128,3584]{1,0:T(8,128)(2,1)}, bf16[128,3584]{1,0:T(8,128)(2,1)}, u32[]{:S(2)}, u32[]{:S(2)}) collective-permute-start(bf16[128,3584]{1,0:T(8,128)(2,1)} %collective-permute-done.5.refs_2_.refs_4_), channel_id=1, source_target_pairs={{2,4},{3,5},{4,2},{5,3},{10,12},{11,13},{12,10},{13,11},{18,20},{1... | collective-permute-start | bytes 2752520 | tf_op jit(solution)/shard_map/ppermute | solution.py:263
  50.1 21.0 %collective-permute-start.7 = (bf16[128,3584]{1,0:T(8,128)(2,1)S(1)}, bf16[128,3584]{1,0:T(8,128)(2,1)S(1)}, u32[]{:S(2)}, u32[]{:S(2)}) collective-permute-start(bf16[128,3584]{1,0:T(8,128)(2,1)S(1)} %get-tuple-element.40.refs_1_), channel_id=1, source_target_pairs={{0,2},{1,3},{6,4},{7,5},{8,10},{9,11},{14,12},{15,13},{16,18},{17,... | collective-permute-start | bytes 2752520 | tf_op jit(solution)/shard_map/ppermute | solution.py:263
  53.8 67.4 %collective-permute-start.2 = (bf16[160,3584]{1,0:T(8,128)(2,1)}, bf16[160,3584]{1,0:T(8,128)(2,1)}, u32[]{:S(2)}, u32[]{:S(2)}) collective-permute-start(bf16[160,3584]{1,0:T(8,128)(2,1)} %get-tuple-element.31.refs_6_), channel_id=1, source_target_pairs={{0,1},{1,0},{2,3},{3,2},{4,5},{5,4},{6,7},{7,6},{8,9},{9,8},{10,11... | collective-permute-start | bytes 3440648 | tf_op jit(solution)/shard_map/ppermute | solution.py:263
  56.7 50.3 %collective-permute-start.12 = (bf16[160,3584]{1,0:T(8,128)(2,1)}, bf16[160,3584]{1,0:T(8,128)(2,1)}, u32[]{:S(2)}, u32[]{:S(2)}) collective-permute-start(bf16[160,3584]{1,0:T(8,128)(2,1)} %get-tuple-element.39.refs_7_), channel_id=1, source_target_pairs={{0,1},{1,0},{2,3},{3,2},{4,5},{5,4},{6,7},{7,6},{8,9},{9,8},{10,11... | collective-permute-start | bytes 3440648 | tf_op jit(solution)/shard_map/ppermute | solution.py:263
  58.3 22.6 %collective-permute-start.11 = (bf16[128,3584]{1,0:T(8,128)(2,1)}, bf16[128,3584]{1,0:T(8,128)(2,1)S(1)}, u32[]{:S(2)}, u32[]{:S(2)}) collective-permute-start(bf16[128,3584]{1,0:T(8,128)(2,1)} %after.8.refs_3_.refs_5_), channel_id=1, source_target_pairs={{2,0},{3,1},{4,6},{5,7},{10,8},{11,9},{12,14},{13,15},{18,16},{19,... | collective-permute-start | bytes 2752520 | tf_op jit(solution)/shard_map/ppermute | solution.py:263
  72.7 48.5 %collective-permute-start.10 = (bf16[128,3584]{1,0:T(8,128)(2,1)}, bf16[128,3584]{1,0:T(8,128)(2,1)}, u32[]{:S(2)}, u32[]{:S(2)}) collective-permute-start(bf16[128,3584]{1,0:T(8,128)(2,1)} %add.86.refs_1_), channel_id=1, source_target_pairs={{2,4},{3,5},{4,2},{5,3},{10,12},{11,13},{12,10},{13,11},{18,20},{1... | collective-permute-start | bytes 2752520 | tf_op jit(solution)/shard_map/ppermute | solution.py:263
  74.3 21.6 %collective-permute-start.14 = (bf16[128,3584]{1,0:T(8,128)(2,1)}, bf16[128,3584]{1,0:T(8,128)(2,1)S(1)}, u32[]{:S(2)}, u32[]{:S(2)}) collective-permute-start(bf16[128,3584]{1,0:T(8,128)(2,1)} %after.9.refs_7_.refs_1_), channel_id=1, source_target_pairs={{0,2},{1,3},{6,4},{7,5},{8,10},{9,11},{14,12},{15,13},{16,18},{17,... | collective-permute-start | bytes 2752520 | tf_op jit(solution)/shard_map/ppermute | solution.py:263
  86.0 31.4 %collective-permute-start.13 = (bf16[160,1536]{1,0:T(8,128)(2,1)S(1)}, bf16[160,1536]{1,0:T(8,128)(2,1)S(1)}, u32[]{:S(2)}, u32[]{:S(2)}) collective-permute-start(bf16[160,1536]{1,0:T(8,128)(2,1)S(1)} %get-tuple-element.44.refs_3_), channel_id=1, source_target_pairs={{0,1},{1,0},{2,3},{3,2},{4,5},{5,4},{6,7},{7,6},{8,9},{9,8},{10,11... | collective-permute-start | bytes 1474568 | tf_op jit(solution)/shard_map/ppermute | solution.py:263
  95.9 34.4 %collective-permute-start.16 = (bf16[160,2048]{1,0:T(8,128)(2,1)}, bf16[160,2048]{1,0:T(8,128)(2,1)}, u32[]{:S(2)}, u32[]{:S(2)}) collective-permute-start(bf16[160,2048]{1,0:T(8,128)(2,1)} %get-tuple-element.49), channel_id=1, source_target_pairs={{0,1},{1,0},{2,3},{3,2},{4,5},{5,4},{6,7},{7,6},{8,9},{9,8},{10,11... | collective-permute-start | bytes 1966088 | tf_op jit(solution)/shard_map/ppermute | solution.py:263
  107.0 43.2 %collective-permute-start.19 = (bf16[128,3584]{1,0:T(8,128)(2,1)}, bf16[128,3584]{1,0:T(8,128)(2,1)}, u32[]{:S(2)}, u32[]{:S(2)}) collective-permute-start(bf16[128,3584]{1,0:T(8,128)(2,1)} %add.87.refs_6_), channel_id=1, source_target_pairs={{2,4},{3,5},{4,2},{5,3},{10,12},{11,13},{12,10},{13,11},{18,20},{1... | collective-permute-start | bytes 2752520 | tf_op jit(solution)/shard_map/ppermute | solution.py:263
  125.5 37.8 %collective-permute-start.15 = (bf16[128,3584]{1,0:T(8,128)(2,1)}, bf16[128,3584]{1,0:T(8,128)(2,1)}, u32[]{:S(2)}, u32[]{:S(2)}) collective-permute-start(bf16[128,3584]{1,0:T(8,128)(2,1)} %get-tuple-element.47), channel_id=1, source_target_pairs={{0,2},{1,3},{2,0},{3,1},{4,6},{5,7},{6,4},{7,5},{8,10},{9,11},{10,... | collective-permute-start | bytes 2752520 | tf_op jit(solution)/shard_map/ppermute | solution.py:263
  128.8 34.5 %collective-permute-start.20 = (bf16[256,1536]{1,0:T(8,128)(2,1)}, bf16[256,1536]{1,0:T(8,128)(2,1)}, u32[]{:S(2)}, u32[]{:S(2)}) collective-permute-start(bf16[256,1536]{1,0:T(8,128)(2,1)} %get-tuple-element.50.refs_6_), channel_id=1, source_target_pairs={{0,16},{8,24},{16,0},{24,8},{1,17},{9,25},{17,1},{25,9},{2,18},{10... | collective-permute-start | bytes 2359304 | tf_op jit(solution)/shard_map/ppermute | solution.py:266
  137.3 12.9 %collective-permute-start.18 = (bf16[512,2048]{1,0:T(8,128)(2,1)}, bf16[512,2048]{1,0:T(8,128)(2,1)}, u32[]{:S(2)}, u32[]{:S(2)}) collective-permute-start(bf16[512,2048]{1,0:T(8,128)(2,1)} %get-tuple-element.52.refs_5_), channel_id=1, source_target_pairs={{0,8},{8,0},{16,24},{24,16},{1,9},{9,1},{17,25},{25,17},{2,10},{10... | collective-permute-start | bytes 6291464 | tf_op jit(solution)/shard_map/ppermute | solution.py:266
  162.7 25.2 %collective-permute-start.25 = (bf16[256,2048]{1,0:T(8,128)(2,1)S(1)}, bf16[256,2048]{1,0:T(8,128)(2,1)S(1)}, u32[]{:S(2)}, u32[]{:S(2)}) collective-permute-start(bf16[256,2048]{1,0:T(8,128)(2,1)S(1)} %copy-done.8), channel_id=1, source_target_pairs={{0,16},{8,24},{16,0},{24,8},{1,17},{9,25},{17,1},{25,9},{2,18},{10... | collective-permute-start | bytes 3145736 | tf_op jit(solution)/shard_map/ppermute | solution.py:266
  165.3 9.2 %collective-permute-start.24 = (f32[2,80]{1,0:T(2,128)S(1)}, f32[2,80]{1,0:T(2,128)S(1)}, u32[]{:S(2)}, u32[]{:S(2)}) collective-permute-start(f32[2,80]{1,0:T(2,128)S(1)} %bitcast.66), channel_id=1, source_target_pairs={{0,6},{1,7},{6,0},{7,1},{2,4},{3,5},{4,2},{5,3},{8,14},{9,15},{14,... | collective-permute-start | bytes 1928 | tf_op jit(solution)/shard_map/ppermute | solution.py:263
  168.2 6.3 %collective-permute-start.23 = (f32[2,80]{1,0:T(2,128)S(1)}, f32[2,80]{1,0:T(2,128)S(1)}, u32[]{:S(2)}, u32[]{:S(2)}) collective-permute-start(f32[2,80]{1,0:T(2,128)S(1)} %select_bitcast_fusion), channel_id=1, source_target_pairs={{0,4},{1,5},{4,0},{5,1},{2,6},{3,7},{6,2},{7,3},{8,12},{9,13},{12,... | collective-permute-start | bytes 1928 | tf_op jit(solution)/shard_map/ppermute | solution.py:263
  168.6 5.8 %collective-permute-start.22 = (f32[2,80]{1,0:T(2,128)S(1)}, f32[2,80]{1,0:T(2,128)S(1)}, u32[]{:S(2)}, u32[]{:S(2)}) collective-permute-start(f32[2,80]{1,0:T(2,128)S(1)} %bitcast.65), channel_id=1, source_target_pairs={{0,2},{1,3},{2,0},{3,1},{4,6},{5,7},{6,4},{7,5},{8,10},{9,11},{10,... | collective-permute-start | bytes 1928 | tf_op jit(solution)/shard_map/ppermute | solution.py:263
  (45 other events, 256.0 us)

commit v3 on v2

--- a/solution.py
+++ b/solution.py
@@ -11,7 +11,7 @@
 F32 = jnp.float32
 CHUNKS = 2
 COST = 10**11
-COSTS = {'kept2': 1}
+COSTS = {'positions1': 1, 'packed_near1': 1, 'turned1': 1, 'kept2': 1}
 LIMIT = 24
 LIMITS = {'hidden': 60, 'made': 60}
 
@@ -222,8 +222,11 @@
     n_scalar = 0 if scalars is None else 1
 
     def body(*refs):
-        first = n_scalar + n_in
-        kernel(*refs[:first], *refs[first + n_dep:])
+        first, end = n_scalar + n_in, n_scalar + n_in + n_dep + len(outs) - 1
+        refs[end][...] = jnp.zeros((8, 128), F32)
+        kernel(*refs[:first], *refs[first + n_dep:end], *refs[end + 1:])
+
+    outs = list(outs) + [((8, 128), F32, (8, 128), lambda *_: (0, 0))]
 
     specs = [pl.BlockSpec(block, index) for _, block, index in ins]
     specs += [pl.BlockSpec(memory_space=pl.ANY)] * n_dep
@@ -275,7 +278,7 @@
         features = down_weight.shape[2]
         tile = 512
         tiles = features // tile
-        first = tiles // 2
+        first = (tiles + 1) // 2
         begin, count = (0, first), (first, tiles - first)
         widths = [n * tile for n in count]
         spans = [(b * tile, (b + n) * tile) for b, n in zip(begin, count)]
@@ -287,8 +290,8 @@
             named.append(kernel.__name__)
             cost = COSTS.get(f"{named[-1]}{named.count(named[-1])}", COST)
             got = call(kernel, grid, ins, outs, scratch, scalars, tuple(last) + tuple(deps), cost)
-            last[:] = [got[0]]
-            return got
+            last[:] = got[-1:]
+            return got[:-1]
 
         def hold(a, *deps):
             a = after(a, *last, *deps)
@@ -309,8 +312,6 @@
         buddies = over_expert(cotangent, buddy)
         mids = over_expert(cotangent, middle)
         table = jnp.concatenate([routes.astype(F32), gate_prob], axis=1).T
-        pair = jnp.concatenate([table, over_expert(table, buddy)])
-        far_pair = over_expert(pair, skip)
 
         def whole(a):
             return (a, a.shape, lambda *_: (0,) * a.ndim)
@@ -346,33 +347,35 @@
 
         def product(q):
             def made(s, *refs):
-                *given, w, near_ref, far_ref, last_ref, rows = refs
+                *given, w, w_low, near_ref, far_ref, rows = refs
 
                 @pl.when(pl.program_id(0) == 0)
                 def _():
                     for i, ref in enumerate(given):
                         rows[i * cap:(i + 1) * cap] = ref[0]
 
-                out = dot(rows[...], w[0]).astype(BF16)
-                near_ref[...] = out[:half]
-                far_ref[...] = out[half:half + cap]
-                last_ref[...] = out[half + cap:]
+                middle_row = ff // 2
+                out = dot(rows[:, :middle_row], w[0]) + dot(rows[:, middle_row:], w_low[0])
+                near_ref[...] = out[:half].astype(BF16)
+                far_ref[...] = out[half:].astype(BF16)
 
             ins = [
                 (blocks_in, (1, cap, ff), lambda j, s, i=i: (s[q * nz + i], 0, 0)) for i in range(nz)
             ]
-            ins.append((down_weight, (1, ff, broad), lambda j, s: (0, 0, j)))
+            for r in range(2):
+                ins.append((down_weight, (1, ff // 2, broad), lambda j, s, r=r: (0, r, j)))
             return chain(
-                made, (features // broad,), ins, [broadly(half), broadly(cap), broadly(cap)],
+                made, (features // broad,), ins, [broadly(half), broadly(half)],
                 [pltpu.VMEM((nz * cap, ff), BF16)],
             )
 
-        there_near, there_far, there_last = product(1)
-        rs_last = over_expert(there_last, swap_x)
+        there_near, there_far = product(1)
+        pair = jnp.concatenate([table, over_expert(table, buddy)])
         rs_far = over_expert(there_far, swap_x)
-        rs_near = over_expert(there_near, swap_x)
-
-        here_near, here_far, here_last = product(0)
+
+        here_near, here_far = product(0)
+        pair = hold(pair)
+        far_pair = over_expert(pair, skip)
 
         def onehot(pos_ref, row):
             slot = lax.broadcasted_iota(jnp.int32, (cap, tok), 0)
@@ -418,9 +421,10 @@
                 send = send.at[:, (k - moved) * tile:(k - moved + 1) * tile]
                 pack_rows(pos_ref, gate_ref, 2, held, send, keep_ref.at[:, at])
 
-        def shared_far(s, pos_ref, gate_ref, here2, there2, here3, there3, far_ref, last_ref):
-            for row, here, there, ref in ((2, here2, there2, far_ref), (3, here3, there3, last_ref)):
-                total = spread_rows(pos_ref, gate_ref, row, here[...], there[...])
+        def shared_far(s, pos_ref, gate_ref, here, there, far_ref, last_ref):
+            for i, ref in enumerate((far_ref, last_ref)):
+                lines = slice(i * cap, (i + 1) * cap)
+                total = spread_rows(pos_ref, gate_ref, 2 + i, here[lines], there[lines])
                 ref[...] = total.astype(BF16)
 
         def shared_near(s, pos_ref, gate_ref, here, there, sum_ref, keep_ref, send_ref):
@@ -449,12 +453,10 @@
             out_ref[...] = rows[:, pl.ds(first, part)].T
 
         slots = n_expert * cap
-        (hidden_t,) = chain(
-            turned, (n_dp,),
-            [(blocks_in, (1, cap, ff), lambda j, s, i=i: (s[i], 0, 0)) for i in range(n_expert)],
-            [((ff, slots), BF16, (part, slots), lambda j, *_: (j, 0))],
-            [pltpu.VMEM((slots, ff), BF16)],
-        )
+
+        mids = hold(mids, buddies)
+        mid_last = over_expert(buddies, middle)
+        out_far = over_expert(mids, outward)
 
         def positions(s, near_ref, far_ref, pos_ref, gate_ref):
             middle_here = s[at_middle] == 1
@@ -560,22 +562,28 @@
                 (), deps,
             )
 
-        mids = hold(mids, buddies)
-        mid_last = over_expert(buddies, middle)
-        out_far = over_expert(mids, outward)
+        there_near = hold(there_near)
         send, own_near = chain(
             sliced(packed_near, 2), (1,),
             [whole(a) for a in (pos, gate, cotangent, buddies)], [entire(half), entire(half)],
         )
         ag_near = over_expert(send, swap_x)
+        rs_near = over_expert(there_near, swap_x)
+        (hidden_t,) = chain(
+            turned, (n_dp,),
+            [(blocks_in, (1, cap, ff), lambda j, s, i=i: (s[i], 0, 0)) for i in range(n_expert)],
+            [((ff, slots), BF16, (part, slots), lambda j, *_: (j, 0))],
+            [pltpu.VMEM((slots, ff), BF16)],
+        )
         sum_far, sum_last = chain(
             sliced(shared_far, 2), (1,),
-            [whole(a) for a in (pos, gate, here_far, rs_far, here_last, rs_last)],
+            [whole(a) for a in (pos, gate, here_far, rs_far)],
             [entire(tok), entire(tok)],
         )
         one = over_expert(sum_last, inward)
         mid_last = hold(mid_last, out_far)
         out_last = over_expert(mid_last, outward)
+        rs_near = hold(rs_near)
         two = over_expert(plus(sum_last, one), middle)
         sum_far = hold(sum_far, one)
         one_far = over_expert(sum_far, inward)

time: 193 us -> 179 us (0.927)
  waiting for transfers between devices: 57.5 us -> 40 us
  starting transfers between devices: 39.6 us -> 41.7 us
    ppermute x22 -> x21, waiting for transfers between devices: 44.9 us -> 32.3 us  [over_expert(): return lax.ppermute(a, 'expert', pairs)]
    ppermute x4, waiting for transfers between devices: 12.6 us -> 7.7 us  [over_dp(): return lax.ppermute(a, 'dp', pairs)]
    ppermute x22 -> x21, starting transfers between devices: 37.2 us -> 39.5 us  [over_expert(): return lax.ppermute(a, 'expert', pairs)]
    unnamed x86 -> x94, local copies, waits for them, and re-layouts: 15.6 us -> 16.7 us
  transfers between devices with their start and end apart: 26 -> 25, of which waited for: 10 -> 11; matrix products, arithmetic and copies ran while one was open for 4% -> 4% of each run, Pallas kernels for 36% -> 38%
where the time goes in v3:
time: 179 us; the launch traced here: 178 us
  Pallas kernels  71.5 us (40%)
  starting transfers between devices  41.7 us (23%)
  waiting for transfers between devices  40 us (22%)
  local copies, waits for them, and re-layouts  18.7 us (10%)
  other arithmetic  5.42 us (3%)
    pallas_call x17, Pallas kernels, call(): pl.pallas_call(body, out_shape=[jax.ShapeDtypeStruct(shape, dtype) for sh...  71.5 us
    ppermute x21, starting transfers between devices, over_expert(): return lax.ppermute(a, 'expert', pairs)  39.5 us
    ppermute x21, waiting for transfers between devices, over_expert(): return lax.ppermute(a, 'expert', pairs)  32.3 us
    unnamed x94, local copies, waits for them, and re-layouts  16.7 us
    ppermute x4, waiting for transfers between devices, over_dp(): return lax.ppermute(a, 'dp', pairs)  7.7 us
  transfers between devices with their start and end apart: 25, of which 11 were waited for; matrix products, arithmetic and copies ran while one was open for 4% of the time, Pallas kernels for 38%

profile of v3, /device:TPU:0, one launch (start us, length us, event | category | flops | bytes accessed | tf_op | source)
XLA Modules:
  0.0 178.3 jit_solution(6911549626260549278)
XLA Ops:
  2.3 4.9 %collective-permute-start.3 = (bf16[128,3584]{1,0:T(8,128)(2,1)}, bf16[128,3584]{1,0:T(8,128)(2,1)}, u32[]{:S(2)}, u32[]{:S(2)}) collective-permute-start(bf16[128,3584]{1,0:T(8,128)(2,1)} %refs_3_.2), channel_id=1, source_target_pairs={{0,2},{1,3},{2,0},{3,1},{4,6},{5,7},{6,4},{7,5},{8,10},{9,11},{10,... | collective-permute-start | bytes 2752520 | tf_op jit(solution)/shard_map/ppermute | solution.py:266
  10.6 7.5 %made.2 = (bf16[160,3584]{1,0:T(8,128)(2,1)}, bf16[160,3584]{1,0:T(8,128)(2,1)}, f32[8,128]{1,0:T(8,128)}) custom-call(s32[15]{0:T(128)} %concatenate.17.refs_0_, bf16[8,80,1024]{2,1,0:T(8,128)(2,1)} %bitcast.39, bf16[8,80,1024]{2,1,0:T(8,128)(2,1)} %bitcast.40, bf16[8,80,1024]{2,1,0:T(8,128)(2,1)} %bitcast.41, bf16[8,80,1024]{2,1,0:T(8,128)(2,1)} %bitcast.42, ...), custom_call_target="tpu_custom_call" | custom-call | flops 99999997952 | bytes 333333344 | tf_op jit(solution)/shard_map/made/pallas_call | solution.py:233
  19.6 7.5 %made.3 = (bf16[160,3584]{1,0:T(8,128)(2,1)}, bf16[160,3584]{1,0:T(8,128)(2,1)}, f32[8,128]{1,0:T(8,128)}) custom-call(s32[15]{0:T(128)} %concatenate.17.refs_0_, bf16[8,80,1024]{2,1,0:T(8,128)(2,1)} %bitcast.43, bf16[8,80,1024]{2,1,0:T(8,128)(2,1)} %bitcast.44, bf16[8,80,1024]{2,1,0:T(8,128)(2,1)} %bitcast.45, bf16[8,80,1024]{2,1,0:T(8,128)(2,1)} %bitcast.46, ...), custom_call_target="tpu_custom_call" | custom-call | flops 99999997952 | bytes 333333344 | tf_op jit(solution)/shard_map/made/pallas_call | solution.py:233
  37.8 2.5 %packed_near.1 = (bf16[160,3584]{1,0:T(8,128)(2,1)S(1)}, bf16[160,3584]{1,0:T(8,128)(2,1)S(1)}, f32[8,128]{1,0:T(8,128)S(1)}) custom-call(s32[15]{0:T(128)S(1)} %copy-done.15, s32[8,128]{1,0:T(8,128)S(1)} %get-tuple-element.52.refs_1_, f32[8,128]{1,0:T(8,128)S(1)} %get-tuple-element.53.refs_2_, bf16[128,3584]{1,0:T(8,128)(2,1)S(1)} %copy-done.11, ...), custom_call_target="tpu_custom_call" | custom-call | flops 1 | tf_op jit(solution)/shard_map/packed_near/pallas_call | solution.py:233
  43.4 3.2 %collective-permute-done.6.refs_4_ = bf16[160,3584]{1,0:T(8,128)(2,1)} collective-permute-done((bf16[160,3584]{1,0:T(8,128)(2,1)}, bf16[160,3584]{1,0:T(8,128)(2,1)}, u32[]{:S(2)}, u32[]{:S(2)}) %collective-permute-start.6) | collective-permute-done | bytes 1146912 | tf_op jit(solution)/shard_map/ppermute | solution.py:266
  46.6 3.9 %shared_far.1 = (bf16[128,3584]{1,0:T(8,128)(2,1)S(1)}, bf16[128,3584]{1,0:T(8,128)(2,1)}, f32[8,128]{1,0:T(8,128)S(1)}) custom-call(s32[15]{0:T(128)S(1)} %copy-done.15, s32[8,128]{1,0:T(8,128)S(1)} %get-tuple-element.52.refs_1_, f32[8,128]{1,0:T(8,128)S(1)} %get-tuple-element.53.refs_2_, bf16[160,3584]{1,0:T(8,128)(2,1)S(1)} %copy-done.33, ...), custom_call_target="tpu_custom_call" | custom-call | flops 99999997952 | bytes 333333344 | tf_op jit(solution)/shard_map/shared_far/pallas_call | solution.py:233
  52.0 4.9 %collective-permute-start.8 = (bf16[128,3584]{1,0:T(8,128)(2,1)}, bf16[128,3584]{1,0:T(8,128)(2,1)}, u32[]{:S(2)}, u32[]{:S(2)}) collective-permute-start(bf16[128,3584]{1,0:T(8,128)(2,1)} %get-tuple-element.62.refs_1_), channel_id=1, source_target_pairs={{0,2},{1,3},{6,4},{7,5},{8,10},{9,11},{14,12},{15,13},{16,18},{17,... | collective-permute-start | bytes 2752520 | tf_op jit(solution)/shard_map/ppermute | solution.py:266
  61.8 9.2 %collective-permute-done.4.refs_0_ = bf16[160,3584]{1,0:T(8,128)(2,1)S(1)} collective-permute-done((bf16[160,3584]{1,0:T(8,128)(2,1)}, bf16[160,3584]{1,0:T(8,128)(2,1)S(1)}, u32[]{:S(2)}, u32[]{:S(2)}) %collective-permute-start.4) | collective-permute-done | bytes 1146912 | tf_op jit(solution)/shard_map/ppermute | solution.py:266
  74.1 3.0 %add.86 = (bf16[128,3584]{1,0:T(8,128)(2,1)}, f32[8,128]{1,0:T(8,128)S(1)}) custom-call(s32[15]{0:T(128)S(1)} %copy-done.15, bf16[128,3584]{1,0:T(8,128)(2,1)} %get-tuple-element.62.refs_1_, bf16[128,3584]{1,0:T(8,128)(2,1)} %collective-permute-done.8.refs_2_, bf16[160,3584]{1,0:T(8,128)(2,1)S(1)} %copy-done.9), custom_call_target="tpu_custom_call" | custom-call | flops 99999997952 | bytes 333333344 | tf_op jit(solution)/shard_map/add/pallas_call | solution.py:233
  78.7 5.4 %collective-permute-start.13 = (bf16[128,3584]{1,0:T(8,128)(2,1)}, bf16[128,3584]{1,0:T(8,128)(2,1)S(1)}, u32[]{:S(2)}, u32[]{:S(2)}) collective-permute-start(bf16[128,3584]{1,0:T(8,128)(2,1)} %after.15.refs_7_.refs_1_), channel_id=1, source_target_pairs={{0,2},{1,3},{6,4},{7,5},{8,10},{9,11},{14,12},{15,13},{16,18},{17,... | collective-permute-start | bytes 2752520 | tf_op jit(solution)/shard_map/ppermute | solution.py:266
  84.1 2.4 %collective-permute-done.10.refs_6_ = bf16[128,3584]{1,0:T(8,128)(2,1)S(1)} collective-permute-done((bf16[128,3584]{1,0:T(8,128)(2,1)}, bf16[128,3584]{1,0:T(8,128)(2,1)S(1)}, u32[]{:S(2)}, u32[]{:S(2)}) %collective-permute-start.10) | collective-permute-done | bytes 917536 | tf_op jit(solution)/shard_map/ppermute | solution.py:266
  87.6 3.6 %packed_far.1 = (bf16[160,2048]{1,0:T(8,128)(2,1)S(1)}, bf16[160,1536]{1,0:T(8,128)(2,1)}, bf16[160,3584]{1,0:T(8,128)(2,1)S(1)}, f32[8,128]{1,0:T(8,128)S(1)}) custom-call(s32[15]{0:T(128)S(1)} %copy-done.15, s32[8,128]{1,0:T(8,128)S(1)} %get-tuple-element.52.refs_1_, f32[8,128]{1,0:T(8,128)S(1)} %get-tuple-element.53.refs_2_, ...), custom_call_target="tpu_custom_call" | custom-call | flops 99999997952 | bytes 333333344 | tf_op jit(solution)/shard_map/packed_far/pallas_call | solution.py:233
  93.2 6.5 %collective-permute-done.13.refs_2_ = bf16[128,3584]{1,0:T(8,128)(2,1)S(1)} collective-permute-done((bf16[128,3584]{1,0:T(8,128)(2,1)}, bf16[128,3584]{1,0:T(8,128)(2,1)S(1)}, u32[]{:S(2)}, u32[]{:S(2)}) %collective-permute-start.13) | collective-permute-done | bytes 917536 | tf_op jit(solution)/shard_map/ppermute | solution.py:266
  102.8 6.9 %collective-permute-done.12.refs_4_ = bf16[160,2048]{1,0:T(8,128)(2,1)S(1)} collective-permute-done((bf16[160,2048]{1,0:T(8,128)(2,1)S(1)}, bf16[160,2048]{1,0:T(8,128)(2,1)S(1)}, u32[]{:S(2)}, u32[]{:S(2)}) %collective-permute-start.12) | collective-permute-done | bytes 655392 | tf_op jit(solution)/shard_map/ppermute | solution.py:266
  109.7 4.6 %gave.2 = (bf16[512,2048]{1,0:T(8,128)(2,1)S(1)}, bf16[640,2048]{1,0:T(8,128)(2,1)S(1)}, f32[8,128]{1,0:T(8,128)S(1)}) custom-call(s32[15]{0:T(128)S(1)} %copy-done.15, bf16[160,3584]{1,0:T(8,128)(2,1)S(1)} %copy-done.24, bf16[160,3584]{1,0:T(8,128)(2,1)S(1)} %get-tuple-element.67.refs_2_, bf16[160,3584]{1,0:T(8,128)(2,1)} %collective-permute-done.11.refs_3_, ...), custom_call_target="tpu_custom_call" | custom-call | flops 99999997952 | bytes 333333344 | tf_op jit(solution)/shard_map/gave/pallas_call | solution.py:233
  114.4 4.1 %shared_near.1 = (f32[128,3584]{1,0:T(8,128)S(1)}, bf16[128,3584]{1,0:T(8,128)(2,1)}, f32[8,128]{1,0:T(8,128)S(1)}) custom-call(s32[15]{0:T(128)S(1)} %copy-done.15, s32[8,128]{1,0:T(8,128)S(1)} %get-tuple-element.52.refs_1_, f32[8,128]{1,0:T(8,128)S(1)} %get-tuple-element.53.refs_2_, bf16[160,3584]{1,0:T(8,128)(2,1)S(1)} %copy-done.32, ...), custom_call_target="tpu_custom_call" | custom-call | flops 99999997952 | bytes 333333344 | tf_op jit(solution)/shard_map/shared_near/pallas_call | solution.py:233
  120.6 4.0 %kept.2 = (bf16[256,2048]{1,0:T(8,128)(2,1)}, f32[256,2048]{1,0:T(8,128)S(1)}, f32[8,128]{1,0:T(8,128)S(1)}) custom-call(s32[15]{0:T(128)S(1)} %copy-done.15, bf16[640,2048]{1,0:T(8,128)(2,1)S(1)} %get-tuple-element.76.refs_1_, bf16[1024,640]{1,0:T(8,128)(2,1)S(1)} %get-tuple-element.70.refs_5_.refs_2_, ...), custom_call_target="tpu_custom_call" | custom-call | flops 99999997952 | bytes 333333344 | tf_op jit(solution)/shard_map/kept/pallas_call | solution.py:233
  124.6 4.9 %gave.3 = (bf16[512,1536]{1,0:T(8,128)(2,1)}, bf16[640,1536]{1,0:T(8,128)(2,1)S(1)}, f32[8,128]{1,0:T(8,128)S(1)}) custom-call(s32[15]{0:T(128)S(1)} %copy-done.15, bf16[160,3584]{1,0:T(8,128)(2,1)S(1)} %copy-done.24, bf16[160,3584]{1,0:T(8,128)(2,1)S(1)} %copy-done.35, bf16[160,3584]{1,0:T(8,128)(2,1)} %collective-permute-done.11.refs_3_, ...), custom_call_target="tpu_custom_call" | custom-call | flops 99999997952 | bytes 333333344 | tf_op jit(solution)/shard_map/gave/pallas_call | solution.py:233
  132.3 13.1 %hidden.1 = (bf16[8,80,1024]{2,1,0:T(8,128)(2,1)}, f32[8,80,128]{2,1,0:T(8,128)}, f32[8,128]{1,0:T(8,128)}) custom-call(s32[15]{0:T(128)} %concatenate.17.refs_0_, bf16[640,2048]{1,0:T(8,128)(2,1)} %copy-done.27, bf16[640,1536]{1,0:T(8,128)(2,1)} %copy-done.4, bf16[1,1024,3584]{2,1,0:T(8,128)(2,1)} %refs_3_.3, bf16[8,80,1024]{2,1,0:T(8,128)(2,1)} %bitcast.47, ...), custom_call_target="tpu_custom_call" | custom-call | flops 99999997952 | bytes 333333344 | tf_op jit(solution)/shard_map/hidden/pallas_call | solution.py:233
  147.4 2.7 %kept.3 = (bf16[256,1536]{1,0:T(8,128)(2,1)S(1)}, f32[256,1536]{1,0:T(8,128)S(1)}, f32[8,128]{1,0:T(8,128)S(1)}) custom-call(s32[15]{0:T(128)S(1)} %copy-done.16, bf16[640,1536]{1,0:T(8,128)(2,1)S(1)} %copy-done.5, bf16[1024,640]{1,0:T(8,128)(2,1)S(1)} %copy-done.7, bf16[512,1536]{1,0:T(8,128)(2,1)S(1)} %collective-permute-done.17.refs_3_, ...), custom_call_target="tpu_custom_call" | custom-call | flops 1 | tf_op jit(solution)/shard_map/kept/pallas_call | solution.py:233
  159.5 2.7 %collective-permute-start.21 = (f32[2,80]{1,0:T(2,128)S(1)}, f32[2,80]{1,0:T(2,128)S(1)}, u32[]{:S(2)}, u32[]{:S(2)}) collective-permute-start(f32[2,80]{1,0:T(2,128)S(1)} %bitcast.64), channel_id=1, source_target_pairs={{0,2},{1,3},{2,0},{3,1},{4,6},{5,7},{6,4},{7,5},{8,10},{9,11},{10,... | collective-permute-start | bytes 1928 | tf_op jit(solution)/shard_map/ppermute | solution.py:266
  163.7 3.5 %add_three.1 = (bf16[128,3584]{1,0:T(8,128)(2,1)}, f32[8,128]{1,0:T(8,128)S(1)}) custom-call(s32[15]{0:T(128)S(1)} %copy-done.16, f32[128,3584]{1,0:T(8,128)S(1)} %copy-done.31, bf16[128,3584]{1,0:T(8,128)(2,1)} %after.18.refs_1_.refs_2_, bf16[128,3584]{1,0:T(8,128)(2,1)} %after.16.refs_4_.refs_3_, bf16[256,2048]{1,0:T(8,128)(2,1)} %after.19.refs_4_.refs_2_), custom_call_target="tpu_custom_call" | custom-call | flops 99999997952 | bytes 333333344 | tf_op jit(solution)/shard_map/add_three/pallas_call | solution.py:233
  168.0 7.2 %collective-permute-done.24.refs_4_ = bf16[256,1536]{1,0:T(8,128)(2,1)S(1)} collective-permute-done((bf16[256,1536]{1,0:T(8,128)(2,1)}, bf16[256,1536]{1,0:T(8,128)(2,1)S(1)}, u32[]{:S(2)}, u32[]{:S(2)}) %collective-permute-start.24) | collective-permute-done | bytes 786464 | tf_op jit(solution)/shard_map/ppermute | solution.py:269
  175.3 3.0 %add_chunks.1 = (bf16[1,256,3584]{2,1,0:T(8,128)(2,1)}, f32[8,128]{1,0:T(8,128)}) custom-call(s32[15]{0:T(128)S(1)} %copy-done.16, f32[256,2048]{1,0:T(8,128)S(1)} %copy-done.29, bf16[256,2048]{1,0:T(8,128)(2,1)} %after.19.refs_4_.refs_2_, f32[256,1536]{1,0:T(8,128)S(1)} %copy-done.22, bf16[256,1536]{1,0:T(8,128)(2,1)S(1)} %collective-permute-done.24.refs_4_, ...), custom_call_target="tpu_custom_call" | custom-call | flops 99999997952 | bytes 333333344 | tf_op jit(solution)/shard_map/add_chunks/pallas_call | solution.py:233
  (169 shorter events, 56.1 us)
Async XLA Ops:
  0.6 30.0 %collective-permute-start.2 = (bf16[128,3584]{1,0:T(8,128)(2,1)}, bf16[128,3584]{1,0:T(8,128)(2,1)}, u32[]{:S(2)}, u32[]{:S(2)}) collective-permute-start(bf16[128,3584]{1,0:T(8,128)(2,1)} %refs_3_.2), channel_id=1, source_target_pairs={{2,4},{3,5},{4,2},{5,3},{10,12},{11,13},{12,10},{13,11},{18,20},{1... | collective-permute-start | bytes 2752520 | tf_op jit(solution)/shard_map/ppermute | solution.py:266
  2.3 28.3 %collective-permute-start.3 = (bf16[128,3584]{1,0:T(8,128)(2,1)}, bf16[128,3584]{1,0:T(8,128)(2,1)}, u32[]{:S(2)}, u32[]{:S(2)}) collective-permute-start(bf16[128,3584]{1,0:T(8,128)(2,1)} %refs_3_.2), channel_id=1, source_target_pairs={{0,2},{1,3},{2,0},{3,1},{4,6},{5,7},{6,4},{7,5},{8,10},{9,11},{10,... | collective-permute-start | bytes 2752520 | tf_op jit(solution)/shard_map/ppermute | solution.py:266
  9.2 18.5 %collective-permute-start = (f32[8,128]{1,0:T(8,128)}, f32[8,128]{1,0:T(8,128)}, u32[]{:S(2)}, u32[]{:S(2)}) collective-permute-start(f32[8,128]{1,0:T(8,128)} %maximum_bitcast_fusion), channel_id=1, source_target_pairs={{0,2},{1,3},{2,0},{3,1},{4,6},{5,7},{6,4},{7,5},{8,10},{9,11},{10,... | collective-permute-start | bytes 12296 | tf_op jit(solution)/shard_map/ppermute | solution.py:266
  18.1 28.5 %collective-permute-start.6 = (bf16[160,3584]{1,0:T(8,128)(2,1)}, bf16[160,3584]{1,0:T(8,128)(2,1)}, u32[]{:S(2)}, u32[]{:S(2)}) collective-permute-start(bf16[160,3584]{1,0:T(8,128)(2,1)} %get-tuple-element.58), channel_id=1, source_target_pairs={{0,1},{1,0},{2,3},{3,2},{4,5},{5,4},{6,7},{7,6},{8,9},{9,8},{10,11... | collective-permute-start | bytes 3440648 | tf_op jit(solution)/shard_map/ppermute | solution.py:266
  29.0 4.8 %collective-permute-start.1 = (f32[16,128]{1,0:T(8,128)}, f32[16,128]{1,0:T(8,128)S(1)}, u32[]{:S(2)}, u32[]{:S(2)}) collective-permute-start(f32[16,128]{1,0:T(8,128)} %after.10.refs_1_), channel_id=1, source_target_pairs={{0,4},{1,5},{4,0},{5,1},{2,6},{3,7},{6,2},{7,3},{8,12},{9,13},{12,... | collective-permute-start | bytes 24584 | tf_op jit(solution)/shard_map/ppermute | solution.py:266
  30.6 29.0 %collective-permute-start.7 = (bf16[128,3584]{1,0:T(8,128)(2,1)}, bf16[128,3584]{1,0:T(8,128)(2,1)}, u32[]{:S(2)}, u32[]{:S(2)}) collective-permute-start(bf16[128,3584]{1,0:T(8,128)(2,1)} %after.11.refs_3_), channel_id=1, source_target_pairs={{2,0},{3,1},{4,6},{5,7},{10,8},{11,9},{12,14},{13,15},{18,16},{19,... | collective-permute-start | bytes 2752520 | tf_op jit(solution)/shard_map/ppermute | solution.py:266
  35.0 36.0 %collective-permute-start.4 = (bf16[160,3584]{1,0:T(8,128)(2,1)}, bf16[160,3584]{1,0:T(8,128)(2,1)S(1)}, u32[]{:S(2)}, u32[]{:S(2)}) collective-permute-start(bf16[160,3584]{1,0:T(8,128)(2,1)} %after.12.refs_5_), channel_id=1, source_target_pairs={{0,1},{1,0},{2,3},{3,2},{4,5},{5,4},{6,7},{7,6},{8,9},{9,8},{10,11... | collective-permute-start | bytes 3440648 | tf_op jit(solution)/shard_map/ppermute | solution.py:266
  42.6 17.0 %collective-permute-start.5 = (bf16[128,3584]{1,0:T(8,128)(2,1)}, bf16[128,3584]{1,0:T(8,128)(2,1)S(1)}, u32[]{:S(2)}, u32[]{:S(2)}) collective-permute-start(bf16[128,3584]{1,0:T(8,128)(2,1)} %collective-permute-done.3.refs_2_.refs_4_), channel_id=1, source_target_pairs={{2,4},{3,5},{4,2},{5,3},{10,12},{11,13},{12,10},{13,11},{18,20},{1... | collective-permute-start | bytes 2752520 | tf_op jit(solution)/shard_map/ppermute | solution.py:266
  52.0 20.8 %collective-permute-start.8 = (bf16[128,3584]{1,0:T(8,128)(2,1)}, bf16[128,3584]{1,0:T(8,128)(2,1)}, u32[]{:S(2)}, u32[]{:S(2)}) collective-permute-start(bf16[128,3584]{1,0:T(8,128)(2,1)} %get-tuple-element.62.refs_1_), channel_id=1, source_target_pairs={{0,2},{1,3},{6,4},{7,5},{8,10},{9,11},{14,12},{15,13},{16,18},{17,... | collective-permute-start | bytes 2752520 | tf_op jit(solution)/shard_map/ppermute | solution.py:266
  58.1 44.7 %collective-permute-start.11 = (bf16[160,3584]{1,0:T(8,128)(2,1)}, bf16[160,3584]{1,0:T(8,128)(2,1)}, u32[]{:S(2)}, u32[]{:S(2)}) collective-permute-start(bf16[160,3584]{1,0:T(8,128)(2,1)} %copy-done.25), channel_id=1, source_target_pairs={{0,1},{1,0},{2,3},{3,2},{4,5},{5,4},{6,7},{7,6},{8,9},{9,8},{10,11... | collective-permute-start | bytes 3440648 | tf_op jit(solution)/shard_map/ppermute | solution.py:266
  60.5 25.9 %collective-permute-start.10 = (bf16[128,3584]{1,0:T(8,128)(2,1)}, bf16[128,3584]{1,0:T(8,128)(2,1)S(1)}, u32[]{:S(2)}, u32[]{:S(2)}) collective-permute-start(bf16[128,3584]{1,0:T(8,128)(2,1)} %after.13.refs_1_.refs_5_), channel_id=1, source_target_pairs={{2,0},{3,1},{4,6},{5,7},{10,8},{11,9},{12,14},{13,15},{18,16},{19,... | collective-permute-start | bytes 2752520 | tf_op jit(solution)/shard_map/ppermute | solution.py:266
  77.1 37.3 %collective-permute-start.9 = (bf16[128,3584]{1,0:T(8,128)(2,1)}, bf16[128,3584]{1,0:T(8,128)(2,1)}, u32[]{:S(2)}, u32[]{:S(2)}) collective-permute-start(bf16[128,3584]{1,0:T(8,128)(2,1)} %get-tuple-element.63), channel_id=1, source_target_pairs={{2,4},{3,5},{4,2},{5,3},{10,12},{11,13},{12,10},{13,11},{18,20},{1... | collective-permute-start | bytes 2752520 | tf_op jit(solution)/shard_map/ppermute | solution.py:266
  78.7 21.0 %collective-permute-start.13 = (bf16[128,3584]{1,0:T(8,128)(2,1)}, bf16[128,3584]{1,0:T(8,128)(2,1)S(1)}, u32[]{:S(2)}, u32[]{:S(2)}) collective-permute-start(bf16[128,3584]{1,0:T(8,128)(2,1)} %after.15.refs_7_.refs_1_), channel_id=1, source_target_pairs={{0,2},{1,3},{6,4},{7,5},{8,10},{9,11},{14,12},{15,13},{16,18},{17,... | collective-permute-start | bytes 2752520 | tf_op jit(solution)/shard_map/ppermute | solution.py:266
  91.2 18.5 %collective-permute-start.12 = (bf16[160,2048]{1,0:T(8,128)(2,1)S(1)}, bf16[160,2048]{1,0:T(8,128)(2,1)S(1)}, u32[]{:S(2)}, u32[]{:S(2)}) collective-permute-start(bf16[160,2048]{1,0:T(8,128)(2,1)S(1)} %get-tuple-element.69), channel_id=1, source_target_pairs={{0,1},{1,0},{2,3},{3,2},{4,5},{5,4},{6,7},{7,6},{8,9},{9,8},{10,11... | collective-permute-start | bytes 1966088 | tf_op jit(solution)/shard_map/ppermute | solution.py:266
  92.9 31.7 %collective-permute-start.15 = (bf16[160,1536]{1,0:T(8,128)(2,1)}, bf16[160,1536]{1,0:T(8,128)(2,1)}, u32[]{:S(2)}, u32[]{:S(2)}) collective-permute-start(bf16[160,1536]{1,0:T(8,128)(2,1)} %get-tuple-element.77), channel_id=1, source_target_pairs={{0,1},{1,0},{2,3},{3,2},{4,5},{5,4},{6,7},{7,6},{8,9},{9,8},{10,11... | collective-permute-start | bytes 1474568 | tf_op jit(solution)/shard_map/ppermute | solution.py:266
  101.2 44.2 %collective-permute-start.18 = (bf16[128,3584]{1,0:T(8,128)(2,1)}, bf16[128,3584]{1,0:T(8,128)(2,1)}, u32[]{:S(2)}, u32[]{:S(2)}) collective-permute-start(bf16[128,3584]{1,0:T(8,128)(2,1)} %get-tuple-element.85), channel_id=1, source_target_pairs={{2,4},{3,5},{4,2},{5,3},{10,12},{11,13},{12,10},{13,11},{18,20},{1... | collective-permute-start | bytes 2752520 | tf_op jit(solution)/shard_map/ppermute | solution.py:266
  114.3 6.2 %collective-permute-start.16 = (bf16[512,2048]{1,0:T(8,128)(2,1)S(1)}, bf16[512,2048]{1,0:T(8,128)(2,1)S(1)}, u32[]{:S(2)}, u32[]{:S(2)}) collective-permute-start(bf16[512,2048]{1,0:T(8,128)(2,1)S(1)} %get-tuple-element.78), channel_id=1, source_target_pairs={{0,8},{8,0},{16,24},{24,16},{1,9},{9,1},{17,25},{25,17},{2,10},{10... | collective-permute-start | bytes 6291464 | tf_op jit(solution)/shard_map/ppermute | solution.py:269
  118.5 37.7 %collective-permute-start.14 = (bf16[128,3584]{1,0:T(8,128)(2,1)}, bf16[128,3584]{1,0:T(8,128)(2,1)}, u32[]{:S(2)}, u32[]{:S(2)}) collective-permute-start(bf16[128,3584]{1,0:T(8,128)(2,1)} %get-tuple-element.75), channel_id=1, source_target_pairs={{0,2},{1,3},{2,0},{3,1},{4,6},{5,7},{6,4},{7,5},{8,10},{9,11},{10,... | collective-permute-start | bytes 2752520 | tf_op jit(solution)/shard_map/ppermute | solution.py:266
  130.8 14.7 %collective-permute-start.17 = (bf16[512,1536]{1,0:T(8,128)(2,1)}, bf16[512,1536]{1,0:T(8,128)(2,1)S(1)}, u32[]{:S(2)}, u32[]{:S(2)}) collective-permute-start(bf16[512,1536]{1,0:T(8,128)(2,1)} %get-tuple-element.84), channel_id=1, source_target_pairs={{0,8},{8,0},{16,24},{24,16},{1,9},{9,1},{17,25},{25,17},{2,10},{10... | collective-permute-start | bytes 4718600 | tf_op jit(solution)/shard_map/ppermute | solution.py:269
  130.8 25.9 %collective-permute-start.19 = (bf16[256,2048]{1,0:T(8,128)(2,1)}, bf16[256,2048]{1,0:T(8,128)(2,1)}, u32[]{:S(2)}, u32[]{:S(2)}) collective-permute-start(bf16[256,2048]{1,0:T(8,128)(2,1)} %get-tuple-element.88), channel_id=1, source_target_pairs={{0,16},{8,24},{16,0},{24,8},{1,17},{9,25},{17,1},{25,9},{2,18},{10... | collective-permute-start | bytes 3145736 | tf_op jit(solution)/shard_map/ppermute | solution.py:269
  155.6 19.7 %collective-permute-start.24 = (bf16[256,1536]{1,0:T(8,128)(2,1)}, bf16[256,1536]{1,0:T(8,128)(2,1)S(1)}, u32[]{:S(2)}, u32[]{:S(2)}) collective-permute-start(bf16[256,1536]{1,0:T(8,128)(2,1)} %copy-done.26), channel_id=1, source_target_pairs={{0,16},{8,24},{16,0},{24,8},{1,17},{9,25},{17,1},{25,9},{2,18},{10... | collective-permute-start | bytes 2359304 | tf_op jit(solution)/shard_map/ppermute | solution.py:269
  157.7 9.5 %collective-permute-start.23 = (f32[2,80]{1,0:T(2,128)S(1)}, f32[2,80]{1,0:T(2,128)S(1)}, u32[]{:S(2)}, u32[]{:S(2)}) collective-permute-start(f32[2,80]{1,0:T(2,128)S(1)} %bitcast.65), channel_id=1, source_target_pairs={{0,6},{1,7},{6,0},{7,1},{2,4},{3,5},{4,2},{5,3},{8,14},{9,15},{14,... | collective-permute-start | bytes 1928 | tf_op jit(solution)/shard_map/ppermute | solution.py:266
  159.1 8.1 %collective-permute-start.22 = (f32[2,80]{1,0:T(2,128)S(1)}, f32[2,80]{1,0:T(2,128)S(1)}, u32[]{:S(2)}, u32[]{:S(2)}) collective-permute-start(f32[2,80]{1,0:T(2,128)S(1)} %select_bitcast_fusion), channel_id=1, source_target_pairs={{0,4},{1,5},{4,0},{5,1},{2,6},{3,7},{6,2},{7,3},{8,12},{9,13},{12,... | collective-permute-start | bytes 1928 | tf_op jit(solution)/shard_map/ppermute | solution.py:266
  159.5 7.7 %collective-permute-start.21 = (f32[2,80]{1,0:T(2,128)S(1)}, f32[2,80]{1,0:T(2,128)S(1)}, u32[]{:S(2)}, u32[]{:S(2)}) collective-permute-start(f32[2,80]{1,0:T(2,128)S(1)} %bitcast.64), channel_id=1, source_target_pairs={{0,2},{1,3},{2,0},{3,1},{4,6},{5,7},{6,4},{7,5},{8,10},{9,11},{10,... | collective-permute-start | bytes 1928 | tf_op jit(solution)/shard_map/ppermute | solution.py:266
  (48 other events, 285.2 us)

commit v4 on v3

--- a/solution.py
+++ b/solution.py
@@ -13,7 +13,7 @@
 COST = 10**11
 COSTS = {'positions1': 1, 'packed_near1': 1, 'turned1': 1, 'kept2': 1}
 LIMIT = 24
-LIMITS = {'hidden': 60, 'made': 60}
+LIMITS = {'hidden': 40, 'made': 60}
 
 
 def split_expert(n):
@@ -454,8 +454,9 @@
 
         slots = n_expert * cap
 
-        mids = hold(mids, buddies)
+        buddies = hold(buddies)
         mid_last = over_expert(buddies, middle)
+        mids = hold(mids)
         out_far = over_expert(mids, outward)
 
         def positions(s, near_ref, far_ref, pos_ref, gate_ref):

time: 179 us -> 178 us (level)
  waiting for transfers between devices: 40 us -> 43.4 us
  Pallas kernels: 71.5 us -> 68.5 us
    pallas_call x17, Pallas kernels: 71.5 us -> 68.5 us  [call(): pl.pallas_call(body, out_shape=[jax.ShapeDtypeStruct(shape, dtype) for sh...]
    unnamed x94 -> x92, local copies, waits for them, and re-layouts: 16.7 us -> 15.3 us
  transfers between devices with their start and end apart: 25 -> 25, of which waited for: 11 -> 9; matrix products, arithmetic and copies ran while one was open for 4% -> 4% of each run, Pallas kernels for 38% -> 37%
where the time goes in v4:
time: 178 us; the launch traced here: 177 us
  Pallas kernels  68.5 us (38%)
  waiting for transfers between devices  43.4 us (24%)
  starting transfers between devices  41.3 us (23%)
  local copies, waits for them, and re-layouts  17.3 us (10%)
  other arithmetic  5.43 us (3%)
    pallas_call x17, Pallas kernels, call(): pl.pallas_call(body, out_shape=[jax.ShapeDtypeStruct(shape, dtype) for sh...  68.5 us
    ppermute x21, starting transfers between devices, over_expert(): return lax.ppermute(a, 'expert', pairs)  39 us
    ppermute x21, waiting for transfers between devices, over_expert(): return lax.ppermute(a, 'expert', pairs)  33.9 us
    unnamed x92, local copies, waits for them, and re-layouts  15.3 us
    ppermute x4, waiting for transfers between devices, over_dp(): return lax.ppermute(a, 'dp', pairs)  9.43 us
  transfers between devices with their start and end apart: 25, of which 9 were waited for; matrix products, arithmetic and copies ran while one was open for 4% of the time, Pallas kernels for 37%

profile of v4, /device:TPU:0, one launch (start us, length us, event | category | flops | bytes accessed | tf_op | source)
XLA Modules:
  0.0 177.0 jit_solution(10912039873567965317)
XLA Ops:
  2.3 4.9 %collective-permute-start.3 = (bf16[128,3584]{1,0:T(8,128)(2,1)}, bf16[128,3584]{1,0:T(8,128)(2,1)}, u32[]{:S(2)}, u32[]{:S(2)}) collective-permute-start(bf16[128,3584]{1,0:T(8,128)(2,1)} %refs_3_.2), channel_id=1, source_target_pairs={{0,2},{1,3},{2,0},{3,1},{4,6},{5,7},{6,4},{7,5},{8,10},{9,11},{10,... | collective-permute-start | bytes 2752520 | tf_op jit(solution)/shard_map/ppermute | solution.py:266
  10.6 7.5 %made.2 = (bf16[160,3584]{1,0:T(8,128)(2,1)}, bf16[160,3584]{1,0:T(8,128)(2,1)}, f32[8,128]{1,0:T(8,128)}) custom-call(s32[15]{0:T(128)} %concatenate.17.refs_0_, bf16[8,80,1024]{2,1,0:T(8,128)(2,1)} %bitcast.39, bf16[8,80,1024]{2,1,0:T(8,128)(2,1)} %bitcast.40, bf16[8,80,1024]{2,1,0:T(8,128)(2,1)} %bitcast.41, bf16[8,80,1024]{2,1,0:T(8,128)(2,1)} %bitcast.42, ...), custom_call_target="tpu_custom_call" | custom-call | flops 99999997952 | bytes 333333344 | tf_op jit(solution)/shard_map/made/pallas_call | solution.py:233
  19.6 7.6 %made.3 = (bf16[160,3584]{1,0:T(8,128)(2,1)}, bf16[160,3584]{1,0:T(8,128)(2,1)}, f32[8,128]{1,0:T(8,128)}) custom-call(s32[15]{0:T(128)} %concatenate.17.refs_0_, bf16[8,80,1024]{2,1,0:T(8,128)(2,1)} %bitcast.43, bf16[8,80,1024]{2,1,0:T(8,128)(2,1)} %bitcast.44, bf16[8,80,1024]{2,1,0:T(8,128)(2,1)} %bitcast.45, bf16[8,80,1024]{2,1,0:T(8,128)(2,1)} %bitcast.46, ...), custom_call_target="tpu_custom_call" | custom-call | flops 99999997952 | bytes 333333344 | tf_op jit(solution)/shard_map/made/pallas_call | solution.py:233
  37.8 2.5 %packed_near.1 = (bf16[160,3584]{1,0:T(8,128)(2,1)S(1)}, bf16[160,3584]{1,0:T(8,128)(2,1)S(1)}, f32[8,128]{1,0:T(8,128)S(1)}) custom-call(s32[15]{0:T(128)S(1)} %copy-done.14, s32[8,128]{1,0:T(8,128)S(1)} %get-tuple-element.52.refs_1_, f32[8,128]{1,0:T(8,128)S(1)} %get-tuple-element.53.refs_2_, bf16[128,3584]{1,0:T(8,128)(2,1)S(1)} %copy-done.8, ...), custom_call_target="tpu_custom_call" | custom-call | flops 1 | tf_op jit(solution)/shard_map/packed_near/pallas_call | solution.py:233
  42.7 3.9 %collective-permute-done.6.refs_4_ = bf16[160,3584]{1,0:T(8,128)(2,1)} collective-permute-done((bf16[160,3584]{1,0:T(8,128)(2,1)}, bf16[160,3584]{1,0:T(8,128)(2,1)}, u32[]{:S(2)}, u32[]{:S(2)}) %collective-permute-start.6) | collective-permute-done | bytes 1146912 | tf_op jit(solution)/shard_map/ppermute | solution.py:266
  46.6 3.9 %shared_far.1 = (bf16[128,3584]{1,0:T(8,128)(2,1)S(1)}, bf16[128,3584]{1,0:T(8,128)(2,1)}, f32[8,128]{1,0:T(8,128)S(1)}) custom-call(s32[15]{0:T(128)S(1)} %copy-done.14, s32[8,128]{1,0:T(8,128)S(1)} %get-tuple-element.52.refs_1_, f32[8,128]{1,0:T(8,128)S(1)} %get-tuple-element.53.refs_2_, bf16[160,3584]{1,0:T(8,128)(2,1)S(1)} %copy-done.33, ...), custom_call_target="tpu_custom_call" | custom-call | flops 99999997952 | bytes 333333344 | tf_op jit(solution)/shard_map/shared_far/pallas_call | solution.py:233
  52.0 4.0 %collective-permute-start.8 = (bf16[128,3584]{1,0:T(8,128)(2,1)}, bf16[128,3584]{1,0:T(8,128)(2,1)S(1)}, u32[]{:S(2)}, u32[]{:S(2)}) collective-permute-start(bf16[128,3584]{1,0:T(8,128)(2,1)} %get-tuple-element.62.refs_1_), channel_id=1, source_target_pairs={{0,2},{1,3},{6,4},{7,5},{8,10},{9,11},{14,12},{15,13},{16,18},{17,... | collective-permute-start | bytes 2752520 | tf_op jit(solution)/shard_map/ppermute | solution.py:266
  60.9 10.3 %collective-permute-done.4.refs_0_ = bf16[160,3584]{1,0:T(8,128)(2,1)} collective-permute-done((bf16[160,3584]{1,0:T(8,128)(2,1)}, bf16[160,3584]{1,0:T(8,128)(2,1)}, u32[]{:S(2)}, u32[]{:S(2)}) %collective-permute-start.4) | collective-permute-done | bytes 1146912 | tf_op jit(solution)/shard_map/ppermute | solution.py:266
  72.0 2.8 %add.86 = (bf16[128,3584]{1,0:T(8,128)(2,1)}, f32[8,128]{1,0:T(8,128)S(1)}) custom-call(s32[15]{0:T(128)S(1)} %copy-done.14, bf16[128,3584]{1,0:T(8,128)(2,1)} %get-tuple-element.62.refs_1_, bf16[128,3584]{1,0:T(8,128)(2,1)S(1)} %collective-permute-done.8.refs_2_, bf16[160,3584]{1,0:T(8,128)(2,1)} %after.16.refs_3_.refs_4_), custom_call_target="tpu_custom_call" | custom-call | flops 99999997952 | bytes 333333344 | tf_op jit(solution)/shard_map/add/pallas_call | solution.py:233
  76.4 5.6 %collective-permute-start.13 = (bf16[128,3584]{1,0:T(8,128)(2,1)}, bf16[128,3584]{1,0:T(8,128)(2,1)S(1)}, u32[]{:S(2)}, u32[]{:S(2)}) collective-permute-start(bf16[128,3584]{1,0:T(8,128)(2,1)} %after.17.refs_7_.refs_1_), channel_id=1, source_target_pairs={{0,2},{1,3},{6,4},{7,5},{8,10},{9,11},{14,12},{15,13},{16,18},{17,... | collective-permute-start | bytes 2752520 | tf_op jit(solution)/shard_map/ppermute | solution.py:266
  83.2 3.9 %packed_far.1 = (bf16[160,2048]{1,0:T(8,128)(2,1)S(1)}, bf16[160,1536]{1,0:T(8,128)(2,1)}, bf16[160,3584]{1,0:T(8,128)(2,1)S(1)}, f32[8,128]{1,0:T(8,128)S(1)}) custom-call(s32[15]{0:T(128)S(1)} %copy-done.14, s32[8,128]{1,0:T(8,128)S(1)} %get-tuple-element.52.refs_1_, f32[8,128]{1,0:T(8,128)S(1)} %get-tuple-element.53.refs_2_, ...), custom_call_target="tpu_custom_call" | custom-call | flops 99999997952 | bytes 333333344 | tf_op jit(solution)/shard_map/packed_far/pallas_call | solution.py:233
  89.1 8.2 %collective-permute-done.13.refs_2_ = bf16[128,3584]{1,0:T(8,128)(2,1)S(1)} collective-permute-done((bf16[128,3584]{1,0:T(8,128)(2,1)}, bf16[128,3584]{1,0:T(8,128)(2,1)S(1)}, u32[]{:S(2)}, u32[]{:S(2)}) %collective-permute-start.13) | collective-permute-done | bytes 917536 | tf_op jit(solution)/shard_map/ppermute | solution.py:266
  100.5 9.2 %collective-permute-done.12.refs_4_ = bf16[160,2048]{1,0:T(8,128)(2,1)S(1)} collective-permute-done((bf16[160,2048]{1,0:T(8,128)(2,1)S(1)}, bf16[160,2048]{1,0:T(8,128)(2,1)S(1)}, u32[]{:S(2)}, u32[]{:S(2)}) %collective-permute-start.12) | collective-permute-done | bytes 655392 | tf_op jit(solution)/shard_map/ppermute | solution.py:266
  109.7 4.5 %gave.2 = (bf16[512,2048]{1,0:T(8,128)(2,1)S(1)}, bf16[640,2048]{1,0:T(8,128)(2,1)S(1)}, f32[8,128]{1,0:T(8,128)S(1)}) custom-call(s32[15]{0:T(128)S(1)} %copy-done.14, bf16[160,3584]{1,0:T(8,128)(2,1)S(1)} %copy-done.24, bf16[160,3584]{1,0:T(8,128)(2,1)S(1)} %get-tuple-element.67.refs_2_, bf16[160,3584]{1,0:T(8,128)(2,1)} %collective-permute-done.11.refs_3_, ...), custom_call_target="tpu_custom_call" | custom-call | flops 99999997952 | bytes 333333344 | tf_op jit(solution)/shard_map/gave/pallas_call | solution.py:233
  114.3 4.1 %shared_near.1 = (f32[128,3584]{1,0:T(8,128)S(1)}, bf16[128,3584]{1,0:T(8,128)(2,1)}, f32[8,128]{1,0:T(8,128)S(1)}) custom-call(s32[15]{0:T(128)S(1)} %copy-done.14, s32[8,128]{1,0:T(8,128)S(1)} %get-tuple-element.52.refs_1_, f32[8,128]{1,0:T(8,128)S(1)} %get-tuple-element.53.refs_2_, bf16[160,3584]{1,0:T(8,128)(2,1)S(1)} %copy-done.32, ...), custom_call_target="tpu_custom_call" | custom-call | flops 99999997952 | bytes 333333344 | tf_op jit(solution)/shard_map/shared_near/pallas_call | solution.py:233
  120.5 4.0 %kept.2 = (bf16[256,2048]{1,0:T(8,128)(2,1)}, f32[256,2048]{1,0:T(8,128)S(1)}, f32[8,128]{1,0:T(8,128)S(1)}) custom-call(s32[15]{0:T(128)S(1)} %copy-done.14, bf16[640,2048]{1,0:T(8,128)(2,1)S(1)} %get-tuple-element.76.refs_1_, bf16[1024,640]{1,0:T(8,128)(2,1)S(1)} %get-tuple-element.70.refs_5_.refs_2_, ...), custom_call_target="tpu_custom_call" | custom-call | flops 99999997952 | bytes 333333344 | tf_op jit(solution)/shard_map/kept/pallas_call | solution.py:233
  125.9 5.4 %gave.3 = (bf16[512,1536]{1,0:T(8,128)(2,1)}, bf16[640,1536]{1,0:T(8,128)(2,1)S(1)}, f32[8,128]{1,0:T(8,128)S(1)}) custom-call(s32[15]{0:T(128)S(1)} %copy-done.14, bf16[160,3584]{1,0:T(8,128)(2,1)S(1)} %copy-done.25, bf16[160,3584]{1,0:T(8,128)(2,1)S(1)} %copy-done.35, bf16[160,3584]{1,0:T(8,128)(2,1)} %collective-permute-done.11.refs_3_, ...), custom_call_target="tpu_custom_call" | custom-call | flops 99999997952 | bytes 333333344 | tf_op jit(solution)/shard_map/gave/pallas_call | solution.py:233
  133.0 9.6 %hidden.1 = (bf16[8,80,1024]{2,1,0:T(8,128)(2,1)}, f32[8,80,128]{2,1,0:T(8,128)S(1)}, f32[8,128]{1,0:T(8,128)S(1)}) custom-call(s32[15]{0:T(128)S(1)} %copy-done.14, bf16[640,2048]{1,0:T(8,128)(2,1)S(1)} %get-tuple-element.76.refs_1_, bf16[640,1536]{1,0:T(8,128)(2,1)S(1)} %get-tuple-element.81.refs_2_.refs_1_, bf16[1,1024,3584]{2,1,0:T(8,128)(2,1)S(1)} %copy-done.20, ...), custom_call_target="tpu_custom_call" | custom-call | flops 99999997952 | bytes 333333344 | tf_op jit(solution)/shard_map/hidden/pallas_call | solution.py:233
  145.4 2.7 %kept.3 = (bf16[256,1536]{1,0:T(8,128)(2,1)S(1)}, f32[256,1536]{1,0:T(8,128)S(1)}, f32[8,128]{1,0:T(8,128)S(1)}) custom-call(s32[15]{0:T(128)S(1)} %copy-done.14, bf16[640,1536]{1,0:T(8,128)(2,1)S(1)} %get-tuple-element.81.refs_2_.refs_1_, bf16[1024,640]{1,0:T(8,128)(2,1)S(1)} %copy-done.7, bf16[512,1536]{1,0:T(8,128)(2,1)S(1)} %collective-permute-done.17.refs_3_, ...), custom_call_target="tpu_custom_call" | custom-call | flops 1 | tf_op jit(solution)/shard_map/kept/pallas_call | solution.py:233
  154.2 3.7 %collective-permute-done.19.refs_0_ = bf16[256,2048]{1,0:T(8,128)(2,1)} collective-permute-done((bf16[256,2048]{1,0:T(8,128)(2,1)}, bf16[256,2048]{1,0:T(8,128)(2,1)}, u32[]{:S(2)}, u32[]{:S(2)}) %collective-permute-start.19) | collective-permute-done | bytes 1048608 | tf_op jit(solution)/shard_map/ppermute | solution.py:269
  159.6 2.7 %collective-permute-start.21 = (f32[2,80]{1,0:T(2,128)S(1)}, f32[2,80]{1,0:T(2,128)S(1)}, u32[]{:S(2)}, u32[]{:S(2)}) collective-permute-start(f32[2,80]{1,0:T(2,128)S(1)} %bitcast.64), channel_id=1, source_target_pairs={{0,2},{1,3},{2,0},{3,1},{4,6},{5,7},{6,4},{7,5},{8,10},{9,11},{10,... | collective-permute-start | bytes 1928 | tf_op jit(solution)/shard_map/ppermute | solution.py:266
  163.8 3.5 %add_three.1 = (bf16[128,3584]{1,0:T(8,128)(2,1)}, f32[8,128]{1,0:T(8,128)S(1)}) custom-call(s32[15]{0:T(128)S(1)} %copy-done.14, f32[128,3584]{1,0:T(8,128)S(1)} %copy-done.31, bf16[128,3584]{1,0:T(8,128)(2,1)} %after.20.refs_1_.refs_2_, bf16[128,3584]{1,0:T(8,128)(2,1)} %after.18.refs_4_.refs_3_, bf16[256,2048]{1,0:T(8,128)(2,1)} %after.21.refs_4_.refs_2_), custom_call_target="tpu_custom_call" | custom-call | flops 99999997952 | bytes 333333344 | tf_op jit(solution)/shard_map/add_three/pallas_call | solution.py:233
  168.2 5.8 %collective-permute-done.24.refs_4_ = bf16[256,1536]{1,0:T(8,128)(2,1)S(1)} collective-permute-done((bf16[256,1536]{1,0:T(8,128)(2,1)}, bf16[256,1536]{1,0:T(8,128)(2,1)S(1)}, u32[]{:S(2)}, u32[]{:S(2)}) %collective-permute-start.24) | collective-permute-done | bytes 786464 | tf_op jit(solution)/shard_map/ppermute | solution.py:269
  174.0 3.0 %add_chunks.1 = (bf16[1,256,3584]{2,1,0:T(8,128)(2,1)}, f32[8,128]{1,0:T(8,128)}) custom-call(s32[15]{0:T(128)S(1)} %copy-done.14, f32[256,2048]{1,0:T(8,128)S(1)} %copy-done.29, bf16[256,2048]{1,0:T(8,128)(2,1)} %after.21.refs_4_.refs_2_, f32[256,1536]{1,0:T(8,128)S(1)} %copy-done.22, bf16[256,1536]{1,0:T(8,128)(2,1)S(1)} %collective-permute-done.24.refs_4_, ...), custom_call_target="tpu_custom_call" | custom-call | flops 99999997952 | bytes 333333344 | tf_op jit(solution)/shard_map/add_chunks/pallas_call | solution.py:233
  (168 shorter events, 52.8 us)
Async XLA Ops:
  0.6 30.8 %collective-permute-start.2 = (bf16[128,3584]{1,0:T(8,128)(2,1)}, bf16[128,3584]{1,0:T(8,128)(2,1)}, u32[]{:S(2)}, u32[]{:S(2)}) collective-permute-start(bf16[128,3584]{1,0:T(8,128)(2,1)} %refs_3_.2), channel_id=1, source_target_pairs={{2,4},{3,5},{4,2},{5,3},{10,12},{11,13},{12,10},{13,11},{18,20},{1... | collective-permute-start | bytes 2752520 | tf_op jit(solution)/shard_map/ppermute | solution.py:266
  2.3 28.3 %collective-permute-start.3 = (bf16[128,3584]{1,0:T(8,128)(2,1)}, bf16[128,3584]{1,0:T(8,128)(2,1)}, u32[]{:S(2)}, u32[]{:S(2)}) collective-permute-start(bf16[128,3584]{1,0:T(8,128)(2,1)} %refs_3_.2), channel_id=1, source_target_pairs={{0,2},{1,3},{2,0},{3,1},{4,6},{5,7},{6,4},{7,5},{8,10},{9,11},{10,... | collective-permute-start | bytes 2752520 | tf_op jit(solution)/shard_map/ppermute | solution.py:266
  9.2 18.5 %collective-permute-start = (f32[8,128]{1,0:T(8,128)}, f32[8,128]{1,0:T(8,128)}, u32[]{:S(2)}, u32[]{:S(2)}) collective-permute-start(f32[8,128]{1,0:T(8,128)} %maximum_bitcast_fusion), channel_id=1, source_target_pairs={{0,2},{1,3},{2,0},{3,1},{4,6},{5,7},{6,4},{7,5},{8,10},{9,11},{10,... | collective-permute-start | bytes 12296 | tf_op jit(solution)/shard_map/ppermute | solution.py:266
  18.1 28.5 %collective-permute-start.6 = (bf16[160,3584]{1,0:T(8,128)(2,1)}, bf16[160,3584]{1,0:T(8,128)(2,1)}, u32[]{:S(2)}, u32[]{:S(2)}) collective-permute-start(bf16[160,3584]{1,0:T(8,128)(2,1)} %get-tuple-element.58), channel_id=1, source_target_pairs={{0,1},{1,0},{2,3},{3,2},{4,5},{5,4},{6,7},{7,6},{8,9},{9,8},{10,11... | collective-permute-start | bytes 3440648 | tf_op jit(solution)/shard_map/ppermute | solution.py:266
  30.6 28.1 %collective-permute-start.5 = (bf16[128,3584]{1,0:T(8,128)(2,1)}, bf16[128,3584]{1,0:T(8,128)(2,1)S(1)}, u32[]{:S(2)}, u32[]{:S(2)}) collective-permute-start(bf16[128,3584]{1,0:T(8,128)(2,1)} %after.12.refs_1_.refs_4_), channel_id=1, source_target_pairs={{2,4},{3,5},{4,2},{5,3},{10,12},{11,13},{12,10},{13,11},{18,20},{1... | collective-permute-start | bytes 2752520 | tf_op jit(solution)/shard_map/ppermute | solution.py:266
  31.5 27.2 %collective-permute-start.7 = (bf16[128,3584]{1,0:T(8,128)(2,1)}, bf16[128,3584]{1,0:T(8,128)(2,1)}, u32[]{:S(2)}, u32[]{:S(2)}) collective-permute-start(bf16[128,3584]{1,0:T(8,128)(2,1)} %after.13.refs_3_), channel_id=1, source_target_pairs={{2,0},{3,1},{4,6},{5,7},{10,8},{11,9},{12,14},{13,15},{18,16},{19,... | collective-permute-start | bytes 2752520 | tf_op jit(solution)/shard_map/ppermute | solution.py:266
  35.0 36.2 %collective-permute-start.4 = (bf16[160,3584]{1,0:T(8,128)(2,1)}, bf16[160,3584]{1,0:T(8,128)(2,1)}, u32[]{:S(2)}, u32[]{:S(2)}) collective-permute-start(bf16[160,3584]{1,0:T(8,128)(2,1)} %after.14.refs_5_), channel_id=1, source_target_pairs={{0,1},{1,0},{2,3},{3,2},{4,5},{5,4},{6,7},{7,6},{8,9},{9,8},{10,11... | collective-permute-start | bytes 3440648 | tf_op jit(solution)/shard_map/ppermute | solution.py:266
  52.0 20.0 %collective-permute-start.8 = (bf16[128,3584]{1,0:T(8,128)(2,1)}, bf16[128,3584]{1,0:T(8,128)(2,1)S(1)}, u32[]{:S(2)}, u32[]{:S(2)}) collective-permute-start(bf16[128,3584]{1,0:T(8,128)(2,1)} %get-tuple-element.62.refs_1_), channel_id=1, source_target_pairs={{0,2},{1,3},{6,4},{7,5},{8,10},{9,11},{14,12},{15,13},{16,18},{17,... | collective-permute-start | bytes 2752520 | tf_op jit(solution)/shard_map/ppermute | solution.py:266
  57.2 43.3 %collective-permute-start.11 = (bf16[160,3584]{1,0:T(8,128)(2,1)}, bf16[160,3584]{1,0:T(8,128)(2,1)}, u32[]{:S(2)}, u32[]{:S(2)}) collective-permute-start(bf16[160,3584]{1,0:T(8,128)(2,1)} %copy-done.26), channel_id=1, source_target_pairs={{0,1},{1,0},{2,3},{3,2},{4,5},{5,4},{6,7},{7,6},{8,9},{9,8},{10,11... | collective-permute-start | bytes 3440648 | tf_op jit(solution)/shard_map/ppermute | solution.py:266
  59.6 22.4 %collective-permute-start.10 = (bf16[128,3584]{1,0:T(8,128)(2,1)}, bf16[128,3584]{1,0:T(8,128)(2,1)}, u32[]{:S(2)}, u32[]{:S(2)}) collective-permute-start(bf16[128,3584]{1,0:T(8,128)(2,1)} %after.15.refs_1_.refs_5_), channel_id=1, source_target_pairs={{2,0},{3,1},{4,6},{5,7},{10,8},{11,9},{12,14},{13,15},{18,16},{19,... | collective-permute-start | bytes 2752520 | tf_op jit(solution)/shard_map/ppermute | solution.py:266
  74.8 39.5 %collective-permute-start.9 = (bf16[128,3584]{1,0:T(8,128)(2,1)}, bf16[128,3584]{1,0:T(8,128)(2,1)}, u32[]{:S(2)}, u32[]{:S(2)}) collective-permute-start(bf16[128,3584]{1,0:T(8,128)(2,1)} %get-tuple-element.63), channel_id=1, source_target_pairs={{2,4},{3,5},{4,2},{5,3},{10,12},{11,13},{12,10},{13,11},{18,20},{1... | collective-permute-start | bytes 2752520 | tf_op jit(solution)/shard_map/ppermute | solution.py:266
  76.4 20.9 %collective-permute-start.13 = (bf16[128,3584]{1,0:T(8,128)(2,1)}, bf16[128,3584]{1,0:T(8,128)(2,1)S(1)}, u32[]{:S(2)}, u32[]{:S(2)}) collective-permute-start(bf16[128,3584]{1,0:T(8,128)(2,1)} %after.17.refs_7_.refs_1_), channel_id=1, source_target_pairs={{0,2},{1,3},{6,4},{7,5},{8,10},{9,11},{14,12},{15,13},{16,18},{17,... | collective-permute-start | bytes 2752520 | tf_op jit(solution)/shard_map/ppermute | solution.py:266
  87.1 22.6 %collective-permute-start.12 = (bf16[160,2048]{1,0:T(8,128)(2,1)S(1)}, bf16[160,2048]{1,0:T(8,128)(2,1)S(1)}, u32[]{:S(2)}, u32[]{:S(2)}) collective-permute-start(bf16[160,2048]{1,0:T(8,128)(2,1)S(1)} %get-tuple-element.69), channel_id=1, source_target_pairs={{0,1},{1,0},{2,3},{3,2},{4,5},{5,4},{6,7},{7,6},{8,9},{9,8},{10,11... | collective-permute-start | bytes 1966088 | tf_op jit(solution)/shard_map/ppermute | solution.py:266
  88.5 37.4 %collective-permute-start.15 = (bf16[160,1536]{1,0:T(8,128)(2,1)}, bf16[160,1536]{1,0:T(8,128)(2,1)}, u32[]{:S(2)}, u32[]{:S(2)}) collective-permute-start(bf16[160,1536]{1,0:T(8,128)(2,1)} %get-tuple-element.77), channel_id=1, source_target_pairs={{0,1},{1,0},{2,3},{3,2},{4,5},{5,4},{6,7},{7,6},{8,9},{9,8},{10,11... | collective-permute-start | bytes 1474568 | tf_op jit(solution)/shard_map/ppermute | solution.py:266
  98.9 45.2 %collective-permute-start.18 = (bf16[128,3584]{1,0:T(8,128)(2,1)}, bf16[128,3584]{1,0:T(8,128)(2,1)}, u32[]{:S(2)}, u32[]{:S(2)}) collective-permute-start(bf16[128,3584]{1,0:T(8,128)(2,1)} %get-tuple-element.85), channel_id=1, source_target_pairs={{2,4},{3,5},{4,2},{5,3},{10,12},{11,13},{12,10},{13,11},{18,20},{1... | collective-permute-start | bytes 2752520 | tf_op jit(solution)/shard_map/ppermute | solution.py:266
  114.2 6.2 %collective-permute-start.16 = (bf16[512,2048]{1,0:T(8,128)(2,1)S(1)}, bf16[512,2048]{1,0:T(8,128)(2,1)S(1)}, u32[]{:S(2)}, u32[]{:S(2)}) collective-permute-start(bf16[512,2048]{1,0:T(8,128)(2,1)S(1)} %get-tuple-element.78), channel_id=1, source_target_pairs={{0,8},{8,0},{16,24},{24,16},{1,9},{9,1},{17,25},{25,17},{2,10},{10... | collective-permute-start | bytes 6291464 | tf_op jit(solution)/shard_map/ppermute | solution.py:269
  118.4 35.7 %collective-permute-start.14 = (bf16[128,3584]{1,0:T(8,128)(2,1)}, bf16[128,3584]{1,0:T(8,128)(2,1)}, u32[]{:S(2)}, u32[]{:S(2)}) collective-permute-start(bf16[128,3584]{1,0:T(8,128)(2,1)} %get-tuple-element.75), channel_id=1, source_target_pairs={{0,2},{1,3},{2,0},{3,1},{4,6},{5,7},{6,4},{7,5},{8,10},{9,11},{10,... | collective-permute-start | bytes 2752520 | tf_op jit(solution)/shard_map/ppermute | solution.py:266
  131.3 12.7 %collective-permute-start.17 = (bf16[512,1536]{1,0:T(8,128)(2,1)}, bf16[512,1536]{1,0:T(8,128)(2,1)S(1)}, u32[]{:S(2)}, u32[]{:S(2)}) collective-permute-start(bf16[512,1536]{1,0:T(8,128)(2,1)} %get-tuple-element.84), channel_id=1, source_target_pairs={{0,8},{8,0},{16,24},{24,16},{1,9},{9,1},{17,25},{25,17},{2,10},{10... | collective-permute-start | bytes 4718600 | tf_op jit(solution)/shard_map/ppermute | solution.py:269
  131.5 26.3 %collective-permute-start.19 = (bf16[256,2048]{1,0:T(8,128)(2,1)}, bf16[256,2048]{1,0:T(8,128)(2,1)}, u32[]{:S(2)}, u32[]{:S(2)}) collective-permute-start(bf16[256,2048]{1,0:T(8,128)(2,1)} %get-tuple-element.88), channel_id=1, source_target_pairs={{0,16},{8,24},{16,0},{24,8},{1,17},{9,25},{17,1},{25,9},{2,18},{10... | collective-permute-start | bytes 3145736 | tf_op jit(solution)/shard_map/ppermute | solution.py:269
  152.0 5.8 %collective-permute-start.20 = (f32[4,80]{1,0:T(4,128)S(1)}, f32[4,80]{1,0:T(4,128)S(1)}, u32[]{:S(2)}, u32[]{:S(2)}) collective-permute-start(f32[4,80]{1,0:T(4,128)S(1)} %get-tuple-element.97), channel_id=1, source_target_pairs={{0,1},{1,0},{2,3},{3,2},{4,5},{5,4},{6,7},{7,6},{8,9},{9,8},{10,11... | collective-permute-start | bytes 3848 | tf_op jit(solution)/shard_map/ppermute | solution.py:266
  153.6 20.4 %collective-permute-start.24 = (bf16[256,1536]{1,0:T(8,128)(2,1)}, bf16[256,1536]{1,0:T(8,128)(2,1)S(1)}, u32[]{:S(2)}, u32[]{:S(2)}) collective-permute-start(bf16[256,1536]{1,0:T(8,128)(2,1)} %copy-done.27), channel_id=1, source_target_pairs={{0,16},{8,24},{16,0},{24,8},{1,17},{9,25},{17,1},{25,9},{2,18},{10... | collective-permute-start | bytes 2359304 | tf_op jit(solution)/shard_map/ppermute | solution.py:269
  157.8 9.5 %collective-permute-start.23 = (f32[2,80]{1,0:T(2,128)S(1)}, f32[2,80]{1,0:T(2,128)S(1)}, u32[]{:S(2)}, u32[]{:S(2)}) collective-permute-start(f32[2,80]{1,0:T(2,128)S(1)} %bitcast.65), channel_id=1, source_target_pairs={{0,6},{1,7},{6,0},{7,1},{2,4},{3,5},{4,2},{5,3},{8,14},{9,15},{14,... | collective-permute-start | bytes 1928 | tf_op jit(solution)/shard_map/ppermute | solution.py:266
  159.3 8.1 %collective-permute-start.22 = (f32[2,80]{1,0:T(2,128)S(1)}, f32[2,80]{1,0:T(2,128)S(1)}, u32[]{:S(2)}, u32[]{:S(2)}) collective-permute-start(f32[2,80]{1,0:T(2,128)S(1)} %select_bitcast_fusion), channel_id=1, source_target_pairs={{0,4},{1,5},{4,0},{5,1},{2,6},{3,7},{6,2},{7,3},{8,12},{9,13},{12,... | collective-permute-start | bytes 1928 | tf_op jit(solution)/shard_map/ppermute | solution.py:266
  159.6 7.7 %collective-permute-start.21 = (f32[2,80]{1,0:T(2,128)S(1)}, f32[2,80]{1,0:T(2,128)S(1)}, u32[]{:S(2)}, u32[]{:S(2)}) collective-permute-start(f32[2,80]{1,0:T(2,128)S(1)} %bitcast.64), channel_id=1, source_target_pairs={{0,2},{1,3},{2,0},{3,1},{4,6},{5,7},{6,4},{7,5},{8,10},{9,11},{10,... | collective-permute-start | bytes 1928 | tf_op jit(solution)/shard_map/ppermute | solution.py:266
  (47 other events, 289.8 us)

commit v5 on v4

--- a/solution.py
+++ b/solution.py
@@ -13,7 +13,7 @@
 COST = 10**11
 COSTS = {'positions1': 1, 'packed_near1': 1, 'turned1': 1, 'kept2': 1}
 LIMIT = 24
-LIMITS = {'hidden': 40, 'made': 60}
+LIMITS = {'hidden': 40, 'made': 40}
 
 
 def split_expert(n):

time: 178 us -> 181 us (1.017)
  local copies, waits for them, and re-layouts: 17.3 us -> 25.4 us
  Pallas kernels: 68.5 us -> 63.7 us
    unnamed x92 -> x102, local copies, waits for them, and re-layouts: 15.3 us -> 23.9 us
    pallas_call x17, Pallas kernels: 68.5 us -> 63.6 us  [call(): pl.pallas_call(body, out_shape=[jax.ShapeDtypeStruct(shape, dtype) for sh...]
  transfers between devices with their start and end apart: 25 -> 25, of which waited for: 9 -> 8; matrix products, arithmetic and copies ran while one was open for 4% -> 4% of each run, Pallas kernels for 37% -> 34%
where the time goes in v5:
time: 181 us; the launch traced here: 180 us
  Pallas kernels  63.7 us (35%)
  waiting for transfers between devices  44 us (24%)
  starting transfers between devices  40.2 us (22%)
  local copies, waits for them, and re-layouts  25.4 us (14%)
  other arithmetic  5.44 us (3%)
    pallas_call x17, Pallas kernels, call(): pl.pallas_call(body, out_shape=[jax.ShapeDtypeStruct(shape, dtype) for sh...  63.6 us
    ppermute x21, starting transfers between devices, over_expert(): return lax.ppermute(a, 'expert', pairs)  37.9 us
    ppermute x21, waiting for transfers between devices, over_expert(): return lax.ppermute(a, 'expert', pairs)  34.5 us
    unnamed x102, local copies, waits for them, and re-layouts  23.9 us
    ppermute x4, waiting for transfers between devices, over_dp(): return lax.ppermute(a, 'dp', pairs)  9.51 us
  transfers between devices with their start and end apart: 25, of which 8 were waited for; matrix products, arithmetic and copies ran while one was open for 4% of the time, Pallas kernels for 34%

profile of v5, /device:TPU:0, one launch (start us, length us, event | category | flops | bytes accessed | tf_op | source)
XLA Modules:
  0.0 179.7 jit_solution(204946979527277036)
XLA Ops:
  2.2 5.0 %collective-permute-start.3 = (bf16[128,3584]{1,0:T(8,128)(2,1)}, bf16[128,3584]{1,0:T(8,128)(2,1)}, u32[]{:S(2)}, u32[]{:S(2)}) collective-permute-start(bf16[128,3584]{1,0:T(8,128)(2,1)} %refs_3_.2), channel_id=1, source_target_pairs={{0,2},{1,3},{2,0},{3,1},{4,6},{5,7},{6,4},{7,5},{8,10},{9,11},{10,... | collective-permute-start | bytes 2752520 | tf_op jit(solution)/shard_map/ppermute | solution.py:266
  11.4 3.1 %copy-done.22 = bf16[1,1024,3584]{2,1,0:T(8,128)(2,1)S(1)} copy-done((bf16[1,1024,3584]{2,1,0:T(8,128)(2,1)S(1)}, bf16[1,1024,3584]{2,1,0:T(8,128)(2,1)}, u32[]{:S(2)}) %copy-start.22) | copy-done | bytes 7340056
  14.5 5.4 %made.2 = (bf16[160,3584]{1,0:T(8,128)(2,1)S(1)}, bf16[160,3584]{1,0:T(8,128)(2,1)}, f32[8,128]{1,0:T(8,128)S(1)}) custom-call(s32[15]{0:T(128)S(1)} %concatenate.17.refs_0_, bf16[8,80,1024]{2,1,0:T(8,128)(2,1)S(1)} %bitcast.39, bf16[8,80,1024]{2,1,0:T(8,128)(2,1)S(1)} %bitcast.40, bf16[8,80,1024]{2,1,0:T(8,128)(2,1)S(1)} %bitcast.41, ...), custom_call_target="tpu_custom_call" | custom-call | flops 99999997952 | bytes 333333344 | tf_op jit(solution)/shard_map/made/pallas_call | solution.py:233
  22.4 4.8 %made.3 = (bf16[160,3584]{1,0:T(8,128)(2,1)S(1)}, bf16[160,3584]{1,0:T(8,128)(2,1)S(1)}, f32[8,128]{1,0:T(8,128)S(1)}) custom-call(s32[15]{0:T(128)S(1)} %concatenate.17.refs_0_, bf16[8,80,1024]{2,1,0:T(8,128)(2,1)S(1)} %bitcast.43, bf16[8,80,1024]{2,1,0:T(8,128)(2,1)S(1)} %bitcast.44, bf16[8,80,1024]{2,1,0:T(8,128)(2,1)S(1)} %bitcast.45, ...), custom_call_target="tpu_custom_call" | custom-call | flops 99999997952 | bytes 333333344 | tf_op jit(solution)/shard_map/made/pallas_call | solution.py:233
  44.5 4.9 %collective-permute-done.6.refs_4_ = bf16[160,3584]{1,0:T(8,128)(2,1)} collective-permute-done((bf16[160,3584]{1,0:T(8,128)(2,1)}, bf16[160,3584]{1,0:T(8,128)(2,1)}, u32[]{:S(2)}, u32[]{:S(2)}) %collective-permute-start.6) | collective-permute-done | bytes 1146912 | tf_op jit(solution)/shard_map/ppermute | solution.py:266
  49.4 3.9 %shared_far.1 = (bf16[128,3584]{1,0:T(8,128)(2,1)S(1)}, bf16[128,3584]{1,0:T(8,128)(2,1)}, f32[8,128]{1,0:T(8,128)S(1)}) custom-call(s32[15]{0:T(128)S(1)} %concatenate.17.refs_0_, s32[8,128]{1,0:T(8,128)S(1)} %get-tuple-element.52.refs_1_, f32[8,128]{1,0:T(8,128)S(1)} %get-tuple-element.53.refs_2_, bf16[160,3584]{1,0:T(8,128)(2,1)S(1)} %copy-done.38, ...), custom_call_target="tpu_custom_call" | custom-call | flops 99999997952 | bytes 333333344 | tf_op jit(solution)/shard_map/shared_far/pallas_call | solution.py:233
  54.9 4.0 %collective-permute-start.8 = (bf16[128,3584]{1,0:T(8,128)(2,1)}, bf16[128,3584]{1,0:T(8,128)(2,1)S(1)}, u32[]{:S(2)}, u32[]{:S(2)}) collective-permute-start(bf16[128,3584]{1,0:T(8,128)(2,1)} %get-tuple-element.62.refs_1_), channel_id=1, source_target_pairs={{0,2},{1,3},{6,4},{7,5},{8,10},{9,11},{14,12},{15,13},{16,18},{17,... | collective-permute-start | bytes 2752520 | tf_op jit(solution)/shard_map/ppermute | solution.py:266
  63.8 10.2 %collective-permute-done.4.refs_0_ = bf16[160,3584]{1,0:T(8,128)(2,1)} collective-permute-done((bf16[160,3584]{1,0:T(8,128)(2,1)}, bf16[160,3584]{1,0:T(8,128)(2,1)}, u32[]{:S(2)}, u32[]{:S(2)}) %collective-permute-start.4) | collective-permute-done | bytes 1146912 | tf_op jit(solution)/shard_map/ppermute | solution.py:266
  74.9 2.8 %add.86 = (bf16[128,3584]{1,0:T(8,128)(2,1)}, f32[8,128]{1,0:T(8,128)S(1)}) custom-call(s32[15]{0:T(128)S(1)} %concatenate.17.refs_0_, bf16[128,3584]{1,0:T(8,128)(2,1)} %get-tuple-element.62.refs_1_, bf16[128,3584]{1,0:T(8,128)(2,1)S(1)} %collective-permute-done.8.refs_2_, bf16[160,3584]{1,0:T(8,128)(2,1)} %after.16.refs_3_.refs_4_), custom_call_target="tpu_custom_call" | custom-call | flops 99999997952 | bytes 333333344 | tf_op jit(solution)/shard_map/add/pallas_call | solution.py:233
  79.3 5.3 %collective-permute-start.13 = (bf16[128,3584]{1,0:T(8,128)(2,1)}, bf16[128,3584]{1,0:T(8,128)(2,1)S(1)}, u32[]{:S(2)}, u32[]{:S(2)}) collective-permute-start(bf16[128,3584]{1,0:T(8,128)(2,1)} %after.17.refs_7_.refs_1_), channel_id=1, source_target_pairs={{0,2},{1,3},{6,4},{7,5},{8,10},{9,11},{14,12},{15,13},{16,18},{17,... | collective-permute-start | bytes 2752520 | tf_op jit(solution)/shard_map/ppermute | solution.py:266
  85.8 3.9 %packed_far.1 = (bf16[160,2048]{1,0:T(8,128)(2,1)S(1)}, bf16[160,1536]{1,0:T(8,128)(2,1)}, bf16[160,3584]{1,0:T(8,128)(2,1)S(1)}, f32[8,128]{1,0:T(8,128)S(1)}) custom-call(s32[15]{0:T(128)S(1)} %concatenate.17.refs_0_, s32[8,128]{1,0:T(8,128)S(1)} %get-tuple-element.52.refs_1_, f32[8,128]{1,0:T(8,128)S(1)} %get-tuple-element.53.refs_2_, ...), custom_call_target="tpu_custom_call" | custom-call | flops 99999997952 | bytes 333333344 | tf_op jit(solution)/shard_map/packed_far/pallas_call | solution.py:233
  91.6 7.9 %collective-permute-done.13.refs_2_ = bf16[128,3584]{1,0:T(8,128)(2,1)S(1)} collective-permute-done((bf16[128,3584]{1,0:T(8,128)(2,1)}, bf16[128,3584]{1,0:T(8,128)(2,1)S(1)}, u32[]{:S(2)}, u32[]{:S(2)}) %collective-permute-start.13) | collective-permute-done | bytes 917536 | tf_op jit(solution)/shard_map/ppermute | solution.py:266
  102.6 9.9 %collective-permute-done.12.refs_4_ = bf16[160,2048]{1,0:T(8,128)(2,1)S(1)} collective-permute-done((bf16[160,2048]{1,0:T(8,128)(2,1)S(1)}, bf16[160,2048]{1,0:T(8,128)(2,1)S(1)}, u32[]{:S(2)}, u32[]{:S(2)}) %collective-permute-start.12) | collective-permute-done | bytes 655392 | tf_op jit(solution)/shard_map/ppermute | solution.py:266
  112.5 4.5 %gave.2 = (bf16[512,2048]{1,0:T(8,128)(2,1)S(1)}, bf16[640,2048]{1,0:T(8,128)(2,1)S(1)}, f32[8,128]{1,0:T(8,128)S(1)}) custom-call(s32[15]{0:T(128)S(1)} %concatenate.17.refs_0_, bf16[160,3584]{1,0:T(8,128)(2,1)S(1)} %copy-done.27, bf16[160,3584]{1,0:T(8,128)(2,1)S(1)} %get-tuple-element.67.refs_2_, bf16[160,3584]{1,0:T(8,128)(2,1)} %collective-permute-done.11.refs_3_, ...), custom_call_target="tpu_custom_call" | custom-call | flops 99999997952 | bytes 333333344 | tf_op jit(solution)/shard_map/gave/pallas_call | solution.py:233
  117.1 4.2 %shared_near.1 = (f32[128,3584]{1,0:T(8,128)S(1)}, bf16[128,3584]{1,0:T(8,128)(2,1)}, f32[8,128]{1,0:T(8,128)S(1)}) custom-call(s32[15]{0:T(128)S(1)} %concatenate.17.refs_0_, s32[8,128]{1,0:T(8,128)S(1)} %get-tuple-element.52.refs_1_, f32[8,128]{1,0:T(8,128)S(1)} %get-tuple-element.53.refs_2_, bf16[160,3584]{1,0:T(8,128)(2,1)S(1)} %copy-done.36, ...), custom_call_target="tpu_custom_call" | custom-call | flops 99999997952 | bytes 333333344 | tf_op jit(solution)/shard_map/shared_near/pallas_call | solution.py:233
  123.4 4.0 %kept.2 = (bf16[256,2048]{1,0:T(8,128)(2,1)}, f32[256,2048]{1,0:T(8,128)S(1)}, f32[8,128]{1,0:T(8,128)S(1)}) custom-call(s32[15]{0:T(128)S(1)} %concatenate.17.refs_0_, bf16[640,2048]{1,0:T(8,128)(2,1)S(1)} %get-tuple-element.76.refs_1_, bf16[1024,640]{1,0:T(8,128)(2,1)S(1)} %get-tuple-element.70.refs_5_.refs_2_, ...), custom_call_target="tpu_custom_call" | custom-call | flops 99999997952 | bytes 333333344 | tf_op jit(solution)/shard_map/kept/pallas_call | solution.py:233
  128.7 5.3 %gave.3 = (bf16[512,1536]{1,0:T(8,128)(2,1)}, bf16[640,1536]{1,0:T(8,128)(2,1)S(1)}, f32[8,128]{1,0:T(8,128)S(1)}) custom-call(s32[15]{0:T(128)S(1)} %concatenate.17.refs_0_, bf16[160,3584]{1,0:T(8,128)(2,1)S(1)} %copy-done.28, bf16[160,3584]{1,0:T(8,128)(2,1)S(1)} %copy-done.40, bf16[160,3584]{1,0:T(8,128)(2,1)} %collective-permute-done.11.refs_3_, ...), custom_call_target="tpu_custom_call" | custom-call | flops 99999997952 | bytes 333333344 | tf_op jit(solution)/shard_map/gave/pallas_call | solution.py:233
  135.8 9.7 %hidden.1 = (bf16[8,80,1024]{2,1,0:T(8,128)(2,1)}, f32[8,80,128]{2,1,0:T(8,128)S(1)}, f32[8,128]{1,0:T(8,128)S(1)}) custom-call(s32[15]{0:T(128)S(1)} %concatenate.17.refs_0_, bf16[640,2048]{1,0:T(8,128)(2,1)S(1)} %get-tuple-element.76.refs_1_, bf16[640,1536]{1,0:T(8,128)(2,1)S(1)} %get-tuple-element.81.refs_2_.refs_1_, ...), custom_call_target="tpu_custom_call" | custom-call | flops 99999997952 | bytes 333333344 | tf_op jit(solution)/shard_map/hidden/pallas_call | solution.py:233
  148.1 2.7 %kept.3 = (bf16[256,1536]{1,0:T(8,128)(2,1)S(1)}, f32[256,1536]{1,0:T(8,128)S(1)}, f32[8,128]{1,0:T(8,128)S(1)}) custom-call(s32[15]{0:T(128)S(1)} %concatenate.17.refs_0_, bf16[640,1536]{1,0:T(8,128)(2,1)S(1)} %get-tuple-element.81.refs_2_.refs_1_, bf16[1024,640]{1,0:T(8,128)(2,1)S(1)} %copy-done.9, bf16[512,1536]{1,0:T(8,128)(2,1)S(1)} %collective-permute-done.17.refs_3_, ...), custom_call_target="tpu_custom_call" | custom-call | flops 1 | tf_op jit(solution)/shard_map/kept/pallas_call | solution.py:233
  156.8 3.7 %collective-permute-done.19.refs_0_ = bf16[256,2048]{1,0:T(8,128)(2,1)} collective-permute-done((bf16[256,2048]{1,0:T(8,128)(2,1)}, bf16[256,2048]{1,0:T(8,128)(2,1)}, u32[]{:S(2)}, u32[]{:S(2)}) %collective-permute-start.19) | collective-permute-done | bytes 1048608 | tf_op jit(solution)/shard_map/ppermute | solution.py:269
  162.5 2.6 %collective-permute-start.21 = (f32[2,80]{1,0:T(2,128)S(1)}, f32[2,80]{1,0:T(2,128)S(1)}, u32[]{:S(2)}, u32[]{:S(2)}) collective-permute-start(f32[2,80]{1,0:T(2,128)S(1)} %bitcast.64), channel_id=1, source_target_pairs={{0,2},{1,3},{2,0},{3,1},{4,6},{5,7},{6,4},{7,5},{8,10},{9,11},{10,... | collective-permute-start | bytes 1928 | tf_op jit(solution)/shard_map/ppermute | solution.py:266
  166.6 3.5 %add_three.1 = (bf16[128,3584]{1,0:T(8,128)(2,1)}, f32[8,128]{1,0:T(8,128)S(1)}) custom-call(s32[15]{0:T(128)S(1)} %concatenate.17.refs_0_, f32[128,3584]{1,0:T(8,128)S(1)} %copy-done.34, bf16[128,3584]{1,0:T(8,128)(2,1)} %after.20.refs_1_.refs_2_, bf16[128,3584]{1,0:T(8,128)(2,1)} %after.18.refs_4_.refs_3_, bf16[256,2048]{1,0:T(8,128)(2,1)} %after.21.refs_4_.refs_2_), custom_call_target="tpu_custom_call" | custom-call | flops 99999997952 | bytes 333333344 | tf_op jit(solution)/shard_map/add_three/pallas_call | solution.py:233
  171.0 5.8 %collective-permute-done.24.refs_4_ = bf16[256,1536]{1,0:T(8,128)(2,1)S(1)} collective-permute-done((bf16[256,1536]{1,0:T(8,128)(2,1)}, bf16[256,1536]{1,0:T(8,128)(2,1)S(1)}, u32[]{:S(2)}, u32[]{:S(2)}) %collective-permute-start.24) | collective-permute-done | bytes 786464 | tf_op jit(solution)/shard_map/ppermute | solution.py:269
  176.7 3.0 %add_chunks.1 = (bf16[1,256,3584]{2,1,0:T(8,128)(2,1)}, f32[8,128]{1,0:T(8,128)}) custom-call(s32[15]{0:T(128)S(1)} %concatenate.17.refs_0_, f32[256,2048]{1,0:T(8,128)S(1)} %copy-done.32, bf16[256,2048]{1,0:T(8,128)(2,1)} %after.21.refs_4_.refs_2_, f32[256,1536]{1,0:T(8,128)S(1)} %copy-done.25, bf16[256,1536]{1,0:T(8,128)(2,1)S(1)} %collective-permute-done.24.refs_4_, ...), custom_call_target="tpu_custom_call" | custom-call | flops 99999997952 | bytes 333333344 | tf_op jit(solution)/shard_map/add_chunks/pallas_call | solution.py:233
  (178 shorter events, 58.9 us)
Async XLA Ops:
  0.6 33.3 %collective-permute-start.2 = (bf16[128,3584]{1,0:T(8,128)(2,1)}, bf16[128,3584]{1,0:T(8,128)(2,1)}, u32[]{:S(2)}, u32[]{:S(2)}) collective-permute-start(bf16[128,3584]{1,0:T(8,128)(2,1)} %refs_3_.2), channel_id=1, source_target_pairs={{2,4},{3,5},{4,2},{5,3},{10,12},{11,13},{12,10},{13,11},{18,20},{1... | collective-permute-start | bytes 2752520 | tf_op jit(solution)/shard_map/ppermute | solution.py:266
  2.2 30.9 %collective-permute-start.3 = (bf16[128,3584]{1,0:T(8,128)(2,1)}, bf16[128,3584]{1,0:T(8,128)(2,1)}, u32[]{:S(2)}, u32[]{:S(2)}) collective-permute-start(bf16[128,3584]{1,0:T(8,128)(2,1)} %refs_3_.2), channel_id=1, source_target_pairs={{0,2},{1,3},{2,0},{3,1},{4,6},{5,7},{6,4},{7,5},{8,10},{9,11},{10,... | collective-permute-start | bytes 2752520 | tf_op jit(solution)/shard_map/ppermute | solution.py:266
  9.2 20.7 %collective-permute-start = (f32[8,128]{1,0:T(8,128)}, f32[8,128]{1,0:T(8,128)}, u32[]{:S(2)}, u32[]{:S(2)}) collective-permute-start(f32[8,128]{1,0:T(8,128)} %maximum_bitcast_fusion), channel_id=1, source_target_pairs={{0,2},{1,3},{2,0},{3,1},{4,6},{5,7},{6,4},{7,5},{8,10},{9,11},{10,... | collective-permute-start | bytes 12296 | tf_op jit(solution)/shard_map/ppermute | solution.py:266
  20.9 28.5 %collective-permute-start.6 = (bf16[160,3584]{1,0:T(8,128)(2,1)}, bf16[160,3584]{1,0:T(8,128)(2,1)}, u32[]{:S(2)}, u32[]{:S(2)}) collective-permute-start(bf16[160,3584]{1,0:T(8,128)(2,1)} %get-tuple-element.58), channel_id=1, source_target_pairs={{0,1},{1,0},{2,3},{3,2},{4,5},{5,4},{6,7},{7,6},{8,9},{9,8},{10,11... | collective-permute-start | bytes 3440648 | tf_op jit(solution)/shard_map/ppermute | solution.py:266
  33.1 28.5 %collective-permute-start.5 = (bf16[128,3584]{1,0:T(8,128)(2,1)}, bf16[128,3584]{1,0:T(8,128)(2,1)S(1)}, u32[]{:S(2)}, u32[]{:S(2)}) collective-permute-start(bf16[128,3584]{1,0:T(8,128)(2,1)} %after.12.refs_1_.refs_4_), channel_id=1, source_target_pairs={{2,4},{3,5},{4,2},{5,3},{10,12},{11,13},{12,10},{13,11},{18,20},{1... | collective-permute-start | bytes 2752520 | tf_op jit(solution)/shard_map/ppermute | solution.py:266
  34.0 27.6 %collective-permute-start.7 = (bf16[128,3584]{1,0:T(8,128)(2,1)}, bf16[128,3584]{1,0:T(8,128)(2,1)}, u32[]{:S(2)}, u32[]{:S(2)}) collective-permute-start(bf16[128,3584]{1,0:T(8,128)(2,1)} %after.13.refs_3_), channel_id=1, source_target_pairs={{2,0},{3,1},{4,6},{5,7},{10,8},{11,9},{12,14},{13,15},{18,16},{19,... | collective-permute-start | bytes 2752520 | tf_op jit(solution)/shard_map/ppermute | solution.py:266
  37.2 36.8 %collective-permute-start.4 = (bf16[160,3584]{1,0:T(8,128)(2,1)}, bf16[160,3584]{1,0:T(8,128)(2,1)}, u32[]{:S(2)}, u32[]{:S(2)}) collective-permute-start(bf16[160,3584]{1,0:T(8,128)(2,1)} %after.14.refs_5_), channel_id=1, source_target_pairs={{0,1},{1,0},{2,3},{3,2},{4,5},{5,4},{6,7},{7,6},{8,9},{9,8},{10,11... | collective-permute-start | bytes 3440648 | tf_op jit(solution)/shard_map/ppermute | solution.py:266
  54.9 20.0 %collective-permute-start.8 = (bf16[128,3584]{1,0:T(8,128)(2,1)}, bf16[128,3584]{1,0:T(8,128)(2,1)S(1)}, u32[]{:S(2)}, u32[]{:S(2)}) collective-permute-start(bf16[128,3584]{1,0:T(8,128)(2,1)} %get-tuple-element.62.refs_1_), channel_id=1, source_target_pairs={{0,2},{1,3},{6,4},{7,5},{8,10},{9,11},{14,12},{15,13},{16,18},{17,... | collective-permute-start | bytes 2752520 | tf_op jit(solution)/shard_map/ppermute | solution.py:266
  60.1 42.5 %collective-permute-start.11 = (bf16[160,3584]{1,0:T(8,128)(2,1)}, bf16[160,3584]{1,0:T(8,128)(2,1)}, u32[]{:S(2)}, u32[]{:S(2)}) collective-permute-start(bf16[160,3584]{1,0:T(8,128)(2,1)} %copy-done.29), channel_id=1, source_target_pairs={{0,1},{1,0},{2,3},{3,2},{4,5},{5,4},{6,7},{7,6},{8,9},{9,8},{10,11... | collective-permute-start | bytes 3440648 | tf_op jit(solution)/shard_map/ppermute | solution.py:266
  62.5 22.0 %collective-permute-start.10 = (bf16[128,3584]{1,0:T(8,128)(2,1)}, bf16[128,3584]{1,0:T(8,128)(2,1)}, u32[]{:S(2)}, u32[]{:S(2)}) collective-permute-start(bf16[128,3584]{1,0:T(8,128)(2,1)} %after.15.refs_1_.refs_5_), channel_id=1, source_target_pairs={{2,0},{3,1},{4,6},{5,7},{10,8},{11,9},{12,14},{13,15},{18,16},{19,... | collective-permute-start | bytes 2752520 | tf_op jit(solution)/shard_map/ppermute | solution.py:266
  77.7 39.4 %collective-permute-start.9 = (bf16[128,3584]{1,0:T(8,128)(2,1)}, bf16[128,3584]{1,0:T(8,128)(2,1)}, u32[]{:S(2)}, u32[]{:S(2)}) collective-permute-start(bf16[128,3584]{1,0:T(8,128)(2,1)} %get-tuple-element.63), channel_id=1, source_target_pairs={{2,4},{3,5},{4,2},{5,3},{10,12},{11,13},{12,10},{13,11},{18,20},{1... | collective-permute-start | bytes 2752520 | tf_op jit(solution)/shard_map/ppermute | solution.py:266
  79.3 20.2 %collective-permute-start.13 = (bf16[128,3584]{1,0:T(8,128)(2,1)}, bf16[128,3584]{1,0:T(8,128)(2,1)S(1)}, u32[]{:S(2)}, u32[]{:S(2)}) collective-permute-start(bf16[128,3584]{1,0:T(8,128)(2,1)} %after.17.refs_7_.refs_1_), channel_id=1, source_target_pairs={{0,2},{1,3},{6,4},{7,5},{8,10},{9,11},{14,12},{15,13},{16,18},{17,... | collective-permute-start | bytes 2752520 | tf_op jit(solution)/shard_map/ppermute | solution.py:266
  89.6 22.9 %collective-permute-start.12 = (bf16[160,2048]{1,0:T(8,128)(2,1)S(1)}, bf16[160,2048]{1,0:T(8,128)(2,1)S(1)}, u32[]{:S(2)}, u32[]{:S(2)}) collective-permute-start(bf16[160,2048]{1,0:T(8,128)(2,1)S(1)} %get-tuple-element.69), channel_id=1, source_target_pairs={{0,1},{1,0},{2,3},{3,2},{4,5},{5,4},{6,7},{7,6},{8,9},{9,8},{10,11... | collective-permute-start | bytes 1966088 | tf_op jit(solution)/shard_map/ppermute | solution.py:266
  91.1 37.6 %collective-permute-start.15 = (bf16[160,1536]{1,0:T(8,128)(2,1)}, bf16[160,1536]{1,0:T(8,128)(2,1)}, u32[]{:S(2)}, u32[]{:S(2)}) collective-permute-start(bf16[160,1536]{1,0:T(8,128)(2,1)} %get-tuple-element.77), channel_id=1, source_target_pairs={{0,1},{1,0},{2,3},{3,2},{4,5},{5,4},{6,7},{7,6},{8,9},{9,8},{10,11... | collective-permute-start | bytes 1474568 | tf_op jit(solution)/shard_map/ppermute | solution.py:266
  101.1 45.7 %collective-permute-start.18 = (bf16[128,3584]{1,0:T(8,128)(2,1)}, bf16[128,3584]{1,0:T(8,128)(2,1)}, u32[]{:S(2)}, u32[]{:S(2)}) collective-permute-start(bf16[128,3584]{1,0:T(8,128)(2,1)} %get-tuple-element.85), channel_id=1, source_target_pairs={{2,4},{3,5},{4,2},{5,3},{10,12},{11,13},{12,10},{13,11},{18,20},{1... | collective-permute-start | bytes 2752520 | tf_op jit(solution)/shard_map/ppermute | solution.py:266
  117.0 6.3 %collective-permute-start.16 = (bf16[512,2048]{1,0:T(8,128)(2,1)S(1)}, bf16[512,2048]{1,0:T(8,128)(2,1)S(1)}, u32[]{:S(2)}, u32[]{:S(2)}) collective-permute-start(bf16[512,2048]{1,0:T(8,128)(2,1)S(1)} %get-tuple-element.78), channel_id=1, source_target_pairs={{0,8},{8,0},{16,24},{24,16},{1,9},{9,1},{17,25},{25,17},{2,10},{10... | collective-permute-start | bytes 6291464 | tf_op jit(solution)/shard_map/ppermute | solution.py:269
  121.3 35.5 %collective-permute-start.14 = (bf16[128,3584]{1,0:T(8,128)(2,1)}, bf16[128,3584]{1,0:T(8,128)(2,1)}, u32[]{:S(2)}, u32[]{:S(2)}) collective-permute-start(bf16[128,3584]{1,0:T(8,128)(2,1)} %get-tuple-element.75), channel_id=1, source_target_pairs={{0,2},{1,3},{2,0},{3,1},{4,6},{5,7},{6,4},{7,5},{8,10},{9,11},{10,... | collective-permute-start | bytes 2752520 | tf_op jit(solution)/shard_map/ppermute | solution.py:266
  134.1 12.7 %collective-permute-start.17 = (bf16[512,1536]{1,0:T(8,128)(2,1)}, bf16[512,1536]{1,0:T(8,128)(2,1)S(1)}, u32[]{:S(2)}, u32[]{:S(2)}) collective-permute-start(bf16[512,1536]{1,0:T(8,128)(2,1)} %get-tuple-element.84), channel_id=1, source_target_pairs={{0,8},{8,0},{16,24},{24,16},{1,9},{9,1},{17,25},{25,17},{2,10},{10... | collective-permute-start | bytes 4718600 | tf_op jit(solution)/shard_map/ppermute | solution.py:269
  134.3 26.3 %collective-permute-start.19 = (bf16[256,2048]{1,0:T(8,128)(2,1)}, bf16[256,2048]{1,0:T(8,128)(2,1)}, u32[]{:S(2)}, u32[]{:S(2)}) collective-permute-start(bf16[256,2048]{1,0:T(8,128)(2,1)} %get-tuple-element.88), channel_id=1, source_target_pairs={{0,16},{8,24},{16,0},{24,8},{1,17},{9,25},{17,1},{25,9},{2,18},{10... | collective-permute-start | bytes 3145736 | tf_op jit(solution)/shard_map/ppermute | solution.py:269
  154.7 5.9 %collective-permute-start.20 = (f32[4,80]{1,0:T(4,128)S(1)}, f32[4,80]{1,0:T(4,128)S(1)}, u32[]{:S(2)}, u32[]{:S(2)}) collective-permute-start(f32[4,80]{1,0:T(4,128)S(1)} %get-tuple-element.97), channel_id=1, source_target_pairs={{0,1},{1,0},{2,3},{3,2},{4,5},{5,4},{6,7},{7,6},{8,9},{9,8},{10,11... | collective-permute-start | bytes 3848 | tf_op jit(solution)/shard_map/ppermute | solution.py:266
  156.3 20.5 %collective-permute-start.24 = (bf16[256,1536]{1,0:T(8,128)(2,1)}, bf16[256,1536]{1,0:T(8,128)(2,1)S(1)}, u32[]{:S(2)}, u32[]{:S(2)}) collective-permute-start(bf16[256,1536]{1,0:T(8,128)(2,1)} %copy-done.30), channel_id=1, source_target_pairs={{0,16},{8,24},{16,0},{24,8},{1,17},{9,25},{17,1},{25,9},{2,18},{10... | collective-permute-start | bytes 2359304 | tf_op jit(solution)/shard_map/ppermute | solution.py:269
  160.6 9.5 %collective-permute-start.23 = (f32[2,80]{1,0:T(2,128)S(1)}, f32[2,80]{1,0:T(2,128)S(1)}, u32[]{:S(2)}, u32[]{:S(2)}) collective-permute-start(f32[2,80]{1,0:T(2,128)S(1)} %bitcast.65), channel_id=1, source_target_pairs={{0,6},{1,7},{6,0},{7,1},{2,4},{3,5},{4,2},{5,3},{8,14},{9,15},{14,... | collective-permute-start | bytes 1928 | tf_op jit(solution)/shard_map/ppermute | solution.py:266
  162.0 8.1 %collective-permute-start.22 = (f32[2,80]{1,0:T(2,128)S(1)}, f32[2,80]{1,0:T(2,128)S(1)}, u32[]{:S(2)}, u32[]{:S(2)}) collective-permute-start(f32[2,80]{1,0:T(2,128)S(1)} %select_bitcast_fusion), channel_id=1, source_target_pairs={{0,4},{1,5},{4,0},{5,1},{2,6},{3,7},{6,2},{7,3},{8,12},{9,13},{12,... | collective-permute-start | bytes 1928 | tf_op jit(solution)/shard_map/ppermute | solution.py:266
  162.5 7.6 %collective-permute-start.21 = (f32[2,80]{1,0:T(2,128)S(1)}, f32[2,80]{1,0:T(2,128)S(1)}, u32[]{:S(2)}, u32[]{:S(2)}) collective-permute-start(f32[2,80]{1,0:T(2,128)S(1)} %bitcast.64), channel_id=1, source_target_pairs={{0,2},{1,3},{2,0},{3,1},{4,6},{5,7},{6,4},{7,5},{8,10},{9,11},{10,... | collective-permute-start | bytes 1928 | tf_op jit(solution)/shard_map/ppermute | solution.py:266
  (52 other events, 296.0 us)
